TPU v7x, 32 devices: a whole 2x2x4 slice. The times are simulated.
32 devices in a mesh: lat: 8 (over z, y), lvl: 4 (over x, core).
Axes of the slice: x: 2, y: 2, z: 4, core: 2. Of those that a mesh axis runs over, the one named last changes fastest.
Arguments:
- fields: bfloat16 [80, 2, 256, 192], P('lvl', None, 'lat'), may hold values from -6 to 6
- targets: bfloat16 [80, 2, 256, 192], P('lvl', None, 'lat'), may hold values from -6 to 6
- ocean_depth: int32 [256, 192], P('lat', 'lvl'), may hold values from 0 to 19, as said below
- thickness_class: int32 [19], replicated, may hold values from 1 to 8
- params: float32 [2306304], P(('lat', 'lvl'))
- moment1: float32 [2306304], P(('lat', 'lvl'))
- moment2: float32 [2306304], P(('lat', 'lvl')), as said below
Outputs:
- loss_sum: float32 [], replicated
- loss_count: float32 [], replicated
- grad_norm: float32 [], replicated
- new_params: float32 [2306304], P(('lat', 'lvl'))
- new_moment1: float32 [2306304], P(('lat', 'lvl'))
- new_moment2: float32 [2306304], P(('lat', 'lvl'))
Inputs may be any that keep to these rules, and one draw needn't show every extreme that they name: `ocean_depth`: land cells are 0; every draw has a land cell and a cell with all 19 levels. `moment2`: all entries positive.
All inputs are finite; a program needn't handle non-finite values.
Results may differ from a plain program's by a relative error of at most 0.0045.
Values may be sent and summed in bfloat16 or wider, within the bound.
No kernel may reach another device: no remote copies, remote signals or barrier semaphores. Data moves between devices by JAX's collectives and lax.ppermute only.
A program may use at most 192 MiB of HBM per device.

v0:
```python
import math

import jax
import jax.numpy as jnp
from jax import lax
from jax.sharding import PartitionSpec as P

CIN = 80
WIDTH = 200
EXPAND = 800
WIDTH2 = 400
EXPAND2 = 1600
KSIZE = 7
LEVELS = 19
STEP = 10


CLIP = 0.01
LRATE = 0.05
BETA_ONE = 0.9
BETA_TWO = 0.999
ADAM_EPS = 1e-08
DECAY = 0.1
HEAT_WEIGHT = 40.0
NORM_EPS = 1e-05


def padded(cells, sides, width):
    for axis, dim in sides:
        count = lax.axis_size(axis)
        ends = count - 1
        head = lax.slice_in_dim(cells, 0, width, axis=dim)
        tail = lax.slice_in_dim(cells, cells.shape[dim] - width, cells.shape[dim], axis=dim)
        cells = jnp.concatenate(
            [
                lax.ppermute(tail, axis, [(i, (i + 1) % count) for i in range(ends)]),
                cells,
                lax.ppermute(head, axis, [((i + 1) % count, i) for i in range(ends)]),
            ],
            axis=dim,
        )
    return cells


def block_shapes(chans, hidden):
    return [
        (chans, KSIZE * KSIZE),
        (chans,),
        (chans,),
        (hidden, chans),
        (hidden,),
        (chans, hidden),
        (chans,),
    ]


def pieces_of(flat):
    shapes = (
        [(WIDTH, CIN)]
        + block_shapes(WIDTH, EXPAND)
        + [(WIDTH2, 4 * WIDTH), (WIDTH2,)]
        + block_shapes(WIDTH2, EXPAND2)
        + [(4 * WIDTH, WIDTH2), (WIDTH,), (CIN, WIDTH), (CIN,)]
    )
    result = []
    start = 0
    for shape in shapes:
        amount = math.prod(shape)
        result.append(flat[start : start + amount].reshape(shape))
        start += amount
    return result


def channel_tables(depth, thick):
    channel = jnp.arange(CIN, dtype=jnp.int32)
    level = jnp.where(channel < 4 * LEVELS, channel // 4, 0)
    onehot = (level[:, None] == jnp.arange(LEVELS, dtype=jnp.int32)[None, :]).astype(jnp.float32)
    thickf = thick.astype(jnp.float32)
    chosen = ((channel % 4 == 0) & (channel < 4 * LEVELS)).astype(jnp.float32)
    heat_take = chosen * jnp.sum(onehot * thickf[None, :], axis=1) / jnp.sum(thickf)
    ocean = (level[:, None, None] < depth[None]).astype(jnp.float32)[:, None]
    surface_field = (depth > 0).astype(jnp.float32)[None]
    coarse = jnp.max(depth.reshape(depth.shape[0] // 2, 2, depth.shape[1] // 2, 2), axis=(1, 3))
    surface_two = (coarse > 0).astype(jnp.float32)[None]
    return (heat_take, ocean, surface_field, surface_two)


def depthwise(border_padded, kernel, rows, cols):
    total = jnp.zeros((border_padded.shape[0], border_padded.shape[1], rows, cols), jnp.float32)
    for p in range(KSIZE):
        for q in range(KSIZE):
            total = (
                total
                + kernel[:, p * KSIZE + q][:, None, None, None]
                * border_padded[:, :, p : p + rows, q : q + cols]
            )
    return total


def to_patches(grid):
    chans, batch, rows, cols = grid.shape
    split = grid.reshape(chans, batch, rows // 2, 2, cols // 2, 2)
    return split.transpose(0, 3, 5, 1, 2, 4).reshape(chans * 4, -1)


def from_patches(rows_of, batch, rows, cols):
    chans = rows_of.shape[0] // 4
    split = rows_of.reshape(chans, 2, 2, batch, rows, cols)
    return split.transpose(0, 3, 4, 1, 5, 2).reshape(chans, batch, rows * 2, cols * 2)


def mult(left, right):
    return jnp.dot(left, right, preferred_element_type=jnp.float32)


def contract_cells(left, right):
    return lax.dot_general(
        left, right, (((1,), (1,)), ((), ())), preferred_element_type=jnp.float32
    )


def contract_rows(left, right):
    return lax.dot_general(
        left, right, (((0,), (0,)), ((), ())), preferred_element_type=jnp.float32
    )


def block_forward(border_padded, centre, weights, surface_field, extra):
    kernel, norm_gain, shift, up, up_bias, down, down_bias = weights
    chans, batch, rows, cols = centre.shape
    depthwise_conv_output = depthwise(border_padded, kernel.astype(jnp.float32), rows, cols)
    sums, squares, ocean_cell_total, extra_total = lax.psum(
        (
            jnp.sum(depthwise_conv_output * surface_field, axis=(1, 2, 3)),
            jnp.sum(depthwise_conv_output * depthwise_conv_output * surface_field, axis=(1, 2, 3)),
            batch * jnp.sum(surface_field),
            extra,
        ),
        ("lat", "lvl"),
    )
    ocean_mean = sums / ocean_cell_total
    inverse_deviation = lax.rsqrt(squares / ocean_cell_total - ocean_mean * ocean_mean + NORM_EPS)
    mean_removed = depthwise_conv_output - ocean_mean[:, None, None, None]
    standardized_input = mean_removed * inverse_deviation[:, None, None, None]
    normalized_output = (
        standardized_input * norm_gain.astype(jnp.float32)[:, None, None, None]
        + shift.astype(jnp.float32)[:, None, None, None]
    )
    normalized_output = normalized_output.astype(jnp.bfloat16).reshape(chans, -1)
    act = mult(up, normalized_output) + up_bias.astype(jnp.float32)[:, None]
    gelu_out, gelu_backward_pull = jax.vjp(jax.nn.gelu, act)
    gelu_gated = gelu_out.astype(jnp.bfloat16)
    branch = mult(down, gelu_gated) + down_bias.astype(jnp.float32)[:, None]
    hout = (centre.astype(jnp.float32) + branch.reshape(centre.shape)).astype(jnp.bfloat16)
    ocean_kept = (
        border_padded,
        depthwise_conv_output,
        mean_removed,
        standardized_input,
        ocean_mean,
        inverse_deviation,
        ocean_cell_total,
        normalized_output,
        gelu_gated,
        gelu_backward_pull,
    )
    return (hout, extra_total, ocean_kept)


def block_backward(grad_hout, ocean_kept, weights, surface_field):
    kernel, norm_gain, shift, up, up_bias, down, down_bias = weights
    (
        border_padded,
        depthwise_conv_output,
        mean_removed,
        standardized_input,
        ocean_mean,
        inverse_deviation,
        ocean_cell_total,
        normalized_output,
        gelu_gated,
        gelu_backward_pull,
    ) = ocean_kept
    chans, batch, rows, cols = depthwise_conv_output.shape
    kernelf = kernel.astype(jnp.float32)
    grad_branch = grad_hout.astype(jnp.bfloat16).reshape(chans, -1)
    g_down = contract_cells(grad_branch, gelu_gated)
    g_down_bias = jnp.sum(grad_branch.astype(jnp.float32), axis=1)
    grad_gated = contract_rows(down, grad_branch)
    grad_act = gelu_backward_pull(grad_gated)[0].astype(jnp.bfloat16)
    g_up = contract_cells(grad_act, normalized_output)
    g_up_bias = jnp.sum(grad_act.astype(jnp.float32), axis=1)
    norm_input_gradient = contract_rows(up, grad_act).reshape(depthwise_conv_output.shape)
    gain_gradient = jnp.sum(norm_input_gradient * standardized_input, axis=(1, 2, 3))
    g_shift = jnp.sum(norm_input_gradient, axis=(1, 2, 3))
    standardized_gradient = norm_input_gradient * norm_gain.astype(jnp.float32)[:, None, None, None]
    total_a, total_b = lax.psum(
        (
            jnp.sum(standardized_gradient, axis=(1, 2, 3)),
            jnp.sum(standardized_gradient * mean_removed, axis=(1, 2, 3)),
        ),
        ("lat", "lvl"),
    )
    grad_var = -0.5 * inverse_deviation * inverse_deviation * inverse_deviation * total_b
    grad_first = (-inverse_deviation * total_a - 2.0 * ocean_mean * grad_var) / ocean_cell_total
    grad_second = grad_var / ocean_cell_total
    conv_gradient = standardized_gradient * inverse_deviation[
        :, None, None, None
    ] + surface_field * (
        grad_first[:, None, None, None]
        + 2.0 * (mean_removed + ocean_mean[:, None, None, None]) * grad_second[:, None, None, None]
    )
    conv_gradient = conv_gradient.astype(jnp.bfloat16)
    grad_convf = conv_gradient.astype(jnp.float32)
    kernel_terms = []
    for p in range(KSIZE):
        for q in range(KSIZE):
            kernel_terms.append(
                jnp.sum(
                    border_padded[:, :, p : p + rows, q : q + cols] * grad_convf, axis=(1, 2, 3)
                )
            )
    g_kernel = jnp.stack(kernel_terms, axis=1)
    grad_pad = padded(conv_gradient, (("lat", 2), ("lvl", 3)), 3).astype(jnp.float32)
    flipped = jnp.flip(kernelf.reshape(chans, KSIZE, KSIZE), axis=(1, 2)).reshape(
        chans, KSIZE * KSIZE
    )
    grad_in = grad_hout + depthwise(grad_pad, flipped, rows, cols)
    return (grad_in, [g_kernel, gain_gradient, g_shift, g_up, g_up_bias, g_down, g_down_bias])


def body(fields, targets, ocean_depth, thickness_class, params, moment1, moment2):
    flat_low = lax.all_gather(params.astype(jnp.bfloat16), ("lat", "lvl"), axis=0, tiled=True)
    parts = pieces_of(flat_low)
    stem, downs, downs_bias, ups, ups_bias, head, head_bias = (
        parts[0],
        parts[8],
        parts[9],
        parts[17],
        parts[18],
        parts[19],
        parts[20],
    )
    fine_weights = parts[1:8]
    coarse_weights = parts[10:17]
    inputs, goal = (
        lax.all_to_all(fields, "lvl", split_axis=3, concat_axis=0, tiled=True),
        lax.all_to_all(targets, "lvl", split_axis=3, concat_axis=0, tiled=True),
    )
    batch, rows, cols = (inputs.shape[1], inputs.shape[2], inputs.shape[3])
    heat_take, ocean, surface_field, surface_two = channel_tables(ocean_depth, thickness_class)
    flat_in = inputs.reshape(CIN, -1)
    hzero = mult(stem, flat_in).astype(jnp.bfloat16).reshape(WIDTH, batch, rows, cols)
    border_padded = padded(hzero, (("lat", 2), ("lvl", 3)), 3).astype(jnp.float32)
    hone, count, kept_fine = block_forward(
        border_padded, hzero, fine_weights, surface_field, batch * jnp.sum(ocean)
    )
    patches = to_patches(hone)
    coarse = (mult(downs, patches) + downs_bias.astype(jnp.float32)[:, None]).astype(jnp.bfloat16)
    coarse = coarse.reshape(WIDTH2, batch, rows // 2, cols // 2)
    coarse_pad = padded(coarse, (("lat", 2), ("lvl", 3)), 3).astype(jnp.float32)
    htwo, unused, kept_coarse = block_forward(
        coarse_pad, coarse, coarse_weights, surface_two, jnp.zeros((), jnp.float32)
    )
    htwo_flat = htwo.reshape(WIDTH2, -1)
    upped = mult(ups, htwo_flat) + jnp.repeat(ups_bias.astype(jnp.float32), 4)[:, None]
    upped = from_patches(upped, batch, rows // 2, cols // 2)
    skip = (hone.astype(jnp.float32) + upped).astype(jnp.bfloat16).reshape(WIDTH, -1)
    out = (mult(head, skip) + head_bias.astype(jnp.float32)[:, None]).reshape(
        CIN, batch, rows, cols
    )
    err = out - goal.astype(jnp.float32)
    heat = jnp.sum(heat_take[:, None, None, None] * ocean * err, axis=0)
    loss_part = jnp.sum(ocean * err * err) + HEAT_WEIGHT * jnp.sum(surface_field * heat * heat)
    grad_out = (
        2.0
        / count
        * ocean
        * (err + HEAT_WEIGHT * heat_take[:, None, None, None] * (surface_field * heat)[None])
    )
    grad_out = grad_out.astype(jnp.bfloat16).reshape(CIN, -1)
    g_head = contract_cells(grad_out, skip)
    g_head_bias = jnp.sum(grad_out.astype(jnp.float32), axis=1)
    grad_skip = contract_rows(head, grad_out).reshape(WIDTH, batch, rows, cols)
    grad_up_rows = to_patches(grad_skip.astype(jnp.bfloat16))
    g_ups = contract_cells(grad_up_rows, htwo_flat)
    g_ups_bias = jnp.sum(
        jnp.sum(grad_up_rows.astype(jnp.float32), axis=1).reshape(WIDTH, 4), axis=1
    )
    grad_two = contract_rows(ups, grad_up_rows).reshape(htwo.shape)
    grad_coarse, g_coarse = block_backward(grad_two, kept_coarse, coarse_weights, surface_two)
    grad_coarse = grad_coarse.astype(jnp.bfloat16).reshape(WIDTH2, -1)
    g_downs = contract_cells(grad_coarse, patches)
    g_downs_bias = jnp.sum(grad_coarse.astype(jnp.float32), axis=1)
    grad_hone = grad_skip + from_patches(
        contract_rows(downs, grad_coarse), batch, rows // 2, cols // 2
    )
    grad_zero, g_fine = block_backward(grad_hone, kept_fine, fine_weights, surface_field)
    grad_zero = grad_zero.astype(jnp.bfloat16).reshape(WIDTH, -1)
    g_stem = contract_cells(grad_zero, flat_in)
    pieces = (
        [g_stem]
        + g_fine
        + [g_downs, g_downs_bias]
        + g_coarse
        + [g_ups, g_ups_bias, g_head, g_head_bias]
    )
    joined = jnp.concatenate([piece.reshape(-1) for piece in pieces])
    shard_len = params.shape[0]
    joined = jnp.pad(joined, (0, shard_len * lax.axis_size(("lat", "lvl")) - joined.shape[0]))
    summed = lax.psum(joined, ("lat", "lvl"))
    mine = lax.dynamic_slice_in_dim(summed, lax.axis_index(("lat", "lvl")) * shard_len, shard_len)
    loss_total, square_sum = lax.psum((loss_part, jnp.sum(mine * mine)), ("lat", "lvl"))
    norm = jnp.sqrt(square_sum)
    clipped = mine * jnp.minimum(1.0, CLIP / norm)
    first = BETA_ONE * moment1 + (1.0 - BETA_ONE) * clipped
    second = BETA_TWO * moment2 + (1.0 - BETA_TWO) * clipped * clipped
    ratio = first / (1.0 - BETA_ONE**STEP) / (jnp.sqrt(second / (1.0 - BETA_TWO**STEP)) + ADAM_EPS)
    updated = params - LRATE * (ratio + DECAY * params)
    return (loss_total, count, norm, updated, first, second)


def solution(mesh):
    in_specs = (
        P("lvl", None, "lat", None),
        P("lvl", None, "lat", None),
        P("lat", "lvl"),
        P(),
        P(("lat", "lvl")),
        P(("lat", "lvl")),
        P(("lat", "lvl")),
    )
    out_specs = (P(), P(), P(), P(("lat", "lvl")), P(("lat", "lvl")), P(("lat", "lvl")))
    return jax.shard_map(body, mesh=mesh, in_specs=in_specs, out_specs=out_specs, check_vma=False)
```

profile of v0, /device:TPU:0, one launch (start us, length us, event | category | flops | bytes accessed | tf_op | source)
XLA Modules:
  0.0 1211.6 jit_solution(15618807780145808391)
XLA Ops:
  10.7 3.3 dynamic-update-slice
  18.1 4.2 all-to-all-start
  36.2 3.5 all-to-all-start.1
  43.2 3.0 copy.113
  46.2 3.9 reshape.488
  50.1 3.1 reshape.634
  53.2 3.7 copy.121
  56.9 3.2 reshape.528
  60.1 100.8 %all-reduce.12.cloned.1.call-done = bf16[2306304]{0:T(1024)(128)(2,1)} async-done(((bf16[2306304]{0:T(1024)(128)(2,1)}), bf16[2306304]{0:T(1024)(128)(2,1)}) %all-reduce.12.cloned.1.call-update) | async-done | bytes 4612624
  180.7 2.9 slice_reduce_fusion.47
  194.8 4.6 reshape.498
  199.5 3.2 reshape.500
  207.0 3.1 collective-permute-start
  225.0 22.8 %multiply_reduce_fusion.2 = (f32[200]{0:T(256)S(1)}, f32[200]{0:T(256)S(1)}, f32[200,2,32,48]{0,3,2,1:T(8,128)S(1)}) fusion(f32[32,48]{1,0:T(8,128)S(1)} %compare_convert_fusion.1, f32[200,2,38,54]{0,3,2,1:T(8,128)S(1)} %maximum_convert_fusion, f32[200]{0:T(256)S(1)} %get-tuple-element.164, f32[200]{0:T(256)S(1)} %get-tuple-element.165, ...), kind=kLoop, calls=%fused_computation.291 | loop fusion | flops 62668400 | bytes 122926944 | tf_op jit(solution)/shard_map/reduce_sum | solution.py:135
  247.9 43.7 %all-reduce.6 = (f32[200]{0:T(256)S(1)}, f32[]{:T(128)}, f32[200]{0:T(256)S(1)}) all-reduce(f32[200]{0:T(256)S(1)} %get-tuple-element.107, f32[]{:T(128)S(6)} %mul.2885, f32[200]{0:T(256)S(1)} %get-tuple-element.106), channel_id=1, replica_groups=mesh['lat'=8,'lvl'=4] {'lat','lvl'}, use_global_device_ids=true, to_apply=%region_1.2 | all-reduce | flops 401 | bytes 3208 | tf_op jit(solution)/shard_map/psum | solution.py:132
  292.9 6.3 fusion.9
  305.5 10.8 copy.116
  316.4 10.6 reshape.493
  329.4 4.4 collective-permute-start.4
  349.8 12.6 %multiply_reduce_fusion.8 = (f32[400]{0:T(512)}, f32[400]{0:T(512)}, f32[400,2,16,24]{0,3,2,1:T(8,128)}) fusion(f32[16,24]{1,0:T(8,128)S(1)} %compare_convert_fusion.2, f32[400,2,22,30]{0,3,2,1:T(8,128)S(1)} %maximum_convert_fusion.2, f32[400]{0:T(512)S(1)} %get-tuple-element.115, f32[400]{0:T(512)S(1)} %get-tuple-element.116, ...), kind=kLoop, calls=%fused_computation.455 | loop fusion | flops 31333600 | bytes 61523136 | tf_op jit(solution)/shard_map/reduce_sum | solution.py:134
  362.4 42.5 %all-reduce.5 = (f32[400]{0:T(512)S(1)}, f32[]{:T(128)}, f32[400]{0:T(512)S(1)}, f32[]{:T(128)}) all-reduce(f32[400]{0:T(512)} %get-tuple-element.111, f32[]{:T(128)S(6)} %mul.3046, f32[400]{0:T(512)} %get-tuple-element.110, f32[]{:T(128)S(6)} %mul.3072), channel_id=1, replica_groups=mesh['lat'=8,'lvl'=4] {'lat','lvl'}, use_global_device_ids=true, to_apply=%region_12.13 | all-reduce | flops 802 | bytes 6416 | tf_op jit(solution)/shard_map/psum | solution.py:132
  419.1 6.1 fusion.19
  429.8 11.8 reshape.501
  441.5 15.0 %copy.118 = f32[200,2,2,2,16,24]{0,2,5,1,4,3:T(2,128)} copy(f32[200,2,2,2,16,24]{5,4,3,2,1,0:T(8,128)} %reshape.501) | data formatting | bytes 4915200 | tf_op jit(solution)/shard_map/reshape | solution.py:108
  456.5 5.3 add_convert_fusion
  461.8 5.2 reshape.502
  467.0 3.4 copy.119
  470.5 4.2 multiply_reduce_fusion.10
  481.1 3.8 convert_element_type.299
  484.9 13.3 %copy.127 = bf16[200,2,2,2,16,24]{5,4,3,2,1,0:T(8,128)(2,1)} copy(bf16[200,2,2,2,16,24]{0,2,5,1,4,3:T(2,128)(2,1)} %bitcast.365) | data formatting | bytes 2457600 | tf_op jit(solution)/shard_map/transpose | solution.py:103
  498.1 10.5 reshape.505
  508.6 3.2 convert_reduce_fusion.5
  517.5 5.2 convert_reduce_fusion.1
  531.0 40.4 %all-reduce.4 = (f32[400]{0:T(512)S(1)}, f32[400]{0:T(512)S(1)}) all-reduce(f32[400]{0:T(512)S(1)} %get-tuple-element.109, f32[400]{0:T(512)S(1)} %get-tuple-element.387), channel_id=1, replica_groups=mesh['lat'=8,'lvl'=4] {'lat','lvl'}, use_global_device_ids=true, to_apply=%region_24.25 | all-reduce | flops 800 | bytes 6400 | tf_op jit(solution)/shard_map/psum | solution.py:197
  572.0 6.4 fusion.171
  578.4 3.4 fusion.170
  581.9 4.7 fusion.172
  587.3 3.1 fusion.263
  590.4 4.2 collective-permute-start.8
  598.7 4.2 convert_element_type.325
  611.5 3.9 copy.125
  615.3 3.5 reshape.524
  619.8 4.0 reshape.523
  626.7 5.5 reshape.522
  634.6 12.7 %convert_reduce_fusion.4 = (f32[400]{0:T(512)}, bf16[400,2,16,24]{0,3,2,1:T(8,128)(2,1)S(1)}) fusion(f32[400,2,16,24]{0,3,2,1:T(8,128)} %bitcast.382, f32[400,2,22,30]{0,3,2,1:T(8,128)S(1)} %maximum_convert_fusion.3, f32[400]{0:T(512)S(1)} %bitcast.472, f32[400]{0:T(512)S(1)} %bitcast.473, f32[400]{0:T(512)S(1)} %bitcast.474, f32[400]{0:T(512)S(1)} %bitcast.475, ...), kind=kLoop, calls=%fused_computation.450 | loop fusion | flops 31026800 | bytes 62134400 | tf_op jit(solution)/shard_map/reduce_sum | solution.py:294
  649.6 11.2 reshape.510
  660.8 14.0 %copy.134 = f32[200,2,16,2,24,2]{0,5,4,3,2,1:T(2,128)S(1)} copy(f32[200,2,16,2,24,2]{4,2,1,5,3,0:T(8,128)} %bitcast.355) | data formatting | bytes 4915200 | tf_op jit(solution)/shard_map/transpose | solution.py:109
  674.7 3.4 reshape.513
  678.2 3.6 copy.135
  683.8 10.7 convert_reduce_fusion
  701.0 3.8 multiply_reduce_fusion
  704.8 43.6 %all-reduce.3 = (f32[200]{0:T(256)S(1)}, f32[200]{0:T(256)S(1)}) all-reduce(f32[200]{0:T(256)S(1)} %get-tuple-element.7, f32[200]{0:T(256)S(1)} %get-tuple-element.389), channel_id=1, replica_groups=mesh['lat'=8,'lvl'=4] {'lat','lvl'}, use_global_device_ids=true, to_apply=%region_28.29 | all-reduce | flops 400 | bytes 3200 | tf_op jit(solution)/shard_map/psum | solution.py:197
  749.1 30.5 %fusion.72 = (f32[200]{0:T(256)S(1)}, f32[200]{0:T(256)S(1)}, f32[200]{0:T(256)S(1)}, f32[200]{0:T(256)S(1)}, f32[200]{0:T(256)S(1)}, /*index=5*/f32[200]{0:T(25...) fusion(f32[200,2,38,54]{0,3,2,1:T(8,128)} %copy-done, ...), kind=kLoop, calls=%fused_computation.183 | loop fusion | flops 28258800 | bytes 50405344 | tf_op jit(solution)/shard_map/reduce_sum | solution.py:219
  779.6 7.2 fusion.71
  786.7 9.8 fusion.73
  796.6 4.2 collective-permute-start.12
  802.3 4.3 fusion.261
  814.2 15.3 %copy.131 = f32[200,2,16,2,24,2]{0,1,5,4,3,2:T(2,128)} copy(f32[200,2,16,2,24,2]{4,2,1,5,3,0:T(8,128)} %bitcast.356) | data formatting | bytes 4915200 | tf_op jit(solution)/shard_map/transpose | solution.py:109
  831.8 3.2 reshape.520
  841.8 24.3 %fusion.76 = bf16[200,2,32,48]{0,3,2,1:T(8,128)(2,1)S(1)} fusion(f32[200,2,38,54]{0,3,2,1:T(8,128)S(1)} %maximum_convert_fusion.1, f32[200,2,32,48]{0,3,2,1:T(8,128)S(1)} %bitcast.367, f32[200,2,32,48]{0,1,3,2:T(2,128)} %bitcast.368, f32[200]{0:T(256)} %bitcast.570, f32[200]{0:T(256)} %bitcast.571, f32[200]{0:T(256)} %bitcast.572, f32[200]{0:T(256)} %bitcast.573, ...), kind=kLoop, calls=%fused_computation.188 | loop fusion | flops 61440000 | bytes 126605600 | tf_op jit(solution)/shard_map/convert_element_type | solution.py:299
  866.9 90.8 %concatenate.35 = f32[2306280]{0:T(1024)} concatenate(f32[16000]{0:T(1024)S(1)} %reshape.516, f32[9800]{0:T(1024)S(1)} %reshape.517, f32[200]{0:T(256)S(1)} %get-tuple-element.6, f32[200]{0:T(256)S(1)} %reduce_sum.1207, f32[160000]{0:T(1024)} %reshape.518, f32[800]{0:T(1024)S(1)} %get-tuple-element.391, f32[160000]{0:T(1024)} %reshape.519, f32[200]{0:T(256)S(1)} %get-tuple-element.233, ...), dimensions={0} | concatenate | bytes 18450240 | tf_op jit(solution)/shard_map/concatenate | solution.py:308
  957.7 8.5 pad.4
  968.9 189.4 %all-reduce.10.cloned.1.call-done = f32[2306304]{0:T(1024)} async-done(((f32[2306304]{0:T(1024)}), f32[2306304]{0:T(1024)}) %all-reduce.10.cloned.1.call-update) | async-done | bytes 9225232 | tf_op jit(solution)/shard_map/psum | solution.py:311
  1160.1 40.2 %all-reduce.2 = (f32[]{:T(128)}, f32[]{:T(128)}) all-reduce(f32[]{:T(128)S(6)} %add.973, f32[]{:T(128)} %multiply_reduce_fusion.11), channel_id=1, replica_groups=mesh['lat'=8,'lvl'=4] {'lat','lvl'}, use_global_device_ids=true, to_apply=%region_18.19 | all-reduce | flops 2 | bytes 16 | tf_op jit(solution)/shard_map/psum | solution.py:313
  (704 shorter events, 190.3 us)
Async XLA Ops:
  7.2 153.8 %all-reduce.12.cloned.1.call-start = ((), (), s32[]{:S(2)}) async-start(), calls=%async_computation.3 | async-start | bytes 9228288
  14.0 8.3 copy-start.37
  15.3 9.9 copy-start.256
  18.1 18.1 %all-to-all-start = ((bf16[4,2,30720]{2,1,0:T(2,128)(2,1)}), bf16[4,2,30720]{2,1,0:T(2,128)(2,1)S(1)}, u32[]{:S(2)}, u32[]{:S(2)}) async-start(bf16[4,2,30720]{2,1,0:T(2,128)(2,1)} %reshape.635), calls=%async_computation | async-start | bytes 983040 | tf_op jit(solution)/shard_map/all_to_all | solution.py:247
  23.7 10.8 copy-start.167
  25.8 199.0 %copy-start.40 = (f32[32,48]{1,0:T(8,128)}, f32[32,48]{1,0:T(8,128)S(1)}, u32[]{:S(2)}) copy-start(f32[32,48]{1,0:T(8,128)S(1)} %compare_convert_fusion.1) | copy-start | bytes 18436
  36.2 13.8 %all-to-all-start.1 = ((bf16[4,2,30720]{2,1,0:T(2,128)(2,1)}), bf16[4,2,30720]{2,1,0:T(2,128)(2,1)S(1)}, u32[]{:S(2)}, u32[]{:S(2)}) async-start(bf16[4,2,30720]{2,1,0:T(2,128)(2,1)} %reshape.633), calls=%async_computation.1 | async-start | bytes 983040 | tf_op jit(solution)/shard_map/all_to_all | solution.py:248
  39.7 1118.6 %all-reduce.10.cloned.1.call-start = ((), (), s32[]{:S(2)}) async-start(), calls=%async_computation.2 | async-start | bytes 18456576 | tf_op jit(solution)/shard_map/psum | solution.py:311
  206.3 11.3 copy-start.11
  207.0 10.4 collective-permute-start
  210.1 7.3 collective-permute-start.1
  213.4 79.4 %copy-start.206 = (f32[800]{0:T(1024)}, f32[800]{0:T(1024)S(1)}, u32[]{:S(2)}) copy-start(f32[800]{0:T(1024)S(1)} %slice_convert_fusion.3) | copy-start | bytes 9604
  216.2 201.2 %copy-start.55 = (f32[400]{0:T(512)}, f32[400]{0:T(512)S(1)}, u32[]{:S(2)}) copy-start(f32[400]{0:T(512)S(1)} %get-tuple-element.248) | copy-start | bytes 4804
  217.6 3.6 collective-permute-start.2
  218.9 4.8 collective-permute-start.3
  224.8 23.1 %copy-start = (f32[200,2,38,54]{0,3,2,1:T(8,128)}, f32[200,2,38,54]{0,3,2,1:T(8,128)S(1)}, u32[]{:S(2)}) copy-start(f32[200,2,38,54]{0,3,2,1:T(8,128)S(1)} %maximum_convert_fusion) | copy-start | bytes 9849604
  225.0 67.3 %copy-start.61 = (f32[200]{0:T(256)S(1)}, f32[200]{0:T(256)}, u32[]{:S(2)}) copy-start(f32[200]{0:T(256)} %get-tuple-element.245) | copy-start | bytes 2404
  225.0 67.3 %copy-start.210 = (f32[200]{0:T(256)S(1)}, f32[200]{0:T(256)}, u32[]{:S(2)}) copy-start(f32[200]{0:T(256)} %get-tuple-element.244) | copy-start | bytes 2404
  247.9 51.3 %copy-start.1 = (f32[200,2,32,48]{0,3,2,1:T(8,128)}, f32[200,2,32,48]{0,3,2,1:T(8,128)S(1)}, u32[]{:S(2)}) copy-start(f32[200,2,32,48]{0,3,2,1:T(8,128)S(1)} %get-tuple-element.241) | copy-start | bytes 7372804
  292.9 8.6 copy-start.12
  292.9 8.6 copy-start.45
  292.9 8.6 copy-start.254
  305.5 10.8 copy-start.6
  316.4 10.6 copy-start.18
  316.4 10.6 copy-start.253
  329.4 11.6 copy-start.9
  329.4 10.2 collective-permute-start.4
  333.8 7.0 collective-permute-start.5
  341.0 4.2 collective-permute-start.6
  342.3 7.3 copy-start.63
  342.3 7.3 copy-start.64
  342.5 5.4 collective-permute-start.7
  578.4 8.1 copy-start.2
  587.3 8.7 copy-start.5
  590.4 12.5 %collective-permute-start.8 = (bf16[400,2,3,24]{0,3,2,1:T(8,128)(2,1)}, bf16[400,2,3,24]{0,3,2,1:T(8,128)(2,1)S(1)}, u32[]{:S(2)}, u32[]{:S(2)}) collective-permute-start(bf16[400,2,3,24]{0,3,2,1:T(8,128)(2,1)} %get-tuple-element.270), channel_id=1, source_target_pairs={{0,4},{4,8},{8,12},{12,16},{16,20},{20,24},{24,28},{1,5},{5,9},{9,... | collective-permute-start | bytes 345608 | tf_op jit(solution)/shard_map/ppermute | solution.py:36
  594.6 8.3 copy-start.3
  594.6 8.3 collective-permute-start.9
  598.7 10.3 copy-start.27
  604.6 28.0 %collective-permute-start.10 = (bf16[400,2,22,3]{0,3,2,1:T(4,128)(2,1)}, bf16[400,2,22,3]{0,3,2,1:T(4,128)(2,1)S(1)}, u32[]{:S(2)}, u32[]{:S(2)}) collective-permute-start(bf16[400,2,22,3]{0,3,2,1:T(4,128)(2,1)} %get-tuple-element.266), channel_id=1, source_target_pairs={{0,1},{1,2},{2,3},{4,5},{5,6},{6,7},{8,9},{9,10},{10,11},{12,13},{... | collective-permute-start | bytes 316808 | tf_op jit(solution)/shard_map/ppermute | solution.py:36
  605.9 26.7 %collective-permute-start.11 = (bf16[400,2,22,3]{0,3,2,1:T(4,128)(2,1)}, bf16[400,2,22,3]{0,3,2,1:T(4,128)(2,1)S(1)}, u32[]{:S(2)}, u32[]{:S(2)}) collective-permute-start(bf16[400,2,22,3]{0,3,2,1:T(4,128)(2,1)} %get-tuple-element.267), channel_id=1, source_target_pairs={{1,0},{2,1},{3,2},{5,4},{6,5},{7,6},{9,8},{10,9},{11,10},{13,12},{... | collective-permute-start | bytes 316808 | tf_op jit(solution)/shard_map/ppermute | solution.py:38
  647.2 13.5 %copy-start.16 = (bf16[400,2,16,24]{0,3,2,1:T(8,128)(2,1)}, bf16[400,2,16,24]{0,3,2,1:T(8,128)(2,1)S(1)}, u32[]{:S(2)}) copy-start(bf16[400,2,16,24]{0,3,2,1:T(8,128)(2,1)S(1)} %get-tuple-element.232) | copy-start | bytes 1843204
  683.8 10.8 copy-start.24
  683.8 10.8 copy-start.21
  701.0 48.1 %copy-start.41 = (f32[32,48]{1,0:T(8,128)S(1)}, f32[32,48]{1,0:T(8,128)}, u32[]{:S(2)}) copy-start(f32[32,48]{1,0:T(8,128)} %copy-done.40) | copy-start | bytes 18436
  701.0 78.6 %slice-start = ((s8[4358144]{0:T(1024)(128)(4,1)}), s8[163840]{0:T(1024)(128)(4,1)S(1)}, s32[]{:S(2)}) async-start(s8[4358144]{0:T(1024)(128)(4,1)} %bitcast.353), calls=%async_computation.4 | async-start | bytes 327680
  749.1 30.5 %slice-start.1 = ((s8[4358144]{0:T(1024)(128)(4,1)}), s8[4194304]{0:T(1024)(128)(4,1)S(1)}, s32[]{:S(2)}) async-start(s8[4358144]{0:T(1024)(128)(4,1)} %bitcast.353), calls=%async_computation.5 | async-start | bytes 8388608
  786.7 15.5 %copy-start.25 = (bf16[200,3072]{1,0:T(8,128)(2,1)S(1)}, bf16[200,3072]{1,0:T(8,128)(2,1)}, u32[]{:S(2)}) copy-start(bf16[200,3072]{1,0:T(8,128)(2,1)} %copy-done.24) | copy-start | bytes 3686404
  796.6 10.0 collective-permute-start.12
  800.8 11.3 copy-start.17
  800.8 11.3 copy-start.28
  800.8 7.2 collective-permute-start.13
  808.9 30.3 %collective-permute-start.14 = (bf16[200,2,38,3]{0,3,2,1:T(4,128)(2,1)}, bf16[200,2,38,3]{0,3,2,1:T(4,128)(2,1)}, u32[]{:S(2)}, u32[]{:S(2)}) collective-permute-start(bf16[200,2,38,3]{0,3,2,1:T(4,128)(2,1)} %get-tuple-element.258), channel_id=1, source_target_pairs={{0,1},{1,2},{2,3},{4,5},{5,6},{6,7},{8,9},{9,10},{10,11},{12,13},{... | collective-permute-start | bytes 273608 | tf_op jit(solution)/shard_map/ppermute | solution.py:36
  810.8 28.4 %collective-permute-start.15 = (bf16[200,2,38,3]{0,3,2,1:T(4,128)(2,1)}, bf16[200,2,38,3]{0,3,2,1:T(4,128)(2,1)}, u32[]{:S(2)}, u32[]{:S(2)}) collective-permute-start(bf16[200,2,38,3]{0,3,2,1:T(4,128)(2,1)} %get-tuple-element.259), channel_id=1, source_target_pairs={{1,0},{2,1},{3,2},{5,4},{6,5},{7,6},{9,8},{10,9},{11,10},{13,12},{... | collective-permute-start | bytes 273608 | tf_op jit(solution)/shard_map/ppermute | solution.py:38
  841.7 24.4 %copy-start.14 = (bf16[80,3072]{1,0:T(8,128)(2,1)S(1)}, bf16[80,3072]{1,0:T(8,128)(2,1)}, u32[]{:S(2)}) copy-start(bf16[80,3072]{1,0:T(8,128)(2,1)} %reshape.488) | copy-start | bytes 1474564
  841.7 25.1 %copy-start.47 = (f32[19600]{0:T(1024)S(1)}, f32[19600]{0:T(1024)}, u32[]{:S(2)}) copy-start(f32[19600]{0:T(1024)} %reshape.521) | copy-start | bytes 235204
  841.7 25.1 %copy-start.50 = (f32[16000]{0:T(1024)S(1)}, f32[16000]{0:T(1024)}, u32[]{:S(2)}) copy-start(f32[16000]{0:T(1024)} %reshape.525) | copy-start | bytes 192004
  841.7 25.1 %copy-start.82 = (f32[1600]{0:T(1024)S(1)}, f32[1600]{0:T(1024)}, u32[]{:S(2)}) copy-start(f32[1600]{0:T(1024)} %get-tuple-element.393) | copy-start | bytes 19204
  841.8 25.1 %copy-start.83 = (f32[400]{0:T(512)S(1)}, f32[400]{0:T(512)}, u32[]{:S(2)}) copy-start(f32[400]{0:T(512)} %reduce_sum.1261) | copy-start | bytes 4804
  841.8 25.1 %copy-start.84 = (f32[400]{0:T(512)S(1)}, f32[400]{0:T(512)}, u32[]{:S(2)}) copy-start(f32[400]{0:T(512)} %get-tuple-element.231) | copy-start | bytes 4804
  841.8 25.1 %copy-start.166 = (f32[400]{0:T(512)S(1)}, f32[400]{0:T(512)}, u32[]{:S(2)}) copy-start(f32[400]{0:T(512)} %get-tuple-element.108) | copy-start | bytes 4804
  841.8 25.1 %copy-start.209 = (f32[200]{0:T(256)S(1)}, f32[200]{0:T(256)}, u32[]{:S(2)}) copy-start(f32[200]{0:T(256)} %convert_reduce_fusion.2) | copy-start | bytes 2404
  966.2 234.8 %copy-start.30 = (f32[72072]{0:T(1024)S(1)}, f32[72072]{0:T(1024)}, u32[]{:S(2)}) copy-start(f32[72072]{0:T(1024)} %param.11) | copy-start | bytes 864868
  966.2 234.8 %copy-start.48 = (f32[72072]{0:T(1024)S(1)}, f32[72072]{0:T(1024)}, u32[]{:S(2)}) copy-start(f32[72072]{0:T(1024)} %param.12) | copy-start | bytes 864868
  966.2 234.8 %copy-start.49 = (f32[72072]{0:T(1024)S(1)}, f32[72072]{0:T(1024)}, u32[]{:S(2)}) copy-start(f32[72072]{0:T(1024)} %param.13) | copy-start | bytes 864868
  (224 other events, 937.2 us)
Sparse Core Ops, SparseCore 0:
  14.1 146.7 all-reduce.11
  966.4 191.9 all-reduce.9
where the time goes:
time: 1230 us; the launch traced here: 1210 us
  local copies, waits for them, and re-layouts  374 us (30%)
  waiting for transfers between devices  301 us (24%)
  blocking collectives  210 us (17%)
  other arithmetic  189 us (15%)
  matrix products  72.2 us (6%)
  starting transfers between devices  40.2 us (3%)
  between operations  24.4 us (2%)
    psum x1, waiting for transfers between devices, body(): summed = lax.psum(joined, ('lat', 'lvl'))  189 us
    unnamed x3, waiting for transfers between devices  101 us
    concatenate x1, local copies, waits for them, and re-layouts, body(): joined = jnp.concatenate([piece.reshape(-1) for piece in pieces])  90.8 us
    psum x2, blocking collectives, block_forward(): lax.psum((jnp.sum(depthwise_conv_output * surface_field, axis=(1, 2, 3)),...  86.2 us
    psum x2, blocking collectives, block_backward(): lax.psum((jnp.sum(standardized_gradient, axis=(1, 2, 3)), jnp.sum(standar...  83.9 us
    reduce_sum x6, other arithmetic, block_backward(): jnp.sum(border_padded[:, :, p:p + rows, q:q + cols] * grad_convf, axis=(1...  62 us
    psum x1, blocking collectives, body(): lax.psum((loss_part, jnp.sum(mine * mine)), ('lat', 'lvl'))  40.2 us
    reshape x3, local copies, waits for them, and re-layouts, from_patches(): split = rows_of.reshape(chans, 2, 2, batch, rows, cols)  38 us
  transfers between devices with their start and end apart: 20, of which 8 were waited for; matrix products, arithmetic and copies ran while one was open for 9% of the time, Pallas kernels for 0%

commit v1 on v0

--- a/solution.py
+++ b/solution.py
@@ -23,6 +23,62 @@
 DECAY = 0.1
 HEAT_WEIGHT = 40.0
 NORM_EPS = 1e-05
+
+AXES = ("lat", "lvl")
+
+
+def bit_list():
+    bits = []
+    for axis in AXES:
+        count = lax.axis_size(axis)
+        step = count // 2
+        while step >= 1:
+            bits.append((axis, count, step))
+            step //= 2
+    return bits
+
+
+def exchange(values, axis, count, step):
+    return lax.ppermute(values, axis, [(i, i ^ step) for i in range(count)])
+
+
+def gather_blocks(block):
+    blocks = block[None]
+    for axis, count, step in bit_list():
+        other = exchange(blocks, axis, count, step)
+        high = (lax.axis_index(axis) // step) % 2 == 1
+        blocks = jnp.stack(
+            [jnp.where(high, other, blocks), jnp.where(high, blocks, other)], axis=1
+        ).reshape((-1,) + block.shape)
+    return blocks
+
+
+def scatter_blocks(blocks):
+    for turn, (axis, count, step) in enumerate(reversed(bit_list())):
+        pairs = blocks.reshape((blocks.shape[0] // 2, 2) + blocks.shape[1:])
+        high = (lax.axis_index(axis) // step) % 2 == 1
+        keep = jnp.where(high, pairs[:, 1], pairs[:, 0])
+        send = jnp.where(high, pairs[:, 0], pairs[:, 1])
+        if turn > 0:
+            send = send.astype(jnp.bfloat16)
+        blocks = keep + exchange(send, axis, count, step).astype(jnp.float32)
+    return blocks[0]
+
+
+def total_of(*values):
+    flat = jnp.concatenate([v.reshape(-1).astype(jnp.float32) for v in values])
+    amount = flat.shape[0]
+    rows = -(-amount // 1024) * 8
+    tile = jnp.pad(flat, (0, rows * 128 - amount)).reshape(1, rows, 128)
+    count = lax.axis_size(AXES)
+    got = lax.all_to_all(jnp.broadcast_to(tile, (count, rows, 128)), AXES, 0, 0, tiled=True)
+    summed = jnp.sum(got, axis=0).reshape(-1)
+    result = []
+    start = 0
+    for v in values:
+        result.append(summed[start : start + v.size].reshape(v.shape))
+        start += v.size
+    return result
 
 
 def padded(cells, sides, width):
@@ -129,14 +185,11 @@
     kernel, norm_gain, shift, up, up_bias, down, down_bias = weights
     chans, batch, rows, cols = centre.shape
     depthwise_conv_output = depthwise(border_padded, kernel.astype(jnp.float32), rows, cols)
-    sums, squares, ocean_cell_total, extra_total = lax.psum(
-        (
+    sums, squares, ocean_cell_total, extra_total = total_of(
             jnp.sum(depthwise_conv_output * surface_field, axis=(1, 2, 3)),
             jnp.sum(depthwise_conv_output * depthwise_conv_output * surface_field, axis=(1, 2, 3)),
             batch * jnp.sum(surface_field),
             extra,
-        ),
-        ("lat", "lvl"),
     )
     ocean_mean = sums / ocean_cell_total
     inverse_deviation = lax.rsqrt(squares / ocean_cell_total - ocean_mean * ocean_mean + NORM_EPS)
@@ -194,12 +247,9 @@
     gain_gradient = jnp.sum(norm_input_gradient * standardized_input, axis=(1, 2, 3))
     g_shift = jnp.sum(norm_input_gradient, axis=(1, 2, 3))
     standardized_gradient = norm_input_gradient * norm_gain.astype(jnp.float32)[:, None, None, None]
-    total_a, total_b = lax.psum(
-        (
+    total_a, total_b = total_of(
             jnp.sum(standardized_gradient, axis=(1, 2, 3)),
             jnp.sum(standardized_gradient * mean_removed, axis=(1, 2, 3)),
-        ),
-        ("lat", "lvl"),
     )
     grad_var = -0.5 * inverse_deviation * inverse_deviation * inverse_deviation * total_b
     grad_first = (-inverse_deviation * total_a - 2.0 * ocean_mean * grad_var) / ocean_cell_total
@@ -230,7 +280,10 @@
 
 
 def body(fields, targets, ocean_depth, thickness_class, params, moment1, moment2):
-    flat_low = lax.all_gather(params.astype(jnp.bfloat16), ("lat", "lvl"), axis=0, tiled=True)
+    shard_len = params.shape[0]
+    room = -(-shard_len // 2048) * 2048
+    block = jnp.pad(params.astype(jnp.bfloat16), (0, room - shard_len)).reshape(-1, 128)
+    flat_low = gather_blocks(block).reshape(-1, room)[:, :shard_len].reshape(-1)
     parts = pieces_of(flat_low)
     stem, downs, downs_bias, ups, ups_bias, head, head_bias = (
         parts[0],
@@ -306,11 +359,10 @@
         + [g_ups, g_ups_bias, g_head, g_head_bias]
     )
     joined = jnp.concatenate([piece.reshape(-1) for piece in pieces])
-    shard_len = params.shape[0]
-    joined = jnp.pad(joined, (0, shard_len * lax.axis_size(("lat", "lvl")) - joined.shape[0]))
-    summed = lax.psum(joined, ("lat", "lvl"))
-    mine = lax.dynamic_slice_in_dim(summed, lax.axis_index(("lat", "lvl")) * shard_len, shard_len)
-    loss_total, square_sum = lax.psum((loss_part, jnp.sum(mine * mine)), ("lat", "lvl"))
+    joined = jnp.pad(joined, (0, shard_len * lax.axis_size(AXES) - joined.shape[0]))
+    joined = jnp.pad(joined.reshape(-1, shard_len), ((0, 0), (0, room - shard_len)))
+    mine = scatter_blocks(joined.reshape(-1, room // 128, 128)).reshape(-1)[:shard_len]
+    loss_total, square_sum = total_of(loss_part, jnp.sum(mine * mine))
     norm = jnp.sqrt(square_sum)
     clipped = mine * jnp.minimum(1.0, CLIP / norm)
     first = BETA_ONE * moment1 + (1.0 - BETA_ONE) * clipped

time: 1230 us -> 945 us (0.77)
  blocking collectives: 210 us -> 12.4 us
  waiting for transfers between devices: 301 us -> 123 us
  starting transfers between devices: 40.2 us -> 88.8 us
  matrix products: 72.2 us -> 96.4 us
  other arithmetic: 189 us -> 211 us
  between operations: 24.4 us -> 9.57 us
  local copies, waits for them, and re-layouts: 374 us -> 388 us
    psum x5 -> x0, blocking collectives: 210 us -> none  [the longest x2 86.2 us: block_forward(): lax.psum((jnp.sum(depthwise_conv_output * surface_field, axis=(1, 2, 3)),...]
    psum x1 -> x0, waiting for transfers between devices: 189 us -> none  [body(): summed = lax.psum(joined, ('lat', 'lvl'))]
    ppermute x0 -> x10, waiting for transfers between devices: none -> 107 us  [exchange(): return lax.ppermute(values, axis, [(i, i ^ step) for i in range(count)])]
    unnamed x3 -> x0, waiting for transfers between devices: 101 us -> none
    reshape x0 -> x4, local copies, waits for them, and re-layouts: none -> 40.6 us  [the longest x2 17.1 us: to_patches(): split = grid.reshape(chans, batch, rows // 2, 2, cols // 2, 2)]
    all_to_all x0 -> x4, starting transfers between devices: none -> 32.7 us  [total_of(): lax.all_to_all(jnp.broadcast_to(tile, (count, rows, 128)), AXES, 0, 0, ti...]
    transpose x2 -> x1, local copies, waits for them, and re-layouts: 29.2 us -> 2.43 us  [from_patches(): split.transpose(0, 3, 4, 1, 5, 2).reshape(chans, batch, rows * 2, cols * 2)]
    reduce_sum x1 -> x2, other arithmetic: 12.6 us -> 36 us  [block_forward(): jnp.sum(depthwise_conv_output * surface_field, axis=(1, 2, 3))]
  transfers between devices with their start and end apart: 20 -> 32, of which waited for: 8 -> 16; matrix products, arithmetic and copies ran while one was open for 9% -> 15% of each run, Pallas kernels for 0% -> 0%
where the time goes in v1:
time: 945 us; the launch traced here: 929 us
  local copies, waits for them, and re-layouts  388 us (41%)
  other arithmetic  211 us (22%)
  waiting for transfers between devices  123 us (13%)
  matrix products  96.4 us (10%)
  starting transfers between devices  88.8 us (9%)
  blocking collectives  12.4 us (1%)
  between operations  9.57 us (1%)
    ppermute x10, waiting for transfers between devices, exchange(): return lax.ppermute(values, axis, [(i, i ^ step) for i in range(count)])  107 us
    concatenate x1, local copies, waits for them, and re-layouts, body(): joined = jnp.concatenate([piece.reshape(-1) for piece in pieces])  88.5 us
    reduce_sum x6, other arithmetic, block_backward(): jnp.sum(border_padded[:, :, p:p + rows, q:q + cols] * grad_convf, axis=(1...  61.2 us
    dot_general x7, matrix products, contract_rows(): lax.dot_general(left, right, (((0,), (0,)), ((), ())), preferred_element_...  44.2 us
    reduce_sum x2, other arithmetic, block_forward(): jnp.sum(depthwise_conv_output * surface_field, axis=(1, 2, 3))  36 us
    all_to_all x4, starting transfers between devices, total_of(): lax.all_to_all(jnp.broadcast_to(tile, (count, rows, 128)), AXES, 0, 0, ti...  32.7 us
    unnamed x345, local copies, waits for them, and re-layouts  28.6 us
    dot_general x8, matrix products, contract_cells(): lax.dot_general(left, right, (((1,), (1,)), ((), ())), preferred_element_...  27.7 us
  transfers between devices with their start and end apart: 32, of which 16 were waited for; matrix products, arithmetic and copies ran while one was open for 15% of the time, Pallas kernels for 0%

profile of v1, /device:TPU:0, one launch (start us, length us, event | category | flops | bytes accessed | tf_op | source)
XLA Modules:
  0.0 929.2 jit_solution(16812727035241389999)
XLA Ops:
  1.6 4.1 collective-permute-start
  5.7 7.0 collective-permute-done
  13.6 7.5 collective-permute-done.1
  22.6 12.3 %collective-permute-done.2 = bf16[4,576,128]{2,1,0:T(8,128)(2,1)S(1)} collective-permute-done((bf16[4,576,128]{2,1,0:T(8,128)(2,1)S(1)}, bf16[4,576,128]{2,1,0:T(8,128)(2,1)S(1)}, u32[]{:S(2)}, u32[]{:S(2)}) %collective-permute-start.2) | collective-permute-done | bytes 589856 | tf_op jit(solution)/shard_map/ppermute | solution.py:42
  36.5 24.0 %collective-permute-done.3 = bf16[8,576,128]{2,1,0:T(8,128)(2,1)S(1)} collective-permute-done((bf16[8,576,128]{2,1,0:T(8,128)(2,1)S(1)}, bf16[8,576,128]{2,1,0:T(8,128)(2,1)S(1)}, u32[]{:S(2)}, u32[]{:S(2)}) %collective-permute-start.3) | collective-permute-done | bytes 1179680 | tf_op jit(solution)/shard_map/ppermute | solution.py:42
  92.8 3.9 reshape.643
  99.8 4.1 copy.259
  115.8 11.3 %reshape.640 = bf16[2306304]{0:T(1024)(128)(2,1)} reshape(bf16[32,72072]{1,0:T(8,128)(2,1)} %slice.1924) | data formatting | bytes 9225216 | tf_op jit(solution)/shard_map/reshape | solution.py:286
  145.5 3.9 fusion.283
  166.0 5.6 collective-permute-done.6
  179.3 22.8 %multiply_reduce_fusion.3 = (f32[200]{0:T(256)S(1)}, f32[200]{0:T(256)S(1)}, f32[200,2,32,48]{0,3,2,1:T(8,128)S(1)}) fusion(f32[32,48]{1,0:T(8,128)S(1)} %compare_convert_fusion.1, f32[200,2,38,54]{0,3,2,1:T(8,128)S(1)} %maximum_convert_fusion, f32[200]{0:T(256)S(1)} %get-tuple-element.168, f32[200]{0:T(256)S(1)} %get-tuple-element.169, ...), kind=kLoop, calls=%fused_computation.317 | loop fusion | flops 62668400 | bytes 122926944 | tf_op jit(solution)/shard_map/reduce_sum | solution.py:189
  203.0 9.7 %all-to-all-start.1 = ((f32[32,8,128]{2,1,0:T(8,128)}), f32[32,8,128]{2,1,0:T(8,128)S(1)}, u32[]{:S(2)}, u32[]{:S(2)}) async-start(f32[32,8,128]{2,1,0:T(8,128)} %broadcast_in_dim.25), calls=%async_computation.1 | async-start | bytes 262144 | tf_op jit(solution)/shard_map/all_to_all | solution.py:74
  227.7 5.5 reshape.656
  249.2 6.4 multiply_convert_fusion
  261.9 10.7 %copy.254 = bf16[200,2,2,2,16,24]{5,4,3,2,1,0:T(8,128)(2,1)} copy(bf16[200,2,2,2,16,24]{0,2,5,1,4,3:T(2,128)(2,1)S(1)} %bitcast.564) | data formatting | bytes 2457600 | tf_op jit(solution)/shard_map/transpose | solution.py:159
  272.6 10.6 %reshape.654 = bf16[800,768]{1,0:T(8,128)(2,1)} reshape(bf16[200,2,2,2,16,24]{5,4,3,2,1,0:T(8,128)(2,1)} %copy.254) | data formatting | bytes 2457600 | tf_op jit(solution)/shard_map/reshape | solution.py:159
  305.8 13.1 %multiply_reduce_fusion.8 = (f32[400]{0:T(512)S(1)}, f32[400]{0:T(512)S(1)}, f32[400,2,16,24]{0,3,2,1:T(8,128)}) fusion(f32[16,24]{1,0:T(8,128)S(1)} %compare_convert_fusion.2, f32[400,2,22,30]{0,3,2,1:T(8,128)S(1)} %maximum_convert_fusion.2, f32[400]{0:T(512)} %get-tuple-element.119, f32[400]{0:T(512)} %get-tuple-element.120, f32[400]{0:T(512)} %get-tuple-element.121, ...), kind=kLoop, calls=%fused_computation.489 | loop fusion | flops 31333600 | bytes 61523136 | tf_op jit(solution)/shard_map/reduce_sum | solution.py:189
  319.6 8.4 all-to-all-start.2
  343.1 6.4 multiply_convert_fusion.1
  353.9 11.7 %reshape.663 = f32[200,2,2,2,16,24]{5,4,3,2,1,0:T(8,128)} reshape(f32[800,768]{1,0:T(8,128)} %convolution_add_fusion.2) | data formatting | bytes 4915200 | tf_op jit(solution)/shard_map/reshape | solution.py:164
  365.6 15.0 %copy.256 = f32[200,2,2,2,16,24]{0,2,5,1,4,3:T(2,128)} copy(f32[200,2,2,2,16,24]{5,4,3,2,1,0:T(8,128)} %reshape.663) | data formatting | bytes 4915200 | tf_op jit(solution)/shard_map/reshape | solution.py:164
  380.7 5.3 add_convert_fusion
  386.0 4.0 convert_element_type.382
  390.0 5.3 reshape.664
  399.1 4.2 fusion.247
  409.3 3.9 fusion.297
  417.0 13.3 %copy.265 = bf16[200,2,16,2,24,2]{4,2,1,5,3,0:T(8,128)(2,1)} copy(bf16[200,2,16,2,24,2]{0,5,4,3,2,1:T(2,128)(2,1)} %reshape.667) | data formatting | bytes 2457600 | tf_op jit(solution)/shard_map/reshape | solution.py:158
  430.3 10.6 %reshape.668 = bf16[800,768]{1,0:T(8,128)(2,1)} reshape(bf16[200,2,2,2,16,24]{5,4,3,2,1,0:T(8,128)(2,1)} %bitcast.553) | data formatting | bytes 2457600 | tf_op jit(solution)/shard_map/reshape | solution.py:159
  450.1 4.5 convert_reduce_fusion.4
  458.6 4.2 reshape.685
  462.8 9.4 %fusion.30 = (bf16[768,1600]{0,1:T(8,128)(2,1)}, f32[1600,768]{1,0:T(8,128)S(1)}) fusion(f32[1600,768]{1,0:T(8,128)} %get-tuple-element.395, f32[1600]{0:T(1024)S(1)} %copy-done.45, bf16[400,1600]{1,0:T(8,128)(2,1)} %reshape.655, bf16[400,768]{0,1:T(8,128)(2,1)} %bitcast.805), kind=kOutput, calls=%fused_computation.142 | convolution fusion | flops 1008844800 | bytes 14188800 | tf_op jit(solution)/shard_map/dot_general | solution.py:179
  472.2 7.8 convert_reduce_fusion.2
  479.9 4.5 copy.269
  484.4 6.3 multiply_reduce_fusion.5
  491.5 6.0 all-to-all-start.4
  497.4 5.1 fusion.302
  502.6 5.5 reshape.684
  508.1 5.1 convert_reduce_fusion
  513.9 6.4 fusion.189
  525.4 4.7 fusion.190
  535.1 3.9 fusion.188
  539.3 5.2 stack.459
  547.7 12.6 %convert_reduce_fusion.5 = (f32[400]{0:T(512)}, bf16[400,2,16,24]{0,3,2,1:T(8,128)(2,1)S(1)}) fusion(f32[400,2,16,24]{0,3,2,1:T(8,128)} %get-tuple-element.399, f32[400,2,22,30]{0,3,2,1:T(8,128)S(1)} %maximum_convert_fusion.3, f32[400]{0:T(512)S(1)} %bitcast.687, f32[400]{0:T(512)S(1)} %bitcast.688, f32[400]{0:T(512)S(1)} %bitcast.689, ...), kind=kLoop, calls=%fused_computation.484 | loop fusion | flops 31026800 | bytes 62134400 | tf_op jit(solution)/shard_map/reduce_sum | solution.py:347
  571.8 5.7 convert_reduce_fusion.3
  577.5 5.4 fusion.300
  585.4 11.9 %fusion.13 = (bf16[3072,800]{0,1:T(8,128)(2,1)}, f32[800,3072]{1,0:T(8,128)S(1)}) fusion(f32[800,3072]{1,0:T(8,128)} %get-tuple-element.393, f32[800]{0:T(1024)S(1)} %copy-done.53, bf16[200,800]{1,0:T(8,128)(2,1)S(1)} %copy-done.32, bf16[200,3072]{0,1:T(8,128)(2,1)S(1)} %bitcast.596), kind=kOutput, calls=%fused_computation.116 | convolution fusion | flops 1034649600 | bytes 26128000 | tf_op jit(solution)/shard_map/dot_general | solution.py:179
  597.3 10.0 %convert_reduce_fusion.1 = (f32[800]{0:T(1024)}, bf16[800,3072]{1,0:T(8,128)(2,1)}) fusion(f32[800,3072]{1,0:T(8,128)S(1)} %get-tuple-element.404, f32[800,3072]{1,0:T(8,128)S(1)} %bitcast.567, f32[800]{0:T(1024)S(1)} %copy-done.53), kind=kLoop, calls=%fused_computation.122 | loop fusion | flops 56524000 | bytes 24582400 | tf_op jit(solution)/shard_map/reduce_sum | solution.py:245
  607.3 7.9 copy.274
  615.2 7.3 multiply_reduce_fusion
  623.3 8.7 all-to-all-start.5
  632.1 4.3 fusion.299
  641.0 30.0 %fusion.86 = (f32[200]{0:T(256)S(1)}, f32[200]{0:T(256)S(1)}, f32[200]{0:T(256)S(1)}, f32[200]{0:T(256)S(1)}, f32[200]{0:T(256)S(1)}, /*index=5*/f32[200]{0:T(25...) fusion(f32[200,2,38,54]{0,3,2,1:T(8,128)} %copy-done, ...), kind=kLoop, calls=%fused_computation.209 | loop fusion | flops 28258800 | bytes 50405344 | tf_op jit(solution)/shard_map/reduce_sum | solution.py:269
  675.0 9.2 fusion.87
  687.9 6.9 fusion.85
  698.3 23.4 %fusion.90 = bf16[200,2,32,48]{0,3,2,1:T(8,128)(2,1)} fusion(f32[200,2,32,48]{0,3,2,1:T(8,128)S(1)} %copy-done.5, f32[200,2,38,54]{0,3,2,1:T(8,128)S(1)} %maximum_convert_fusion.1, f32[200]{0:T(256)S(1)} %bitcast.737, f32[200]{0:T(256)} %bitcast.738, f32[200]{0:T(256)} %bitcast.739, f32[200]{0:T(256)} %bitcast.740, f32[200]{0:T(256)} %bitcast.741, ...), kind=kLoop, calls=%fused_computation.214 | loop fusion | flops 60825600 | bytes 124148000 | tf_op jit(solution)/shard_map/convert_element_type | solution.py:352
  723.8 88.5 %concatenate.54 = f32[2306280]{0:T(1024)} concatenate(f32[16000]{0:T(1024)S(1)} %reshape.678, f32[9800]{0:T(1024)S(1)} %reshape.679, f32[200]{0:T(256)} %get-tuple-element.6, f32[200]{0:T(256)} %get-tuple-element.111, f32[160000]{0:T(1024)} %reshape.680, f32[800]{0:T(1024)S(1)} %copy-done.51, f32[160000]{0:T(1024)} %reshape.681, f32[200]{0:T(256)} %get-tuple-element.228, ...), dimensions={0} | concatenate | bytes 18450240 | tf_op jit(solution)/shard_map/concatenate | solution.py:361
  812.3 8.7 pad.37
  821.0 12.2 %reshape.688 = f32[32,72072]{1,0:T(8,128)} reshape(f32[2306304]{0:T(1024)} %pad.37) | data formatting | bytes 18450432 | tf_op jit(solution)/shard_map/reshape | solution.py:363
  833.3 4.2 pad_bitcast_fusion
  841.7 7.5 collective-permute-done.21
  852.3 26.3 %collective-permute-done.22 = bf16[8,576,128]{2,1,0:T(8,128)(2,1)S(1)} collective-permute-done((bf16[8,576,128]{2,1,0:T(8,128)(2,1)S(1)}, bf16[8,576,128]{2,1,0:T(8,128)(2,1)S(1)}, u32[]{:S(2)}, u32[]{:S(2)}) %collective-permute-start.22) | collective-permute-done | bytes 1179680 | tf_op jit(solution)/shard_map/ppermute | solution.py:42
  881.8 13.1 %collective-permute-done.23 = bf16[4,576,128]{2,1,0:T(8,128)(2,1)S(1)} collective-permute-done((bf16[4,576,128]{2,1,0:T(8,128)(2,1)S(1)}, bf16[4,576,128]{2,1,0:T(8,128)(2,1)S(1)}, u32[]{:S(2)}, u32[]{:S(2)}) %collective-permute-start.23) | collective-permute-done | bytes 589856 | tf_op jit(solution)/shard_map/ppermute | solution.py:42
  897.7 5.8 collective-permute-done.24
  913.1 12.4 %all_to_all.49 = f32[32,8,128]{2,1,0:T(8,128)S(1)} all-to-all(f32[32,8,128]{2,1,0:T(8,128)S(1)} %broadcast_in_dim.34), channel_id=1, replica_groups=mesh['lat'=8,'lvl'=4] {'lat','lvl'}, dimensions={0} | all-to-all | bytes 262144 | tf_op jit(solution)/shard_map/all_to_all | solution.py:74
  (562 shorter events, 268.5 us)
Async XLA Ops:
  1.6 11.1 %collective-permute-start = (bf16[1,576,128]{2,1,0:T(8,128)(2,1)S(1)}, bf16[1,576,128]{2,1,0:T(8,128)(2,1)S(1)}, u32[]{:S(2)}, u32[]{:S(2)}) collective-permute-start(bf16[1,576,128]{2,1,0:T(8,128)(2,1)S(1)} %pad_bitcast_fusion.1), channel_id=1, source_target_pairs={{0,16},{4,20},{8,24},{12,28},{16,0},{20,4},{24,8},{28,12},{1,17},{... | collective-permute-start | bytes 442376 | tf_op jit(solution)/shard_map/ppermute | solution.py:42
  12.8 8.3 collective-permute-start.1
  21.2 13.7 %collective-permute-start.2 = (bf16[4,576,128]{2,1,0:T(8,128)(2,1)S(1)}, bf16[4,576,128]{2,1,0:T(8,128)(2,1)S(1)}, u32[]{:S(2)}, u32[]{:S(2)}) collective-permute-start(bf16[4,576,128]{2,1,0:T(8,128)(2,1)S(1)} %bitcast.592), channel_id=1, source_target_pairs={{0,4},{4,0},{8,12},{12,8},{16,20},{20,16},{24,28},{28,24},{1,5},{5... | collective-permute-start | bytes 1769480 | tf_op jit(solution)/shard_map/ppermute | solution.py:42
  35.1 25.4 %collective-permute-start.3 = (bf16[8,576,128]{2,1,0:T(8,128)(2,1)S(1)}, bf16[8,576,128]{2,1,0:T(8,128)(2,1)S(1)}, u32[]{:S(2)}, u32[]{:S(2)}) collective-permute-start(bf16[8,576,128]{2,1,0:T(8,128)(2,1)S(1)} %bitcast.584), channel_id=1, source_target_pairs={{0,2},{1,3},{2,0},{3,1},{4,6},{5,7},{6,4},{7,5},{8,10},{9,11},{10,... | collective-permute-start | bytes 3538952 | tf_op jit(solution)/shard_map/ppermute | solution.py:42
  62.4 10.6 %copy-start.156 = (s32[19]{0:T(128)S(1)}, s32[19]{0:T(128)}, u32[]{:S(2)}) copy-start(s32[19]{0:T(128)} %param.10) | copy-start | bytes 232
  62.4 44.8 %collective-permute-start.4 = (bf16[16,576,128]{2,1,0:T(8,128)(2,1)}, bf16[16,576,128]{2,1,0:T(8,128)(2,1)}, u32[]{:S(2)}, u32[]{:S(2)}) collective-permute-start(bf16[16,576,128]{2,1,0:T(8,128)(2,1)} %bitcast.16), channel_id=1, source_target_pairs={{0,1},{1,0},{2,3},{3,2},{4,5},{5,4},{6,7},{7,6},{8,9},{9,8},{10,11... | collective-permute-start | bytes 7077896 | tf_op jit(solution)/shard_map/ppermute | solution.py:42
  66.5 16.6 %all-to-all-start = ((bf16[4,2,30720]{2,1,0:T(2,128)(2,1)}), bf16[4,2,30720]{2,1,0:T(2,128)(2,1)S(1)}, u32[]{:S(2)}, u32[]{:S(2)}) async-start(bf16[4,2,30720]{2,1,0:T(2,128)(2,1)} %reshape.808), calls=%async_computation | async-start | bytes 983040 | tf_op jit(solution)/shard_map/all_to_all | solution.py:300
  71.5 10.8 %copy-start.117 = (s32[80]{0:T(128)}, s32[80]{0:T(128)S(1)}, u32[]{:S(2)}) copy-start(s32[80]{0:T(128)S(1)} %fusion.271) | copy-start | bytes 964
  73.5 105.8 %copy-start.26 = (f32[32,48]{1,0:T(8,128)}, f32[32,48]{1,0:T(8,128)S(1)}, u32[]{:S(2)}) copy-start(f32[32,48]{1,0:T(8,128)S(1)} %compare_convert_fusion.1) | copy-start | bytes 18436
  83.1 13.6 %all-to-all-start.3 = ((bf16[4,2,30720]{2,1,0:T(2,128)(2,1)}), bf16[4,2,30720]{2,1,0:T(2,128)(2,1)S(1)}, u32[]{:S(2)}, u32[]{:S(2)}) async-start(bf16[4,2,30720]{2,1,0:T(2,128)(2,1)} %reshape.810), calls=%async_computation.3 | async-start | bytes 983040 | tf_op jit(solution)/shard_map/all_to_all | solution.py:301
  129.2 120.0 %copy-start.52 = (f32[800]{0:T(1024)}, f32[800]{0:T(1024)S(1)}, u32[]{:S(2)}) copy-start(f32[800]{0:T(1024)S(1)} %slice_convert_fusion.3) | copy-start | bytes 9604
  130.6 118.0 %copy-start.54 = (f32[200]{0:T(256)}, f32[200]{0:T(256)S(1)}, u32[]{:S(2)}) copy-start(f32[200]{0:T(256)S(1)} %get-tuple-element.245) | copy-start | bytes 2404
  158.3 13.4 %copy-start.9 = (bf16[200,3072]{1,0:T(8,128)(2,1)}, bf16[200,3072]{1,0:T(8,128)(2,1)S(1)}, u32[]{:S(2)}) copy-start(bf16[200,3072]{1,0:T(8,128)(2,1)S(1)} %convolution_convert_fusion) | copy-start | bytes 3686404
  159.0 7.0 collective-permute-start.5
  162.3 9.3 %collective-permute-start.6 = (bf16[200,2,3,48]{0,3,2,1:T(8,128)(2,1)S(1)}, bf16[200,2,3,48]{0,3,2,1:T(8,128)(2,1)S(1)}, u32[]{:S(2)}, u32[]{:S(2)}) collective-permute-start(bf16[200,2,3,48]{0,3,2,1:T(8,128)(2,1)S(1)} %get-tuple-element.267), channel_id=1, source_target_pairs={{4,0},{8,4},{12,8},{16,12},{20,16},{24,20},{28,24},{5,1},{9,5},{13... | collective-permute-start | bytes 345608 | tf_op jit(solution)/shard_map/ppermute | solution.py:94
  171.7 3.7 collective-permute-start.7
  173.3 4.9 collective-permute-start.8
  179.3 22.9 %copy-start = (f32[200,2,38,54]{0,3,2,1:T(8,128)}, f32[200,2,38,54]{0,3,2,1:T(8,128)S(1)}, u32[]{:S(2)}) copy-start(f32[200,2,38,54]{0,3,2,1:T(8,128)S(1)} %maximum_convert_fusion) | copy-start | bytes 9849604
  202.2 46.4 %copy-start.1 = (f32[200,2,32,48]{0,3,2,1:T(8,128)}, f32[200,2,32,48]{0,3,2,1:T(8,128)S(1)}, u32[]{:S(2)}) copy-start(f32[200,2,32,48]{0,3,2,1:T(8,128)S(1)} %get-tuple-element.239) | copy-start | bytes 7372804
  202.2 13.5 %copy-start.34 = (bf16[16000]{0:T(1024)(128)(2,1)S(1)}, bf16[16000]{0:T(1024)(128)(2,1)}, u32[]{:S(2)}) copy-start(bf16[16000]{0:T(1024)(128)(2,1)} %get-tuple-element.256) | copy-start | bytes 96004
  203.0 44.2 %all-to-all-start.1 = ((f32[32,8,128]{2,1,0:T(8,128)}), f32[32,8,128]{2,1,0:T(8,128)S(1)}, u32[]{:S(2)}, u32[]{:S(2)}) async-start(f32[32,8,128]{2,1,0:T(8,128)} %broadcast_in_dim.25), calls=%async_computation.1 | async-start | bytes 262144 | tf_op jit(solution)/shard_map/all_to_all | solution.py:74
  261.9 10.7 %copy-start.4 = (bf16[200,2,16,2,24,2]{0,5,4,3,2,1:T(2,128)(2,1)}, bf16[200,2,16,2,24,2]{0,5,4,3,2,1:T(2,128)(2,1)S(1)}, u32[]{:S(2)}) copy-start(bf16[200,2,16,2,24,2]{0,5,4,3,2,1:T(2,128)(2,1)S(1)} %convert_element_type.330) | copy-start | bytes 3686404
  272.6 10.6 %copy-start.15 = (bf16[400,800]{1,0:T(8,128)(2,1)S(1)}, bf16[400,800]{1,0:T(8,128)(2,1)}, u32[]{:S(2)}) copy-start(bf16[400,800]{1,0:T(8,128)(2,1)} %reshape.653) | copy-start | bytes 1920004
  272.6 10.6 %copy-start.153 = (f32[400]{0:T(512)S(1)}, f32[400]{0:T(512)}, u32[]{:S(2)}) copy-start(f32[400]{0:T(512)} %get-tuple-element.249) | copy-start | bytes 4804
  285.6 16.2 %copy-start.7 = (bf16[400,768]{0,1:T(8,128)(2,1)}, bf16[400,768]{0,1:T(8,128)(2,1)S(1)}, u32[]{:S(2)}) copy-start(bf16[400,768]{0,1:T(8,128)(2,1)S(1)} %copy.255) | copy-start | bytes 1843204
  285.6 8.1 collective-permute-start.9
  289.4 7.5 collective-permute-start.10
  297.1 5.5 collective-permute-start.11
  298.5 5.1 collective-permute-start.12
  319.6 19.5 %all-to-all-start.2 = ((f32[32,8,128]{2,1,0:T(8,128)}), f32[32,8,128]{2,1,0:T(8,128)}, u32[]{:S(2)}, u32[]{:S(2)}) async-start(f32[32,8,128]{2,1,0:T(8,128)} %broadcast_in_dim.27), calls=%async_computation.2 | async-start | bytes 262144 | tf_op jit(solution)/shard_map/all_to_all | solution.py:74
  333.9 9.1 copy-start.45
  430.3 10.6 %copy-start.160 = (bf16[400,768]{1,0:T(8,128)(2,1)S(1)}, bf16[400,768]{1,0:T(8,128)(2,1)}, u32[]{:S(2)}) copy-start(bf16[400,768]{1,0:T(8,128)(2,1)} %copy-done.159) | copy-start | bytes 1843204
  491.5 21.7 %all-to-all-start.4 = ((f32[32,8,128]{2,1,0:T(8,128)}), f32[32,8,128]{2,1,0:T(8,128)S(1)}, u32[]{:S(2)}, u32[]{:S(2)}) async-start(f32[32,8,128]{2,1,0:T(8,128)} %broadcast_in_dim.30), calls=%async_computation.4 | async-start | bytes 262144 | tf_op jit(solution)/shard_map/all_to_all | solution.py:74
  520.3 14.8 %copy-start.3 = (bf16[400,2,16,24]{0,3,2,1:T(8,128)(2,1)}, bf16[400,2,16,24]{0,3,2,1:T(8,128)(2,1)S(1)}, u32[]{:S(2)}) copy-start(bf16[400,2,16,24]{0,3,2,1:T(8,128)(2,1)S(1)} %get-tuple-element.225) | copy-start | bytes 1843204
  520.3 9.8 %collective-permute-start.13 = (bf16[400,2,3,24]{0,3,2,1:T(8,128)(2,1)S(1)}, bf16[400,2,3,24]{0,3,2,1:T(8,128)(2,1)S(1)}, u32[]{:S(2)}, u32[]{:S(2)}) collective-permute-start(bf16[400,2,3,24]{0,3,2,1:T(8,128)(2,1)S(1)} %get-tuple-element.274), channel_id=1, source_target_pairs={{0,4},{4,8},{8,12},{12,16},{16,20},{20,24},{24,28},{1,5},{5,9},{9,... | collective-permute-start | bytes 345608 | tf_op jit(solution)/shard_map/ppermute | solution.py:92
  524.1 7.5 collective-permute-start.14
  532.5 13.0 %collective-permute-start.15 = (bf16[400,2,22,3]{0,3,2,1:T(4,128)(2,1)}, bf16[400,2,22,3]{0,3,2,1:T(4,128)(2,1)S(1)}, u32[]{:S(2)}, u32[]{:S(2)}) collective-permute-start(bf16[400,2,22,3]{0,3,2,1:T(4,128)(2,1)} %get-tuple-element.270), channel_id=1, source_target_pairs={{0,1},{1,2},{2,3},{4,5},{5,6},{6,7},{8,9},{9,10},{10,11},{12,13},{... | collective-permute-start | bytes 316808 | tf_op jit(solution)/shard_map/ppermute | solution.py:92
  533.8 11.7 %collective-permute-start.16 = (bf16[400,2,22,3]{0,3,2,1:T(4,128)(2,1)}, bf16[400,2,22,3]{0,3,2,1:T(4,128)(2,1)S(1)}, u32[]{:S(2)}, u32[]{:S(2)}) collective-permute-start(bf16[400,2,22,3]{0,3,2,1:T(4,128)(2,1)} %get-tuple-element.271), channel_id=1, source_target_pairs={{1,0},{2,1},{3,2},{5,4},{6,5},{7,6},{9,8},{10,9},{11,10},{13,12},{... | collective-permute-start | bytes 316808 | tf_op jit(solution)/shard_map/ppermute | solution.py:94
  577.5 19.8 %slice-start.2 = ((s8[9830400]{0:T(1024)(128)(4,1)}), s8[1441792]{0:T(1024)(128)(4,1)S(1)}, s32[]{:S(2)}) async-start(s8[9830400]{0:T(1024)(128)(4,1)} %bitcast.566), calls=%async_computation.9 | async-start | bytes 2883584
  585.4 11.9 %slice-start.3 = ((s8[9830400]{0:T(1024)(128)(4,1)}), s8[4194304]{0:T(1024)(128)(4,1)S(1)}, s32[]{:S(2)}) async-start(s8[9830400]{0:T(1024)(128)(4,1)} %bitcast.566), calls=%async_computation.10 | async-start | bytes 8388608
  585.4 11.9 %slice-start.4 = ((s8[9830400]{0:T(1024)(128)(4,1)}), s8[4194304]{0:T(1024)(128)(4,1)S(1)}, s32[]{:S(2)}) async-start(s8[9830400]{0:T(1024)(128)(4,1)} %bitcast.566), calls=%async_computation.11 | async-start | bytes 8388608
  623.3 17.0 %all-to-all-start.5 = ((f32[32,8,128]{2,1,0:T(8,128)}), f32[32,8,128]{2,1,0:T(8,128)S(1)}, u32[]{:S(2)}, u32[]{:S(2)}) async-start(f32[32,8,128]{2,1,0:T(8,128)} %broadcast_in_dim.32), calls=%async_computation.5 | async-start | bytes 262144 | tf_op jit(solution)/shard_map/all_to_all | solution.py:74
  641.0 34.0 %slice-start = ((s8[4358144]{0:T(1024)(128)(4,1)}), s8[4194304]{0:T(1024)(128)(4,1)S(1)}, s32[]{:S(2)}) async-start(s8[4358144]{0:T(1024)(128)(4,1)} %bitcast.549), calls=%async_computation.7 | async-start | bytes 8388608
  641.0 34.0 %slice-start.1 = ((s8[4358144]{0:T(1024)(128)(4,1)}), s8[163840]{0:T(1024)(128)(4,1)S(1)}, s32[]{:S(2)}) async-start(s8[4358144]{0:T(1024)(128)(4,1)} %bitcast.549), calls=%async_computation.8 | async-start | bytes 327680
  671.1 13.1 %collective-permute-start.17 = (bf16[200,2,3,48]{0,3,2,1:T(8,128)(2,1)S(1)}, bf16[200,2,3,48]{0,3,2,1:T(8,128)(2,1)S(1)}, u32[]{:S(2)}, u32[]{:S(2)}) collective-permute-start(bf16[200,2,3,48]{0,3,2,1:T(8,128)(2,1)S(1)} %get-tuple-element.264), channel_id=1, source_target_pairs={{0,4},{4,8},{8,12},{12,16},{16,20},{20,24},{24,28},{1,5},{5,9},{9,... | collective-permute-start | bytes 345608 | tf_op jit(solution)/shard_map/ppermute | solution.py:92
  673.7 10.6 %collective-permute-start.18 = (bf16[200,2,3,48]{0,3,2,1:T(8,128)(2,1)S(1)}, bf16[200,2,3,48]{0,3,2,1:T(8,128)(2,1)S(1)}, u32[]{:S(2)}, u32[]{:S(2)}) collective-permute-start(bf16[200,2,3,48]{0,3,2,1:T(8,128)(2,1)S(1)} %get-tuple-element.265), channel_id=1, source_target_pairs={{4,0},{8,4},{12,8},{16,12},{20,16},{24,20},{28,24},{5,1},{9,5},{13... | collective-permute-start | bytes 345608 | tf_op jit(solution)/shard_map/ppermute | solution.py:94
  685.1 10.6 %collective-permute-start.19 = (bf16[200,2,38,3]{0,3,2,1:T(4,128)(2,1)}, bf16[200,2,38,3]{0,3,2,1:T(4,128)(2,1)S(1)}, u32[]{:S(2)}, u32[]{:S(2)}) collective-permute-start(bf16[200,2,38,3]{0,3,2,1:T(4,128)(2,1)} %get-tuple-element.260), channel_id=1, source_target_pairs={{0,1},{1,2},{2,3},{4,5},{5,6},{6,7},{8,9},{9,10},{10,11},{12,13},{... | collective-permute-start | bytes 273608 | tf_op jit(solution)/shard_map/ppermute | solution.py:92
  686.6 9.1 collective-permute-start.20
  698.2 23.4 %copy-start.12 = (bf16[80,3072]{1,0:T(8,128)(2,1)S(1)}, bf16[80,3072]{1,0:T(8,128)(2,1)}, u32[]{:S(2)}) copy-start(bf16[80,3072]{1,0:T(8,128)(2,1)} %reshape.643) | copy-start | bytes 1474564
  698.2 25.6 %copy-start.6 = (f32[640000]{0:T(1024)S(1)}, f32[640000]{0:T(1024)}, u32[]{:S(2)}) copy-start(f32[640000]{0:T(1024)} %reshape.685) | copy-start | bytes 7680004
  698.2 25.6 %copy-start.33 = (f32[19600]{0:T(1024)S(1)}, f32[19600]{0:T(1024)}, u32[]{:S(2)}) copy-start(f32[19600]{0:T(1024)} %reshape.683) | copy-start | bytes 235204
  698.2 25.6 %copy-start.37 = (f32[16000]{0:T(1024)S(1)}, f32[16000]{0:T(1024)}, u32[]{:S(2)}) copy-start(f32[16000]{0:T(1024)} %reshape.687) | copy-start | bytes 192004
  698.2 25.6 %copy-start.44 = (f32[1600]{0:T(1024)S(1)}, f32[1600]{0:T(1024)}, u32[]{:S(2)}) copy-start(f32[1600]{0:T(1024)} %get-tuple-element.223) | copy-start | bytes 19204
  698.2 25.6 %copy-start.51 = (f32[800]{0:T(1024)S(1)}, f32[800]{0:T(1024)}, u32[]{:S(2)}) copy-start(f32[800]{0:T(1024)} %get-tuple-element.231) | copy-start | bytes 9604
  698.3 25.6 %copy-start.75 = (f32[400]{0:T(512)S(1)}, f32[400]{0:T(512)}, u32[]{:S(2)}) copy-start(f32[400]{0:T(512)} %get-tuple-element.226) | copy-start | bytes 4804
  839.7 9.5 %collective-permute-start.21 = (f32[16,576,128]{2,1,0:T(8,128)S(1)}, f32[16,576,128]{2,1,0:T(8,128)S(1)}, u32[]{:S(2)}, u32[]{:S(2)}) collective-permute-start(f32[16,576,128]{2,1,0:T(8,128)S(1)} %select_bitcast_fusion), channel_id=1, source_target_pairs={{0,1},{1,0},{2,3},{3,2},{4,5},{5,4},{6,7},{7,6},{8,9},{9,8},{10,11... | collective-permute-start | bytes 14155784 | tf_op jit(solution)/shard_map/ppermute | solution.py:42
  850.2 28.3 %collective-permute-start.22 = (bf16[8,576,128]{2,1,0:T(8,128)(2,1)S(1)}, bf16[8,576,128]{2,1,0:T(8,128)(2,1)S(1)}, u32[]{:S(2)}, u32[]{:S(2)}) collective-permute-start(bf16[8,576,128]{2,1,0:T(8,128)(2,1)S(1)} %fusion.244), channel_id=1, source_target_pairs={{0,2},{1,3},{2,0},{3,1},{4,6},{5,7},{6,4},{7,5},{8,10},{9,11},{10,... | collective-permute-start | bytes 3538952 | tf_op jit(solution)/shard_map/ppermute | solution.py:42
  879.1 27.4 %copy-start.42 = (f32[3072]{0:T(1024)S(1)}, f32[3072]{0:T(1024)}, u32[]{:S(2)}) copy-start(f32[3072]{0:T(1024)} %copy-done.41) | copy-start | bytes 36868
  879.1 15.8 %collective-permute-start.23 = (bf16[4,576,128]{2,1,0:T(8,128)(2,1)S(1)}, bf16[4,576,128]{2,1,0:T(8,128)(2,1)S(1)}, u32[]{:S(2)}, u32[]{:S(2)}) collective-permute-start(bf16[4,576,128]{2,1,0:T(8,128)(2,1)S(1)} %fusion.252), channel_id=1, source_target_pairs={{0,4},{4,0},{8,12},{12,8},{16,20},{20,16},{24,28},{28,24},{1,5},{5... | collective-permute-start | bytes 1769480 | tf_op jit(solution)/shard_map/ppermute | solution.py:42
  895.0 31.8 %copy-start.18 = (f32[72072]{0:T(1024)S(1)}, f32[72072]{0:T(1024)}, u32[]{:S(2)}) copy-start(f32[72072]{0:T(1024)} %param.11) | copy-start | bytes 864868
  895.0 31.8 %copy-start.35 = (f32[72072]{0:T(1024)S(1)}, f32[72072]{0:T(1024)}, u32[]{:S(2)}) copy-start(f32[72072]{0:T(1024)} %param.12) | copy-start | bytes 864868
  895.1 31.8 %copy-start.36 = (f32[72072]{0:T(1024)S(1)}, f32[72072]{0:T(1024)}, u32[]{:S(2)}) copy-start(f32[72072]{0:T(1024)} %param.13) | copy-start | bytes 864868
  895.1 8.5 collective-permute-start.24
  903.7 7.9 collective-permute-start.25
  (136 other events, 743.4 us)

commit v2 on v0

v2 whole, which is shorter than its diff:
```python
import math

import jax
import jax.numpy as jnp
from jax import lax
from jax.experimental import pallas as pl
from jax.experimental.pallas import tpu as pltpu
from jax.sharding import PartitionSpec as P

CIN = 80
WIDTH = 200
EXPAND = 800
WIDTH2 = 400
EXPAND2 = 1600
KSIZE = 7
TAPS = KSIZE * KSIZE
LEVELS = 19
STEP = 10

CLIP = 0.01
LRATE = 0.05
BETA_ONE = 0.9
BETA_TWO = 0.999
ADAM_EPS = 1e-08
DECAY = 0.1
HEAT_WEIGHT = 40.0
NORM_EPS = 1e-05

AXES = ("lat", "lvl")

CI = 128
C1 = 256
H1 = 896
C2 = 512
H2 = 1664
BLOCKS = 8
LANES = 128
REACH = KSIZE // 2
GROUPS = 17

f32 = jnp.float32
bf16 = jnp.bfloat16
VMEM_LIMIT = 60 * 1024 * 1024


def bit_list():
    bits = []
    for axis in AXES:
        count = lax.axis_size(axis)
        step = count // 2
        while step >= 1:
            bits.append((axis, count, step))
            step //= 2
    return bits


def exchange(values, axis, count, step):
    return lax.ppermute(values, axis, [(i, i ^ step) for i in range(count)])


def gather_blocks(block):
    blocks = block[None]
    for axis, count, step in bit_list():
        blocks = jnp.concatenate([blocks, exchange(blocks, axis, count, step)], axis=0)
    return blocks


def scatter_blocks(keep, send):
    for turn, (axis, count, step) in enumerate(reversed(bit_list())):
        if turn > 0:
            half = keep.shape[0] // 2
            keep, send = keep[:half], keep[half:].astype(bf16)
        keep = keep + exchange(send, axis, count, step).astype(f32)
    return keep[0]


def spread(tile):
    count = lax.axis_size(AXES)
    copies = jnp.broadcast_to(tile[None], (count,) + tile.shape)
    return lax.all_to_all(copies, AXES, 0, 0, tiled=True)


def neighbours(axis):
    ends = lax.axis_size(axis) - 1
    return [(i, i + 1) for i in range(ends)], [(i + 1, i) for i in range(ends)]


def with_halo(cells):
    rows, cols, blocks, chans = cells.shape
    bands = blocks // 2
    onward, back = neighbours("lvl")
    left = lax.ppermute(cells[:, cols - REACH :], "lvl", onward)
    right = lax.ppermute(cells[:, :REACH], "lvl", back)
    cells = jnp.concatenate([left, cells, right], axis=1)
    cells = cells.reshape(rows, cols + 2 * REACH, 2, bands, chans)
    onward, back = neighbours("lat")
    above = lax.ppermute(cells[rows - REACH :, :, :, bands - 1], "lat", onward)
    below = lax.ppermute(cells[:REACH, :, :, 0], "lat", back)
    top = jnp.concatenate([above[:, :, :, None], cells[rows - REACH :, :, :, : bands - 1]], axis=3)
    bottom = jnp.concatenate([cells[:REACH, :, :, 1:], below[:, :, :, None]], axis=3)
    return jnp.concatenate([top, cells, bottom], axis=0).reshape(
        rows + 2 * REACH, cols + 2 * REACH, blocks, chans
    )


def to_cells(grid):
    chans, batch, rows, cols = grid.shape
    bands = BLOCKS // batch
    split = grid.reshape(chans, batch, bands, rows // bands, cols)
    return split.transpose(3, 4, 1, 2, 0).reshape(rows // bands, cols, BLOCKS, chans)


def depth_cells(depth, batch):
    rows, cols = depth.shape
    bands = BLOCKS // batch
    split = depth.reshape(bands, rows // bands, cols).transpose(1, 2, 0)
    return jnp.concatenate([split] * batch, axis=2)


def block_shapes(chans, hidden):
    return [
        (chans, TAPS),
        (chans,),
        (chans,),
        (hidden, chans),
        (hidden,),
        (chans, hidden),
        (chans,),
    ]


def shapes_of():
    return (
        [(WIDTH, CIN)]
        + block_shapes(WIDTH, EXPAND)
        + [(WIDTH2, 4 * WIDTH), (WIDTH2,)]
        + block_shapes(WIDTH2, EXPAND2)
        + [(4 * WIDTH, WIDTH2), (WIDTH,), (CIN, WIDTH), (CIN,)]
    )


def fill(values, *shape):
    return jnp.pad(values, [(0, n - m) for n, m in zip(shape, values.shape)])


def nt(left, right):
    return lax.dot_general(left, right, (((1,), (1,)), ((), ())), preferred_element_type=f32)


def nn(left, right):
    return lax.dot_general(left, right, (((1,), (0,)), ((), ())), preferred_element_type=f32)


def tn(left, right):
    return lax.dot_general(left, right, (((0,), (0,)), ((), ())), preferred_element_type=f32)


def rows8(start, amount):
    return pl.ds(pl.multiple_of(start * 8, 8), amount * 8)


def convolve(source, taps, rows, cols, emit, carry, flip=False):
    width = cols + 2 * REACH
    strips = cols // 8

    def strip(turn, carry):
        row = turn // strips
        col = (turn % strips) * 8
        total = jnp.zeros((8, 8, LANES), f32)
        for p in range(KSIZE):
            seen = source[rows8((row + p) * width + col, 8 + 2 * REACH), :]
            seen = seen.reshape(8 + 2 * REACH, 8, LANES)
            for q in range(KSIZE):
                tap = p * KSIZE + q
                total = total + seen[q : q + 8] * taps[TAPS - 1 - tap if flip else tap][None]
        return emit(rows8(row * cols + col, 8), total, carry)

    return lax.fori_loop(0, rows * strips, strip, carry)


def row_sum(values):
    return jnp.sum(values, axis=0, keepdims=True)


def norm_rows(got):
    total = jnp.sum(got[...], axis=0)
    cells = total[2:3]
    mean = total[0:1] / cells
    inverse = lax.rsqrt(total[1:2] / cells - mean * mean + NORM_EPS)
    return mean, inverse, cells, total[3:4]


def gelu_pair(act):
    square = act * act
    flat = 0.7978845608028654
    cube = 0.044715
    bent = jnp.tanh(act * (flat + (flat * cube) * square))
    half = 0.5 + 0.5 * bent
    slope = half + 0.5 * act * (1.0 - bent * bent) * (flat + (3.0 * flat * cube) * square)
    return act * half, slope


def quarter(values, rows, cols, p, q):
    chans = values.shape[-1]
    split = values.reshape(rows // 2, 2, cols // 2, 2, 8, chans)
    return split[:, p, :, q].reshape(rows * cols * 2, chans)


def from_quarters(parts, rows, cols):
    chans = parts[0].shape[-1]
    cells = [part.reshape(rows // 2, cols // 2, 8, chans) for part in parts]
    lines = [jnp.stack(cells[2 * p : 2 * p + 2], axis=2) for p in range(2)]
    return jnp.stack(lines, axis=1).reshape(rows * cols * 8, chans)


def call(kernel, outs, grid=(), ins=None, out_specs=None, scratch=(), flops=0, name=None):
    params = dict(out_shape=[jax.ShapeDtypeStruct(s, t) for s, t in outs])
    if ins:
        params.update(in_specs=ins)
    if grid:
        params.update(grid=grid, out_specs=out_specs)
    return pl.pallas_call(
        kernel,
        scratch_shapes=list(scratch),
        compiler_params=pltpu.CompilerParams(vmem_limit_bytes=VMEM_LIMIT),
        cost_estimate=pl.CostEstimate(flops=flops, bytes_accessed=1000000, transcendentals=0),
        name=name,
        **params,
    )


def whole(*shape):
    return pl.BlockSpec(shape, lambda i: (0,) * len(shape))


def band(rows, cols):
    return pl.BlockSpec((rows, cols), lambda i: (i, 0))


def lane_tile(rows):
    return pl.BlockSpec((rows, LANES), lambda i: (0, i))


TAP_TILE = pl.BlockSpec((TAPS, 8, LANES), lambda i: (0, 0, i))


def conv_sums(source, taps, depth, counts, out, stats, rows, cols, masked=None):
    def emit(place, total, carry):
        flat = total.reshape(64, LANES)
        out[place, :] = flat
        kept = jnp.where(depth[place, :] > 0.0, flat, 0.0)
        if masked is not None:
            masked[place, :] = kept.astype(bf16)
        kept_cells = kept.reshape(8, 8, LANES)
        return (carry[0] + jnp.sum(kept_cells, axis=0), carry[1] + jnp.sum(kept_cells * total, axis=0))

    zero = jnp.zeros((8, LANES), f32)
    first, second = convolve(source, taps, rows, cols, emit, (zero, zero))
    stats[...] = counts[...]
    stats[0:1, :] = row_sum(first)
    stats[1:2, :] = row_sum(second)


def stem_kernel(rows, cols, fields, stem, taps, depth, counts, hzero, out, stats, source):
    width = cols + 2 * REACH

    def line(row, carry):
        place = rows8(row * width, width)
        source[place, :] = nt(fields[place, :], stem[...]).astype(bf16).astype(f32)
        return carry

    lax.fori_loop(0, rows + 2 * REACH, line, 0)
    for row in range(rows):
        hzero[rows8(row * cols, cols), :] = source[
            rows8((row + REACH) * width + REACH, cols), :
        ].astype(bf16)
    conv_sums(source, taps, depth, counts, out, stats, rows, cols)


def coarse_conv_kernel(rows, cols, border, taps, depth, counts, out, masked, stats, source):
    source[...] = border[...].astype(f32)
    conv_sums(source, taps, depth, counts, out, stats, rows, cols, masked)


def fine_kernel(cols, got, conv, hzero, vecs, up, up_bias, down, perm, downs, down_rows, hone, gated, slope, patches, coarse, held):
    mean, inverse, _, _ = norm_rows(got)
    scale = inverse * vecs[0:1]
    for part in range(2):
        place = pl.ds(part * cols * 8, cols * 8)
        normal = ((conv[place, :] - mean) * scale + vecs[1:2]).astype(bf16)
        act = nt(normal, up[...]) + up_bias[...]
        value, bend = gelu_pair(act)
        value = value.astype(bf16)
        gated[place, :] = value
        slope[place, :] = bend.astype(bf16)
        branch = nt(value, down[...]) + vecs[2:3]
        full = (hzero[place, :].astype(f32) + branch).astype(bf16)
        hone[place, :] = full
        held[place, :] = full.astype(f32)
    cells = held[...]
    mixed = jnp.zeros((cols * 4, H1), f32)
    for p in range(2):
        for q in range(2):
            mixed = mixed + nn(quarter(cells, 2, cols, p, q).astype(bf16), perm[p * 2 + q])
    mixed = mixed.astype(bf16)
    patches[...] = mixed
    coarse[...] = (nt(mixed, downs[...]) + down_rows[0:1]).astype(bf16)


def middle_kernel(
    cols, got, conv, cells, vecs, up, up_bias, down, ups, fine_rows, head, last_rows, tables, hone, targets, depth,
    skip_out, top_out, dy_out, ds_out, du_out, dtop_out, dv_out, gated_out, da_out, normal_out, dn_out, dx_out,
    sums, hidden_sums,
):
    mean, inverse, _, ocean_count = norm_rows(got)
    scale = inverse * vecs[0:1]
    centred = conv[...] - mean
    normal = (centred * scale + vecs[1:2]).astype(bf16)
    normal_out[...] = normal
    value, bend = gelu_pair(nt(normal, up[...]) + up_bias[...])
    value = value.astype(bf16)
    gated_out[...] = value
    top = (cells[...].astype(f32) + nt(value, down[...]) + vecs[2:3]).astype(bf16)
    top_out[...] = top
    raised = from_quarters([nt(top, ups[k]) + fine_rows[0:1] for k in range(4)], 2, cols)
    skip = (hone[...].astype(f32) + raised).astype(bf16)
    skip_out[...] = skip
    err = nt(skip, head[...]) + last_rows[0:1] - targets[...].astype(f32)
    deep = depth[...]
    ocean = tables[0:1] < deep
    heat_take = tables[1:2]
    err = jnp.where(ocean, err, 0.0)
    heat = jnp.sum(heat_take * err, axis=1, keepdims=True)
    heat = jnp.where(deep > 0.0, heat, 0.0)
    loss = row_sum(err * err) + (HEAT_WEIGHT / LANES) * row_sum(heat * heat)
    dy = jnp.where(ocean, err + HEAT_WEIGHT * heat_take * heat, 0.0) * (2.0 / ocean_count[:, :LANES])
    dy = dy.astype(bf16)
    dy_out[...] = dy
    ds = nn(dy, head[...])
    ds_out[...] = ds
    dtop = jnp.zeros(top.shape, f32)
    du_sum = jnp.zeros((1, C1), f32)
    for k in range(4):
        du = quarter(ds, 2, cols, k // 2, k % 2).astype(bf16)
        du_out[k] = du
        du_sum = du_sum + row_sum(du.astype(f32))
        dtop = dtop + nn(du, ups[k])
    dtop_out[...] = dtop
    dv = dtop.astype(bf16)
    dv_out[...] = dv
    da = (nn(dv, down[...]) * bend).astype(bf16)
    da_out[...] = da
    dn = nn(da, up[...])
    dn_out[...] = dn
    dx_out[...] = (dn * vecs[0:1]).astype(bf16)

    @pl.when(pl.program_id(0) == 0)
    def _():
        sums[...] = jnp.zeros(sums.shape, f32)
        hidden_sums[...] = jnp.zeros(hidden_sums.shape, f32)

    sums[0:1, :] += row_sum(dn)
    sums[1:2, :] += row_sum(dn * centred)
    sums[2:3, :] += row_sum(dv.astype(f32))
    sums[3:4, :C1] += du_sum
    sums[4:5, :CI] += row_sum(dy.astype(f32))
    sums[5:6, :LANES] += loss
    hidden_sums[0:1, :] += row_sum(da.astype(f32))


def coarse_weights_kernel(da, normal, dv, gated, du, top, dy, skip, up_out, down_out, ups_out, head_out):
    up_out[...] = tn(da[...], normal[...])
    down_out[...] = tn(dv[...], gated[...])
    for k in range(4):
        ups_out[k] = tn(du[k], top[...])
    head_out[...] = tn(dy[...], skip[...])


def backward_rows(got, back, gain):
    mean, inverse, cells, _ = norm_rows(got)
    total = jnp.sum(back[...], axis=0)
    total_a = gain * total[0:1]
    total_b = gain * total[1:2]
    dvar = -0.5 * inverse * inverse * inverse * total_b
    first = (-inverse * total_a - 2.0 * mean * dvar) / cells
    second = 2.0 * dvar / cells
    return inverse, first, second


def coarse_conv_back_kernel(
    rows, cols, got, back, vecs, border, dx, masked, mask, taps, dtop, dcells, taps_out, source, slope
):
    inverse, first, second = backward_rows(got, back, vecs[0:1])
    source[...] = border[...].astype(f32)
    slope[...] = (
        (
            dx[...].astype(f32) * inverse
            + jnp.where(mask[...] > 0.0, first, 0.0)
            + masked[...].astype(f32) * second
        )
        .astype(bf16)
        .astype(f32)
    )

    def emit(place, total, carry):
        dcells[place, :] = (dtop[place, :] + total.reshape(64, LANES)).astype(bf16)
        return carry

    convolve(slope, taps, rows, cols, emit, 0, flip=True)
    taps_out[...] = jnp.zeros(taps_out.shape, f32)
    width = cols + 2 * REACH
    for p in range(KSIZE):

        def line(turn, sums):
            row = turn // (cols // 8)
            col = (turn % (cols // 8)) * 8
            seen = source[rows8((row + p) * width + col, 8 + 2 * REACH), :]
            seen = seen.reshape(8 + 2 * REACH, 8, LANES)
            here = slope[rows8((row + REACH) * width + REACH + col, 8), :].reshape(8, 8, LANES)
            return tuple(sums[q] + jnp.sum(seen[q : q + 8] * here, axis=0) for q in range(KSIZE))

        zero = jnp.zeros((8, LANES), f32)
        sums = lax.fori_loop(0, rows * (cols // 8), line, (zero,) * KSIZE)
        for q in range(KSIZE):
            taps_out[p * KSIZE + q : p * KSIZE + q + 1, :] = row_sum(sums[q])


def fine_back_kernel(
    cols, got, dcells, downs, ds, vecs, conv, slope, up, down, dv_out, da_out, dn_out, normal_out, sums, hidden_sums, coarse_sums
):
    mean, inverse, _, _ = norm_rows(got)
    dlow = dcells[...]
    dh = ds[...] + from_quarters([nn(dlow, downs[k]) for k in range(4)], 2, cols)
    dv = dh.astype(bf16)
    dv_out[...] = dv

    @pl.when(pl.program_id(0) == 0)
    def _():
        sums[...] = jnp.zeros(sums.shape, f32)
        hidden_sums[...] = jnp.zeros(hidden_sums.shape, f32)
        coarse_sums[...] = jnp.zeros(coarse_sums.shape, f32)

    coarse_sums[0:1, :] += row_sum(dlow.astype(f32))
    sums[2:3, :] += row_sum(dv.astype(f32))
    for part in range(2):
        place = pl.ds(part * cols * 8, cols * 8)
        centred = conv[place, :] - mean
        normal_out[place, :] = (centred * (inverse * vecs[0:1]) + vecs[1:2]).astype(bf16)
        da = (nn(dv_out[place, :], down[...]) * slope[place, :].astype(f32)).astype(bf16)
        da_out[place, :] = da
        hidden_sums[0:1, :] += row_sum(da.astype(f32))
        dn = nn(da, up[...])
        dn_out[place, :] = dn
        sums[0:1, :] += row_sum(dn)
        sums[1:2, :] += row_sum(dn * centred)


def fine_weights_kernel(da, normal, dv, gated, dcells, patches, up_out, down_out, downs_out):
    up_out[...] = tn(da[...], normal[...])
    down_out[...] = tn(dv[...], gated[...])
    downs_out[...] = tn(dcells[...], patches[...])


def stem_back_kernel(
    rows, cols, got, back, vecs, dn, conv, depth, dv, first_cells, second_cells, third_cells, near, stem, pick,
    stem_out, taps_out, turned, acc, tap_acc, stem3,
):
    inverse, first, second = backward_rows(got, back, vecs[0:1])
    scale = inverse * vecs[0:1]
    amount = cols * 8

    def turn(row, carry):
        place = pl.ds(pl.multiple_of(row * amount, amount), amount)
        ocean = depth[place, :] > 0.0
        ocean = jnp.concatenate([ocean, ocean], axis=1)
        slope = dn[place, :] * scale + jnp.where(ocean, first + conv[place, :] * second, 0.0)
        turned[:, place] = slope.T.astype(bf16)
        return carry

    lax.fori_loop(0, rows, turn, 0)
    acc[...] = tn(dv[...], second_cells[pl.ds(REACH * amount, rows * amount), :])
    lane = lax.broadcasted_iota(jnp.int32, acc.shape, 1)
    acc[...] = jnp.where(lane < CIN, acc[...], 0.0)
    tap_acc[...] = jnp.zeros(tap_acc.shape, f32)
    wide = jnp.concatenate([stem[...].astype(f32), jnp.zeros((C1, C1 - CI), f32)], axis=1)
    stem3[...] = wide + pltpu.roll(wide, CIN, 1) + pltpu.roll(wide, 2 * CIN, 1)

    def group(index, cells, row):
        place = pl.ds(pl.multiple_of(row * amount, amount), rows * amount)
        part = nn(turned[...], cells[place, :])
        acc[...] += part * nt(near[...], pick[index])
        tap_acc[...] += nn((part * stem3[...]).astype(bf16), pick[index])

    def pair(p, carry):
        group(p, first_cells, p)
        group(p + KSIZE, second_cells, p)
        return carry

    lax.fori_loop(0, KSIZE, pair, 0)

    def triple(k, carry):
        group(k + 2 * KSIZE, third_cells, 3 * k)
        return carry

    lax.fori_loop(0, 3, triple, 0)
    full = acc[...]
    stem_out[...] = (
        full[:, :LANES]
        + pltpu.roll(full, C1 - CIN, 1)[:, :LANES]
        + pltpu.roll(full, C1 - 2 * CIN, 1)[:, :LANES]
    )
    taps_out[...] = tap_acc[...]


def period(length):
    return LANES // math.gcd(length, LANES)


def offsets():
    starts = []
    start = 0
    for shape in shapes_of():
        starts.append(start)
        start += math.prod(shape)
    return starts


def shard_places(devices, shard_len):
    firsts = [e * shard_len // 2048 * 16 for e in range(devices)]
    needed = [(e * shard_len % 2048 + shard_len + 2047) // 2048 * 16 for e in range(devices)]
    return firsts, max(needed)


def lane_ids(rows):
    return lax.broadcasted_iota(jnp.int32, (rows, LANES), 1)


def turn_lanes(values, amount):
    amount = amount % LANES
    return values if amount == 0 else pltpu.roll(values, amount, 1)


def read_rows(lines, base, rows, length, put):
    cycle = period(length)
    count = rows // cycle
    step = cycle * length // LANES
    lane = lane_ids(count)
    tiles = -(-length // LANES)
    for s in range(cycle):
        start = base + s * length
        line, phase = start // LANES, start % LANES
        held = [
            lines[pl.ds(line + k, count, stride=step), :] for k in range(-(-(phase + length) // LANES))
        ]
        for m in range(tiles):
            value = held[m]
            if phase and m + 1 < len(held):
                value = jnp.where(lane >= phase, value, held[m + 1])
            value = turn_lanes(value, -phase)
            if length - m * LANES < LANES:
                value = jnp.where(lane < length - m * LANES, value, 0.0)
            put(s, cycle, count, m, value)


def read_vector(lines, base, length, put):
    line, phase = base // LANES, base % LANES
    lane = lane_ids(1)
    for m in range(-(-length // LANES)):
        value = lines[line + m : line + m + 1, :]
        if phase and phase + length > (m + 1) * LANES:
            value = jnp.where(lane >= phase, value, lines[line + m + 1 : line + m + 2, :])
        value = turn_lanes(value, -phase)
        if length - m * LANES < LANES:
            value = jnp.where(lane < length - m * LANES, value, 0.0)
        put(m, value)


def write_rows(lines, base, rows, length, get):
    cycle = period(length)
    count = rows // cycle
    step = cycle * length // LANES
    line, phase = base // LANES, base % LANES
    for k in range(step):
        shared = k == 0 and phase > 0
        amount = count + 1 if shared else count
        lane = lane_ids(amount)
        total = None
        at = 0
        while at < LANES:
            place = k * LANES - phase + at
            row, col = place // length, place % length
            run = min(length - col, LANES - at)
            tile = col // LANES
            value = get(row, cycle, amount, tile)
            if col % LANES + run > LANES:
                value = jnp.where(lane >= col % LANES, value, get(row, cycle, amount, tile + 1))
            value = turn_lanes(value, at - col)
            total = value if total is None else jnp.where(lane >= at, value, total)
            at += run
        put_lines(lines, line + k, amount, step, total, shared)


def put_lines(lines, line, amount, step, values, shared):
    if not shared:
        lines[pl.ds(line, amount, stride=step), :] = values
        return
    before = lines[line : line + 1, :]
    lines[pl.ds(line, amount, stride=step), :] = values
    lines[line : line + 1, :] = lines[line : line + 1, :] + before


def write_vector(lines, base, length, get):
    line, phase = base // LANES, base % LANES
    lane = lane_ids(1)
    tiles = -(-length // LANES)
    zero = jnp.zeros((1, LANES), f32)
    for k in range(-(-(phase + length) // LANES)):
        value = get(k) if k < tiles else zero
        if phase:
            earlier = get(k - 1) if k > 0 else zero
            value = turn_lanes(jnp.where(lane >= LANES - phase, earlier, value), phase)
        if k == 0 and phase:
            value = value + lines[line : line + 1, :]
        lines[line + k : line + k + 1, :] = value


def write_short(lines, base, rows, length, get):
    line, phase = base // LANES, base % LANES
    lane = lane_ids(1)
    for k in range(-(-(phase + rows * length) // LANES)):
        low = k * LANES - phase
        total = jnp.zeros((1, LANES), f32)
        for row in range(max(low // length, 0), min(-(-(low + LANES) // length), rows)):
            at = row * length - low
            value = turn_lanes(get(row), at)
            if at < 0:
                value = jnp.where(lane < at + length, value, 0.0)
            elif at + length > LANES:
                value = jnp.where(lane >= at, value, 0.0)
            total = total + value
        if k == 0 and phase:
            total = total + lines[line : line + 1, :]
        lines[line + k : line + k + 1, :] = total


def read_short(lines, base, rows, length, put):
    lane = lane_ids(1)

    def one(row, carry):
        start = base + row * length
        line, phase = start // LANES, start % LANES
        value = jnp.where(lane >= phase, lines[pl.ds(line, 1), :], lines[pl.ds(line + 1, 1), :])
        value = pltpu.roll(value, LANES - phase, 1)
        put(row, jnp.where(lane < length, value, 0.0))
        return carry

    lax.fori_loop(0, rows, one, 0, unroll=8)


STEM, TAPS1, GAIN1, SHIFT1, UP1, UPB1, DOWN1, DOWNB1, DOWNS, DOWNSB = range(10)
TAPS2, GAIN2, SHIFT2, UP2, UPB2, DOWN2, DOWNB2, UPS, UPSB, HEAD, HEADB = range(10, 21)


def collect(devices, shard_len, me, blocks, lines, low, high):
    firsts, tall = shard_places(devices, shard_len)
    started = False
    for e in range(devices):
        end = firsts[e + 1] + 16 if e + 1 < devices else firsts[e] + tall
        if end <= low or firsts[e] >= high:
            continue
        seat = seat_of(me, e, devices)
        first = firsts[e] - low
        skip = max(0, -first)
        take = min(tall, high - firsts[e])
        if started:
            lines[pl.ds(first, 16), :] += blocks[seat, :16, :].astype(f32)
            skip = 16
        started = True
        if take > skip:
            lines[pl.ds(first + skip, take - skip), :] = blocks[seat, skip:take, :].astype(f32)


def seat_of(me, other, devices):
    away = me ^ other
    seat = 0
    bits = devices.bit_length() - 1
    for b in range(bits):
        seat = seat + ((away >> b) & 1) * (1 << (bits - 1 - b))
    return seat


def matrix_out(held, tall, out, tiles, rows):
    for m in range(tiles):
        if tall > rows:
            held[m * tall + rows : (m + 1) * tall, :] = jnp.zeros((tall - rows, LANES), f32)
        out[:, m * LANES : (m + 1) * LANES] = held[m * tall : (m + 1) * tall, :].astype(bf16)


def read_matrix(lines, shift, piece, held, out):
    rows, length = shapes_of()[piece]
    tall = out.shape[0]

    def put(first, stride, count, tile, value):
        held[pl.ds(tile * tall + first, count, stride=stride), :] = value

    read_rows(lines, offsets()[piece] - shift, rows, length, put)
    matrix_out(held, tall, out, -(-length // LANES), rows)


def read_row(lines, shift, piece, out, row):
    def put(tile, value):
        out[row : row + 1, tile * LANES : (tile + 1) * LANES] = value

    read_vector(lines, offsets()[piece] - shift, shapes_of()[piece][0], put)


def read_taps(lines, shift, piece, held, out, tall):
    def put(row, value):
        held[pl.ds(row, 1), :] = value

    rows = shapes_of()[piece][0]
    read_short(lines, offsets()[piece] - shift, rows, TAPS, put)
    held[rows:tall, :] = jnp.zeros((tall - rows, LANES), f32)
    across = held[:tall, :].T
    for t in range(TAPS):
        out[t] = jnp.broadcast_to(across[t : t + 1, :], (8, tall))


def first_end():
    return -(-offsets()[TAPS2] // 2048) * 16


def rest_start():
    return offsets()[TAPS2] // 2048 * 16


def rest_end():
    return -(-(offsets()[HEADB] + CIN) // 2048) * 16


def first_params_kernel(devices, shard_len, me, blocks, perm, stem, taps1, near1, vecs1, up1, bias1, down1, downs, downs_four, down_rows, lines, held):
    collect(devices, shard_len, me[0], blocks, lines, 0, first_end())
    vecs1[...] = jnp.zeros(vecs1.shape, f32)
    down_rows[...] = jnp.zeros(down_rows.shape, f32)
    bias1[...] = jnp.zeros(bias1.shape, f32)
    read_taps(lines, 0, TAPS1, held, taps1, C1)
    near1[...] = held[:C1, :].astype(bf16)
    read_matrix(lines, 0, STEM, held, stem)
    read_row(lines, 0, GAIN1, vecs1, 0)
    read_row(lines, 0, SHIFT1, vecs1, 1)
    read_row(lines, 0, DOWNB1, vecs1, 2)
    read_row(lines, 0, UPB1, bias1, 0)
    read_row(lines, 0, DOWNSB, down_rows, 0)
    read_matrix(lines, 0, UP1, held, up1)
    read_matrix(lines, 0, DOWN1, held, down1)
    read_matrix(lines, 0, DOWNS, held, downs)
    for k in range(4):
        downs_four[k] = nt(downs[...], perm[k]).astype(bf16)


def rest_params_kernel(devices, shard_len, me, blocks, taps2, vecs2, up2, bias2, down2, ups_four, vecs1, head, last, lines, held):
    shift = rest_start() * LANES
    collect(devices, shard_len, me[0], blocks, lines, rest_start(), rest_end())
    for out in (vecs1, vecs2, bias2, last):
        out[...] = jnp.zeros(out.shape, f32)
    read_taps(lines, shift, TAPS2, held, taps2, C2)
    read_row(lines, shift, GAIN2, vecs2, 0)
    read_row(lines, shift, SHIFT2, vecs2, 1)
    read_row(lines, shift, DOWNB2, vecs2, 2)
    read_row(lines, shift, UPB2, bias2, 0)
    read_row(lines, shift, UPSB, vecs1, 0)
    read_row(lines, shift, HEADB, last, 0)
    read_matrix(lines, shift, UP2, held, up2)
    read_matrix(lines, shift, DOWN2, held, down2)
    read_matrix(lines, shift, HEAD, held, head)
    tiles = C2 // LANES

    def put(first, stride, count, tile, value):
        k = first % 4
        held[pl.ds((k * tiles + tile) * C1 + first // 4, count, stride=stride // 4), :] = value

    rows, length = shapes_of()[UPS]
    read_rows(lines, offsets()[UPS] - shift, rows, length, put)
    for k in range(4):
        for m in range(tiles):
            at = (k * tiles + m) * C1
            held[at + WIDTH : at + C1, :] = jnp.zeros((C1 - WIDTH, LANES), f32)
            ups_four[k, :, m * LANES : (m + 1) * LANES] = held[at : at + C1, :].astype(bf16)


FRONT = 16


def hold_matrix(held, values, row_tiles, rows):
    tall = rows + 2 * FRONT
    zero = jnp.zeros((FRONT, LANES), f32)
    for m in range(row_tiles):
        at = m * tall
        held[at : at + FRONT, :] = zero
        held[at + FRONT : at + FRONT + rows, :] = values(m)
        held[at + FRONT + rows : at + tall, :] = zero


def write_matrix(lines, shift, piece, held, source):
    rows, length = shapes_of()[piece]
    tall = rows + 2 * FRONT
    hold_matrix(held, lambda m: source[:rows, m * LANES : (m + 1) * LANES], -(-length // LANES), rows)

    def get(first, stride, count, tile):
        return held[pl.ds(tile * tall + FRONT + first, count, stride=stride), :]

    write_rows(lines, offsets()[piece] - shift, rows, length, get)


def write_row(lines, shift, piece, get):
    write_vector(lines, offsets()[piece] - shift, shapes_of()[piece][0], get)


def row_of(source, row):
    return lambda m: source[row : row + 1, m * LANES : (m + 1) * LANES]


def norm_row(got, sums):
    def get(m):
        place = slice(m * LANES, (m + 1) * LANES)
        total = jnp.sum(got[:, :, place], axis=0)
        mean = total[0:1] / total[2:3]
        inverse = lax.rsqrt(total[1:2] / total[2:3] - mean * mean + NORM_EPS)
        return sums[1:2, place] * inverse

    return get


def flatten_kernel(
    devices, shard_len, me, got1, got2, g_stem, g_taps1, sums1, hidden1, g_up1, g_down1, g_downs, sums_low, g_taps2,
    sums2, hidden2, g_up2, g_down2, g_ups, g_head, keep, send, lines, held,
):
    def matrix(piece, source):
        write_matrix(lines, 0, piece, held, source)

    def row(piece, get):
        write_row(lines, 0, piece, get)

    matrix(STEM, g_stem)
    write_short(lines, offsets()[TAPS1], WIDTH, TAPS, lambda r: g_taps1[r : r + 1, :])
    row(GAIN1, norm_row(got1, sums1))
    row(SHIFT1, row_of(sums1, 0))
    matrix(UP1, g_up1)
    row(UPB1, row_of(hidden1, 0))
    matrix(DOWN1, g_down1)
    row(DOWNB1, row_of(sums1, 2))
    matrix(DOWNS, g_downs)
    row(DOWNSB, row_of(sums_low, 0))
    across = jnp.concatenate([g_taps2[...], jnp.zeros((LANES - g_taps2.shape[0], C2), f32)], axis=0).T
    held[:C2, :] = across
    write_short(lines, offsets()[TAPS2], WIDTH2, TAPS, lambda r: held[r : r + 1, :])
    row(GAIN2, norm_row(got2, sums2))
    row(SHIFT2, row_of(sums2, 0))
    matrix(UP2, g_up2)
    row(UPB2, row_of(hidden2, 0))
    matrix(DOWN2, g_down2)
    row(DOWNB2, row_of(sums2, 2))
    rows, length = shapes_of()[UPS]
    tiles = C2 // LANES
    tall = WIDTH + 2 * FRONT
    for k in range(4):
        for m in range(tiles):
            at = (k * tiles + m) * tall
            held[at : at + FRONT, :] = jnp.zeros((FRONT, LANES), f32)
            held[at + FRONT : at + FRONT + WIDTH, :] = g_ups[k, :WIDTH, m * LANES : (m + 1) * LANES]
            held[at + FRONT + WIDTH : at + tall, :] = jnp.zeros((FRONT, LANES), f32)

    def get(first, stride, count, tile):
        place = ((first % 4) * tiles + tile) * tall + FRONT + first // 4
        return held[pl.ds(place, count, stride=stride // 4), :]

    write_rows(lines, offsets()[UPS], rows, length, get)
    row(UPSB, row_of(sums2, 3))
    matrix(HEAD, g_head)
    row(HEADB, row_of(sums2, 4))
    end = offsets()[HEADB] + CIN
    last = -(-end // LANES)
    lines[last:, :] = jnp.zeros((lines.shape[0] - last, LANES), f32)

    firsts, tall = shard_places(devices, shard_len)
    half = devices // 2
    for e in range(devices):
        seat = seat_of(me[0], e, devices)

        @pl.when(seat < half)
        def _():
            keep[seat] = lines[firsts[e] : firsts[e] + tall, :]

        @pl.when(seat >= half)
        def _():
            send[seat - half] = lines[firsts[e] : firsts[e] + tall, :].astype(bf16)


def group_taps():
    table = []
    for first in (0, 3):
        for p in range(KSIZE):
            table.append([p * KSIZE + first + t for t in range(3)])
    for k in range(3):
        table.append([(3 * k + t) * KSIZE + 6 if 3 * k + t < KSIZE else -1 for t in range(3)])
    return table


def body(fields, targets, ocean_depth, thickness_class, params, moment1, moment2):
    shard_len = params.shape[0]
    devices = lax.axis_size(AXES)
    me = lax.axis_index(AXES)
    _, tall = shard_places(devices, shard_len)
    at = (me * (shard_len % 2048)) % 2048
    block = lax.dynamic_update_slice(jnp.zeros((tall * LANES,), bf16), params.astype(bf16), (at,))
    blocks = gather_blocks(block.reshape(tall, LANES))
    me_row = jnp.broadcast_to(me, (1,)).astype(jnp.int32)

    inputs = to_cells(lax.all_to_all(fields, "lvl", split_axis=3, concat_axis=0, tiled=True))
    goal = to_cells(lax.all_to_all(targets, "lvl", split_axis=3, concat_axis=0, tiled=True))
    rows, cols, _, _ = inputs.shape
    batch = fields.shape[1]
    half_rows, half_cols = rows // 2, cols // 2
    cells, low_cells = rows * cols * 8, half_rows * half_cols * 8
    wide = with_halo(inputs)
    wide_rows, wide_cols = rows + 2 * REACH, cols + 2 * REACH
    border_cells = wide_rows * wide_cols * 8
    low_border = (half_rows + 2 * REACH) * (half_cols + 2 * REACH) * 8
    fields_in = fill(wide, wide_rows, wide_cols, 8, CI).reshape(border_cells, CI)
    later = jnp.pad(wide, ((0, 2), (0, 0), (0, 0), (0, 0)))

    def three(parts):
        joined = jnp.concatenate(parts, axis=3)
        return fill(joined, wide_rows, cols, 8, C1).reshape(wide_rows * cols * 8, C1)

    first_cells = three([wide[:, k : k + cols] for k in range(3)])
    second_cells = three([wide[:, k : k + cols] for k in range(3, 6)])
    third_cells = three([later[k : k + wide_rows, 6 : 6 + cols] for k in range(3)])
    goal = fill(goal, rows, cols, 8, CI).reshape(cells, CI)

    deep = depth_cells(ocean_depth, batch)
    depth_rows = jnp.broadcast_to(deep.astype(f32)[..., None], deep.shape + (LANES,)).reshape(cells, LANES)
    low = jnp.max(deep.reshape(half_rows, 2, half_cols, 2, 8), axis=(1, 3))
    low_mask = (low > 0).astype(bf16)[..., None]
    low_wide = with_halo(jnp.broadcast_to(low_mask, low_mask.shape[:3] + (LANES,)))
    low_wide = low_wide.reshape(low_border, LANES)
    low_rows = jnp.broadcast_to(low.astype(f32)[..., None], low.shape + (LANES,)).reshape(low_cells, LANES)
    channel = jnp.arange(CI, dtype=jnp.int32)
    level = jnp.where(channel < 4 * LEVELS, channel // 4, 0)
    level_row = jnp.where(channel < CIN, level, LEVELS + 1).astype(f32)
    thickf = thickness_class.astype(f32)
    onehot = (level[:, None] == jnp.arange(LEVELS, dtype=jnp.int32)[None, :]).astype(f32)
    chosen = ((channel % 4 == 0) & (channel < 4 * LEVELS)).astype(f32)
    heat_take = chosen * jnp.sum(onehot * thickf[None, :], axis=1) / jnp.sum(thickf)
    ocean_cells = jnp.sum((level_row[None, None, :] < ocean_depth.astype(f32)[:, :, None]).astype(f32))
    ocean_cells = batch * ocean_cells
    surface_cells = jnp.sum((deep > 0).astype(f32))
    low_surface = jnp.sum((low > 0).astype(f32))
    index8 = jnp.arange(8)[:, None]
    counts1 = jnp.where(index8 == 2, surface_cells, jnp.where(index8 == 3, ocean_cells, 0.0))
    counts1 = jnp.broadcast_to(counts1, (8, C1))
    counts2 = jnp.where(index8 == 2, low_surface, jnp.where(index8 == 3, ocean_cells, 0.0))
    counts2 = jnp.broadcast_to(counts2, (8, C2))

    tables = jnp.pad(jnp.stack([level_row, heat_take]), ((0, 6), (0, 0)))
    source_lane = jnp.arange(C1, dtype=jnp.int32)[None, :, None]
    target_lane = jnp.arange(H1, dtype=jnp.int32)[None, None, :]
    quarter_at = jnp.arange(4, dtype=jnp.int32)[:, None, None]
    perm = ((source_lane * 4 + quarter_at == target_lane) & (source_lane < WIDTH)).astype(bf16)
    table = group_taps()
    third_at = jnp.arange(C1, dtype=jnp.int32) // CIN
    wanted = jnp.array([line + [-1] for line in table], dtype=jnp.int32)[:, third_at]
    pick = (wanted[:, :, None] == jnp.arange(LANES, dtype=jnp.int32)[None, None, :]).astype(bf16)
    smem = pl.BlockSpec(memory_space=pltpu.SMEM)
    vmem = pl.BlockSpec(memory_space=pltpu.VMEM)
    held_room = pltpu.VMEM((4 * H2, LANES), f32)
    stem_in, taps_in1, near1, vecs1, up_in1, bias_in1, down_in1, downs_in, downs_four, down_rows = call(
        lambda *refs: first_params_kernel(devices, shard_len, *refs),
        [
            ((C1, CI), bf16), ((TAPS, 8, C1), f32), ((C1, LANES), bf16), ((8, C1), f32), ((H1, C1), bf16),
            ((1, H1), f32), ((C1, H1), bf16), ((C2, H1), bf16), ((4, C2, C1), bf16), ((8, C2), f32),
        ],
        ins=[smem, vmem, vmem],
        scratch=[pltpu.VMEM((first_end(), LANES), f32), held_room],
        name="first_params",
    )(me_row, blocks, perm)
    taps_in2, vecs2, up_in2, bias_in2, down_in2, ups_four, fine_rows, head_in, last_rows = call(
        lambda *refs: rest_params_kernel(devices, shard_len, *refs),
        [
            ((TAPS, 8, C2), f32), ((8, C2), f32), ((H2, C2), bf16), ((1, H2), f32), ((C2, H2), bf16),
            ((4, C1, C2), bf16), ((8, C1), f32), ((CI, C1), bf16), ((8, CI), f32),
        ],
        ins=[smem, vmem],
        scratch=[pltpu.VMEM((rest_end() - rest_start(), LANES), f32), held_room],
        name="rest_params",
    )(me_row, blocks)

    hzero, conv1, stats1 = call(
        lambda *refs: stem_kernel(rows, cols, *refs),
        [((cells, C1), bf16), ((cells, C1), f32), ((8, C1), f32)],
        grid=(C1 // LANES,),
        ins=[
            whole(border_cells, CI),
            pl.BlockSpec((LANES, CI), lambda i: (i, 0)),
            TAP_TILE,
            whole(cells, LANES),
            lane_tile(8),
        ],
        out_specs=[lane_tile(cells), lane_tile(cells), lane_tile(8)],
        scratch=[pltpu.VMEM((border_cells, LANES), f32)],
        flops=cells * C1 * TAPS * 100,
        name="stem_conv",
    )(fields_in, stem_in, taps_in1, depth_rows, counts1)
    got1 = spread(stats1)
    chunk, low_chunk = 2 * cols * 8, half_cols * 8
    hone, gated1, slope1, patches, coarse = call(
        lambda *refs: fine_kernel(cols, *refs),
        [
            ((cells, C1), bf16),
            ((cells, H1), bf16),
            ((cells, H1), bf16),
            ((low_cells, H1), bf16),
            ((low_cells, C2), bf16),
        ],
        grid=(half_rows,),
        ins=[
            whole(devices, 8, C1), band(chunk, C1), band(chunk, C1), whole(8, C1), whole(H1, C1), whole(1, H1),
            whole(C1, H1), whole(4, C1, H1), whole(C2, H1), whole(8, C2),
        ],
        out_specs=[
            band(chunk, C1), band(chunk, H1), band(chunk, H1), band(low_chunk, H1), band(low_chunk, C2),
        ],
        scratch=[pltpu.VMEM((chunk, C1), f32)],
        flops=cells * C1 * H1 * 8,
        name="fine_forward",
    )(got1, conv1, hzero, vecs1, up_in1, bias_in1, down_in1, perm, downs_in, down_rows)

    border2 = with_halo(coarse.reshape(half_rows, half_cols, 8, C2)).reshape(low_border, C2)
    conv2, masked2, stats2 = call(
        lambda *refs: coarse_conv_kernel(half_rows, half_cols, *refs),
        [((low_cells, C2), f32), ((low_cells, C2), bf16), ((8, C2), f32)],
        grid=(C2 // LANES,),
        ins=[lane_tile(low_border), TAP_TILE, whole(low_cells, LANES), lane_tile(8)],
        out_specs=[lane_tile(low_cells), lane_tile(low_cells), lane_tile(8)],
        scratch=[pltpu.VMEM((low_border, LANES), f32)],
        flops=low_cells * C2 * TAPS * 100,
        name="coarse_conv",
    )(border2, taps_in2, low_rows, counts2)
    got2 = spread(stats2)
    masked_wide = with_halo(masked2.reshape(half_rows, half_cols, 8, C2)).reshape(low_border, C2)
    (
        skip, top, dy, ds, du, dtop, dv2, gated2, da2, normal2, dn2, dx2, sums2, hidden2,
    ) = call(
        lambda *refs: middle_kernel(cols, *refs),
        [
            ((cells, C1), bf16), ((low_cells, C2), bf16), ((cells, CI), bf16), ((cells, C1), f32),
            ((4, low_cells, C1), bf16), ((low_cells, C2), f32), ((low_cells, C2), bf16), ((low_cells, H2), bf16),
            ((low_cells, H2), bf16), ((low_cells, C2), bf16), ((low_cells, C2), f32), ((low_cells, C2), bf16),
            ((8, C2), f32), ((8, H2), f32),
        ],
        grid=(half_rows,),
        ins=[
            whole(devices, 8, C2), band(low_chunk, C2), band(low_chunk, C2), whole(8, C2), whole(H2, C2), whole(1, H2),
            whole(C2, H2), whole(4, C1, C2), whole(8, C1), whole(CI, C1), whole(8, CI), whole(8, CI), band(chunk, C1),
            band(chunk, CI), band(chunk, LANES),
        ],
        out_specs=[
            band(chunk, C1), band(low_chunk, C2), band(chunk, CI), band(chunk, C1),
            pl.BlockSpec((4, low_chunk, C1), lambda i: (0, i, 0)), band(low_chunk, C2), band(low_chunk, C2),
            band(low_chunk, H2), band(low_chunk, H2), band(low_chunk, C2), band(low_chunk, C2), band(low_chunk, C2),
            whole(8, C2), whole(8, H2),
        ],
        flops=low_cells * C2 * H2 * 16,
        name="middle",
    )(
        got2, conv2, coarse, vecs2, up_in2, bias_in2, down_in2, ups_four, fine_rows, head_in, last_rows, tables, hone, goal,
        depth_rows,
    )
    back2 = spread(sums2)
    dx_wide = with_halo(dx2.reshape(half_rows, half_cols, 8, C2)).reshape(low_border, C2)
    g_up2, g_down2, g_ups, g_head = call(
        coarse_weights_kernel,
        [((H2, C2), f32), ((C2, H2), f32), ((4, C1, C2), f32), ((CI, C1), f32)],
        flops=low_cells * C2 * H2 * 8,
        name="coarse_weights",
    )(da2, normal2, dv2, gated2, du, top, dy, skip)
    dcells, g_taps2 = call(
        lambda *refs: coarse_conv_back_kernel(half_rows, half_cols, *refs),
        [((low_cells, C2), bf16), ((56, C2), f32)],
        grid=(C2 // LANES,),
        ins=[
            pl.BlockSpec((devices, 8, LANES), lambda i: (0, 0, i)),
            pl.BlockSpec((devices, 8, LANES), lambda i: (0, 0, i)),
            lane_tile(8), lane_tile(low_border), lane_tile(low_border), lane_tile(low_border),
            whole(low_border, LANES), TAP_TILE, lane_tile(low_cells),
        ],
        out_specs=[lane_tile(low_cells), lane_tile(56)],
        scratch=[pltpu.VMEM((low_border, LANES), f32), pltpu.VMEM((low_border, LANES), f32)],
        flops=low_cells * C2 * TAPS * 200,
        name="coarse_conv_back",
    )(got2, back2, vecs2, border2, dx_wide, masked_wide, low_wide, taps_in2, dtop)

    dv1, da1, dn1, normal1, sums1, hidden1, sums_low = call(
        lambda *refs: fine_back_kernel(cols, *refs),
        [
            ((cells, C1), bf16), ((cells, H1), bf16), ((cells, C1), f32), ((cells, C1), bf16),
            ((8, C1), f32), ((8, H1), f32), ((8, C2), f32),
        ],
        grid=(half_rows,),
        ins=[
            whole(devices, 8, C1), band(low_chunk, C2), whole(4, C2, C1), band(chunk, C1), whole(8, C1),
            band(chunk, C1), band(chunk, H1), whole(H1, C1), whole(C1, H1),
        ],
        out_specs=[
            band(chunk, C1), band(chunk, H1), band(chunk, C1), band(chunk, C1), whole(8, C1), whole(8, H1), whole(8, C2),
        ],
        flops=cells * C1 * H1 * 8,
        name="fine_backward",
    )(got1, dcells, downs_four, ds, vecs1, conv1, slope1, up_in1, down_in1)
    back1 = spread(sums1)
    g_up1, g_down1, g_downs = call(
        fine_weights_kernel,
        [((H1, C1), f32), ((C1, H1), f32), ((C2, H1), f32)],
        flops=cells * C1 * H1 * 6,
        name="fine_weights",
    )(da1, normal1, dv1, gated1, dcells, patches)
    g_stem, g_taps1 = call(
        lambda *refs: stem_back_kernel(rows, cols, *refs),
        [((C1, LANES), f32), ((C1, LANES), f32)],
        scratch=[pltpu.VMEM((C1, cells), bf16), pltpu.VMEM((C1, C1), f32), pltpu.VMEM((C1, LANES), f32), pltpu.VMEM((C1, C1), f32)],
        flops=cells * C1 * C1 * GROUPS * 2,
        name="stem_back",
    )(
        got1, back1, vecs1, dn1, conv1, depth_rows, dv1, first_cells, second_cells, third_cells, near1, stem_in,
        pick,
    )

    keep, send = call(
        lambda *refs: flatten_kernel(devices, shard_len, *refs),
        [((devices // 2, tall, LANES), f32), ((devices // 2, tall, LANES), bf16)],
        ins=[smem] + [vmem] * 17,
        scratch=[pltpu.VMEM((rest_end() + tall, LANES), f32), held_room],
        name="flatten",
    )(
        me_row, got1, got2, g_stem, g_taps1, sums1, hidden1, g_up1, g_down1, g_downs, sums_low, g_taps2, sums2, hidden2,
        g_up2, g_down2, g_ups, g_head,
    )
    mine = scatter_blocks(keep, send).reshape(-1)
    mine = lax.dynamic_slice_in_dim(mine, at, shard_len)
    loss_part = jnp.sum(sums2[5, :LANES])
    last = jnp.broadcast_to(
        jnp.where(index8 == 0, loss_part, jnp.where(index8 == 1, jnp.sum(mine * mine), 0.0)), (8, LANES)
    )
    last = jnp.sum(spread(last), axis=0)
    loss_total, norm = last[0, 0], jnp.sqrt(last[1, 0])
    count = jnp.sum(got1[:, 3, 0])
    clipped = mine * jnp.minimum(1.0, CLIP / norm)
    first = BETA_ONE * moment1 + (1.0 - BETA_ONE) * clipped
    second = BETA_TWO * moment2 + (1.0 - BETA_TWO) * clipped * clipped
    ratio = first / (1.0 - BETA_ONE**STEP) / (jnp.sqrt(second / (1.0 - BETA_TWO**STEP)) + ADAM_EPS)
    updated = params - LRATE * (ratio + DECAY * params)
    return (loss_total, count, norm, updated, first, second)


def solution(mesh):
    in_specs = (
        P("lvl", None, "lat", None),
        P("lvl", None, "lat", None),
        P("lat", "lvl"),
        P(),
        P(("lat", "lvl")),
        P(("lat", "lvl")),
        P(("lat", "lvl")),
    )
    out_specs = (P(), P(), P(), P(("lat", "lvl")), P(("lat", "lvl")), P(("lat", "lvl")))
    return jax.shard_map(body, mesh=mesh, in_specs=in_specs, out_specs=out_specs, check_vma=False)
```

time: 1230 us -> 594 us (0.48)
  local copies, waits for them, and re-layouts: 374 us -> 104 us
  blocking collectives: 210 us -> 0 us
  Pallas kernels: 0 us -> 192 us
  waiting for transfers between devices: 301 us -> 138 us
  other arithmetic: 189 us -> 51.2 us
  matrix products: 72.2 us -> 0 us
  starting transfers between devices: 40.2 us -> 96.3 us
  between operations: 24.4 us -> 4.37 us
    psum x5 -> x0, blocking collectives: 210 us -> none  [the longest x2 86.2 us: block_forward(): lax.psum((jnp.sum(depthwise_conv_output * surface_field, axis=(1, 2, 3)),...]
    pallas_call x0 -> x12, Pallas kernels: none -> 192 us  [the longest x1 26.3 us: body(): call(lambda *refs: stem_back_kernel(rows, cols, *refs), [((C1, LANES), f3...]
    psum x1 -> x0, waiting for transfers between devices: 189 us -> none  [body(): summed = lax.psum(joined, ('lat', 'lvl'))]
    reduce_sum x22 -> x8, other arithmetic: 129 us -> 5.64 us  [the longest x1 1.55 us: body(): count = jnp.sum(got1[:, 3, 0])]
    ppermute x16 -> x30, waiting for transfers between devices: 9.95 us -> 121 us  [the longest x10 97.6 us: exchange(): return lax.ppermute(values, axis, [(i, i ^ step) for i in range(count)])]
    reshape x31 -> x2, local copies, waits for them, and re-layouts: 117 us -> 7.13 us  [the longest x1 5.51 us: with_halo(): jnp.concatenate([top, cells, bottom], axis=0)]
    unnamed x3 -> x0, waiting for transfers between devices: 101 us -> none
    dot_general x23 -> x0, matrix products: 72.2 us -> none  [the longest x7 27.8 us: contract_rows(): lax.dot_general(left, right, (((0,), (0,)), ((), ())), preferred_element_...]
  transfers between devices with their start and end apart: 20 -> 37, of which waited for: 8 -> 21; matrix products, arithmetic and copies ran while one was open for 9% -> 20% of each run, Pallas kernels for 0% -> 9%
where the time goes in v2:
time: 594 us; the launch traced here: 585 us
  Pallas kernels  192 us (32%)
  waiting for transfers between devices  138 us (23%)
  local copies, waits for them, and re-layouts  104 us (18%)
  starting transfers between devices  96.3 us (16%)
  other arithmetic  51.2 us (9%)
    ppermute x10, waiting for transfers between devices, exchange(): return lax.ppermute(values, axis, [(i, i ^ step) for i in range(count)])  97.6 us
    unnamed x66, local copies, waits for them, and re-layouts  29.2 us
    all_to_all x5, starting transfers between devices, spread(): return lax.all_to_all(copies, AXES, 0, 0, tiled=True)  26.5 us
    pallas_call x1, Pallas kernels, body(): call(lambda *refs: stem_back_kernel(rows, cols, *refs), [((C1, LANES), f3...  26.3 us
    pallas_call x1, Pallas kernels, body(): call(lambda *refs: stem_kernel(rows, cols, *refs), [((cells, C1), bf16),...  25.4 us
    pallas_call x1, Pallas kernels, body(): call(lambda *refs: coarse_conv_back_kernel(half_rows, half_cols, *refs),...  24.3 us
    pallas_call x1, Pallas kernels, body(): call(lambda *refs: middle_kernel(cols, *refs), [((cells, C1), bf16), ((lo...  20.2 us
    ppermute x5, starting transfers between devices, with_halo(): above = lax.ppermute(cells[rows - REACH:, :, :, bands - 1], 'lat', onward)  19.5 us
  transfers between devices with their start and end apart: 37, of which 21 were waited for; matrix products, arithmetic and copies ran while one was open for 20% of the time, Pallas kernels for 9%

profile of v2, /device:TPU:0, one launch (start us, length us, event | category | flops | bytes accessed | tf_op | source)
XLA Modules:
  0.0 585.1 jit_solution(1021823948690160966)
XLA Ops:
  3.1 4.1 collective-permute-start.4
  9.5 2.8 reshape.365
  12.3 3.6 all-to-all-start
  16.4 2.4 collective-permute-start.21
  22.5 7.0 %collective-permute-done.5 = bf16[2,592,128]{2,1,0:T(8,128)(2,1)S(1)} collective-permute-done((bf16[2,592,128]{2,1,0:T(8,128)(2,1)S(1)}, bf16[2,592,128]{2,1,0:T(8,128)(2,1)S(1)}, u32[]{:S(2)}, u32[]{:S(2)}) %collective-permute-start.5) | collective-permute-done | bytes 303136 | tf_op jit(solution)/shard_map/ppermute | solution.py:58
  34.3 11.8 %collective-permute-done.6 = bf16[4,592,128]{2,1,0:T(8,128)(2,1)S(1)} collective-permute-done((bf16[4,592,128]{2,1,0:T(8,128)(2,1)S(1)}, bf16[4,592,128]{2,1,0:T(8,128)(2,1)S(1)}, u32[]{:S(2)}, u32[]{:S(2)}) %collective-permute-start.6) | collective-permute-done | bytes 606240 | tf_op jit(solution)/shard_map/ppermute | solution.py:58
  51.8 23.1 %collective-permute-done.7 = bf16[8,592,128]{2,1,0:T(8,128)(2,1)S(1)} collective-permute-done((bf16[8,592,128]{2,1,0:T(8,128)(2,1)S(1)}, bf16[8,592,128]{2,1,0:T(8,128)(2,1)S(1)}, u32[]{:S(2)}, u32[]{:S(2)}) %collective-permute-start.7) | collective-permute-done | bytes 1212448 | tf_op jit(solution)/shard_map/ppermute | solution.py:58
  82.2 2.3 copy.323
  84.5 2.8 reshape.367
  87.7 3.4 collective-permute-start.23
  93.5 3.6 collective-permute-done.24
  97.8 3.5 all-to-all-start.3
  101.3 3.2 reshape.366
  104.5 3.7 copy.303
  110.3 3.0 collective-permute-start
  116.1 3.2 reshape.368
  119.3 3.6 copy.324
  125.6 3.1 copy.307
  128.6 4.0 copy.308
  135.9 5.4 collective-permute-start.2
  143.0 4.8 collective-permute-done.2
  147.8 5.1 maximum_maximum_fusion
  153.0 5.5 copy.312
  160.0 3.2 constant_dynamic-update-slice_fusion.5.refs_1_
  163.2 9.6 %first_params.1 = (bf16[256,128]{1,0:T(8,128)(2,1)}, f32[49,8,256]{2,1,0:T(8,128)}, bf16[256,128]{1,0:T(8,128)(2,1)}, f32[8,256]{1,0:T(8,128)}, bf16[896,256]{1,...) custom-call(s32[1]{0:T(128)} %bitcast.13.refs_0_, ...), custom_call_target="tpu_custom_call" | custom-call | bytes 1000000 | tf_op jit(solution)/shard_map/first_params/pallas_call | solution.py:977
  175.1 25.4 %stem_conv.1 = (bf16[3072,256]{1,0:T(8,128)(2,1)}, f32[3072,256]{1,0:T(8,128)}, f32[8,256]{1,0:T(8,128)}) custom-call(bf16[6048,128]{1,0:T(8,128)(2,1)} %bitcast.116, bf16[256,128]{1,0:T(8,128)(2,1)} %get-tuple-element.69.refs_1_.refs_11_, f32[49,8,256]{2,1,0:T(8,128)} %get-tuple-element.70.refs_2_, f32[3072,128]{1,0:T(8,128)} %broadcast_in_dim.139.refs_3_.refs_14_.refs_5_, ...), custom_call_target="tpu_custom_call" | custom-call | flops 3853516800 | bytes 1000000 | tf_op jit(solution)/shard_map/stem_conv/pallas_call | solution.py:998
  201.9 4.3 all-to-all-start.1
  206.3 5.7 fusion.26
  211.9 4.9 all-to-all-done.1.refs_0_.refs_1_
  217.6 15.3 %fine_forward.1 = (bf16[3072,256]{1,0:T(8,128)(2,1)}, bf16[3072,896]{1,0:T(8,128)(2,1)}, bf16[3072,896]{1,0:T(8,128)(2,1)}, bf16[768,896]{1,0:T(8,128)(2,1)}, bf16[768,512]{1,0:T(8,128)(2,1)}) custom-call(f32[32,8,256]{2,1,0:T(8,128)} %copy-done.10, f32[3072,256]{1,0:T(8,128)} %get-tuple-element.72.refs_1_.refs_5_.refs_4_, ...), custom_call_target="tpu_custom_call" | custom-call | flops 5637144576 | bytes 1000000 | tf_op jit(solution)/shard_map/fine_forward/pallas_call | solution.py:1016
  235.7 7.3 %fusion.12 = (bf16[14,48,8,256]{3,2,1,0:T(8,128)(2,1)}, bf16[14,48,8,256]{3,2,1,0:T(8,128)(2,1)}) fusion(bf16[14,48,8,80]{3,2,1,0:T(8,128)(2,1)} %get-tuple-element.145, bf16[14,48,8,80]{3,2,1,0:T(8,128)(2,1)} %get-tuple-element.146, bf16[14,48,8,80]{3,2,1,0:T(8,128)(2,1)} %get-tuple-element.147, bf16[14,48,8,80]{3,2,1,0:T(8,128)(2,1)S(1)} %get-tuple-element.142, ...), kind=kLoop, calls=%fused_computation.16 | loop fusion | flops 26148864 | bytes 10665984 | tf_op jit(solution)/shard_map/concatenate | solution.py:933
  243.0 12.8 %rest_params.1 = (f32[49,8,512]{2,1,0:T(8,128)}, f32[8,512]{1,0:T(8,128)}, bf16[1664,512]{1,0:T(8,128)(2,1)}, f32[1,1664]{1,0:T(1,128)}, bf16[512,1664]{1,0:T(8,...) custom-call(s32[1]{0:T(128)} %bitcast.13.refs_0_, ...), custom_call_target="tpu_custom_call" | custom-call | bytes 1000000 | tf_op jit(solution)/shard_map/rest_params/pallas_call | solution.py:987
  259.6 3.4 collective-permute-start.11
  266.0 4.4 collective-permute-done.12
  270.4 3.7 maximum_maximum_fusion.1
  276.1 2.3 reshape_reshape.12.refs_0_.refs_3_
  280.0 10.5 %coarse_conv.1 = (f32[768,512]{1,0:T(8,128)}, bf16[768,512]{1,0:T(8,128)(2,1)}, f32[8,512]{1,0:T(8,128)}) custom-call(bf16[2400,512]{1,0:T(8,128)(2,1)} %reshape_reshape.12.refs_0_.refs_3_, f32[49,8,512]{2,1,0:T(8,128)} %get-tuple-element.81.refs_1_.refs_7_, f32[768,128]{1,0:T(8,128)} %broadcast_in_dim.148.refs_2_, f32[8,512]{1,0:T(8,128)} %broadcast_in_dim.150.refs_3_), custom_call_target="tpu_custom_call" | custom-call | flops 1926758400 | bytes 1000000 | tf_op jit(solution)/shard_map/coarse_conv/pallas_call | solution.py:1039
  292.8 4.5 collective-permute-start.17
  297.3 3.2 fusion.16
  303.8 3.8 all-to-all-start.2
  311.9 3.7 collective-permute-start.19
  317.6 5.6 all-to-all-done.2.refs_0_.refs_2_
  324.0 20.2 %middle.1 = (bf16[3072,256]{1,0:T(8,128)(2,1)}, bf16[768,512]{1,0:T(8,128)(2,1)}, bf16[3072,128]{1,0:T(8,128)(2,1)}, f32[3072,256]{1,0:T(8,128)}, bf16[4,768,256...) custom-call(f32[32,8,512]{2,1,0:T(8,128)} %copy-done.6, ...), custom_call_target="tpu_custom_call" | custom-call | flops 10468982784 | bytes 1000000 | tf_op jit(solution)/shard_map/middle/pallas_call | solution.py:1053
  345.8 2.8 collective-permute-start.13
  348.7 3.8 maximum_maximum_fusion.3
  359.0 5.8 all-to-all-start.4
  367.1 3.7 collective-permute-start.15
  372.7 5.7 collective-permute-done.15
  380.6 3.7 maximum_maximum_fusion.2
  389.3 24.3 %coarse_conv_back.1 = (bf16[768,512]{1,0:T(8,128)(2,1)}, f32[56,512]{1,0:T(8,128)}) custom-call(f32[32,8,512]{2,1,0:T(8,128)} %copy-done.6, f32[32,8,512]{2,1,0:T(8,128)} %copy-done.11, f32[8,512]{1,0:T(8,128)} %get-tuple-element.84.refs_3_.refs_2_, bf16[2400,512]{1,0:T(8,128)(2,1)} %reshape_reshape.12.refs_0_.refs_3_, ...), custom_call_target="tpu_custom_call" | custom-call | flops 3853516800 | bytes 1000000 | tf_op jit(solution)/shard_map/coarse_conv_back/pallas_call | solution.py:1087
  413.6 12.6 %fine_backward.1 = (bf16[3072,256]{1,0:T(8,128)(2,1)}, bf16[3072,896]{1,0:T(8,128)(2,1)}, f32[3072,256]{1,0:T(8,128)}, bf16[3072,256]{1,0:T(8,128)(2,1)}, f32[8,...) custom-call(f32[32,8,256]{2,1,0:T(8,128)} %copy-done.10, bf16[768,512]{1,0:T(8,128)(2,1)} %get-tuple-element.97.refs_1_.dcells, ...), custom_call_target="tpu_custom_call" | custom-call | flops 5637144576 | bytes 1000000 | tf_op jit(solution)/shard_map/fine_backward/pallas_call | solution.py:1103
  427.6 7.3 %all-to-all-start.5 = ((f32[32,8,256]{2,1,0:T(8,128)}), f32[32,8,256]{2,1,0:T(8,128)S(1)}, u32[]{:S(2)}, u32[]{:S(2)}) async-start(f32[32,8,256]{2,1,0:T(8,128)} %broadcast_in_dim.164), calls=%async_computation.5 | async-start | bytes 524288 | tf_op jit(solution)/shard_map/all_to_all | solution.py:80
  434.9 9.9 %coarse_weights.1 = (f32[1664,512]{1,0:T(8,128)}, f32[512,1664]{1,0:T(8,128)}, f32[4,256,512]{2,1,0:T(8,128)}, f32[128,256]{1,0:T(8,128)}) custom-call(bf16[768,1664]{1,0:T(8,128)(2,1)} %get-tuple-element.118.da, bf16[768,512]{1,0:T(8,128)(2,1)} %get-tuple-element.119.normal, bf16[768,512]{1,0:T(8,128)(2,1)} %get-tuple-element.120.dv, ...), custom_call_target="tpu_custom_call" | custom-call | flops 5234491392 | bytes 1000000 | tf_op jit(solution)/shard_map/coarse_weights/pallas_call | solution.py:1081
  444.8 11.2 %fine_weights.1 = (f32[896,256]{1,0:T(8,128)}, f32[256,896]{1,0:T(8,128)}, f32[512,896]{1,0:T(8,128)}) custom-call(bf16[3072,896]{1,0:T(8,128)(2,1)} %get-tuple-element.108.da, bf16[3072,256]{1,0:T(8,128)(2,1)} %get-tuple-element.109.normal, bf16[3072,256]{1,0:T(8,128)(2,1)} %get-tuple-element.103.refs_6_.dv, bf16[3072,896]{1,0:T(8,128)(2,1)} %get-tuple-element.110.gated, ...), custom_call_target="tpu_custom_call" | custom-call | flops 4227858432 | bytes 1000000 | tf_op jit(solution)/shard_map/fine_weights/pallas_call | solution.py:1121
  456.7 26.3 %stem_back.1 = (f32[256,128]{1,0:T(8,128)}, f32[256,128]{1,0:T(8,128)}) custom-call(f32[32,8,256]{2,1,0:T(8,128)} %copy-done.10, f32[32,8,256]{2,1,0:T(8,128)} %copy-done.18, f32[8,256]{1,0:T(8,128)} %get-tuple-element.74.refs_3_.refs_4_.refs_2_, f32[3072,256]{1,0:T(8,128)} %get-tuple-element.102.refs_3_, ...), custom_call_target="tpu_custom_call" | custom-call | flops 6845104128 | bytes 1000000 | tf_op jit(solution)/shard_map/stem_back/pallas_call | solution.py:1127
  483.0 13.6 %flatten.1 = (f32[16,592,128]{2,1,0:T(8,128)}, bf16[16,592,128]{2,1,0:T(8,128)(2,1)}) custom-call(s32[1]{0:T(128)} %bitcast.13.refs_0_, f32[32,8,256]{2,1,0:T(8,128)} %copy-done.10, f32[32,8,512]{2,1,0:T(8,128)} %copy-done.6, f32[256,128]{1,0:T(8,128)} %get-tuple-element.105.refs_3_, f32[256,128]{1,0:T(8,128)} %get-tuple-element.106.refs_4_, ...), custom_call_target="tpu_custom_call" | custom-call | bytes 1000000 | tf_op jit(solution)/shard_map/flatten/pallas_call | solution.py:1138
  497.0 4.5 collective-permute-done.25
  501.5 2.9 convert_add_fusion
  506.5 27.1 %collective-permute-done.26 = bf16[8,592,128]{2,1,0:T(8,128)(2,1)S(1)} collective-permute-done((bf16[8,592,128]{2,1,0:T(8,128)(2,1)S(1)}, bf16[8,592,128]{2,1,0:T(8,128)(2,1)S(1)}, u32[]{:S(2)}, u32[]{:S(2)}) %collective-permute-start.26) | collective-permute-done | bytes 1212448 | tf_op jit(solution)/shard_map/ppermute | solution.py:58
  535.6 13.5 %collective-permute-done.27 = bf16[4,592,128]{2,1,0:T(8,128)(2,1)S(1)} collective-permute-done((bf16[4,592,128]{2,1,0:T(8,128)(2,1)S(1)}, bf16[4,592,128]{2,1,0:T(8,128)(2,1)S(1)}, u32[]{:S(2)}, u32[]{:S(2)}) %collective-permute-start.27) | collective-permute-done | bytes 606240 | tf_op jit(solution)/shard_map/ppermute | solution.py:58
  550.8 6.3 %collective-permute-done.28 = bf16[2,592,128]{2,1,0:T(8,128)(2,1)S(1)} collective-permute-done((bf16[2,592,128]{2,1,0:T(8,128)(2,1)S(1)}, bf16[2,592,128]{2,1,0:T(8,128)(2,1)S(1)}, u32[]{:S(2)}, u32[]{:S(2)}) %collective-permute-start.28) | collective-permute-done | bytes 303136 | tf_op jit(solution)/shard_map/ppermute | solution.py:58
  560.6 4.3 collective-permute-done.29
  567.7 5.2 all-to-all-start.6
  574.5 6.7 %all-to-all-done.6 = f32[32,8,128]{2,1,0:T(8,128)S(1)} async-done(((f32[32,8,128]{2,1,0:T(8,128)}), f32[32,8,128]{2,1,0:T(8,128)S(1)}, u32[]{:S(2)}, u32[]{:S(2)}) %all-to-all-start.6) | async-done | bytes 131104 | tf_op jit(solution)/shard_map/all_to_all | solution.py:80
  (204 shorter events, 110.9 us)
Async XLA Ops:
  3.1 17.7 %collective-permute-start.4 = (bf16[1,592,128]{2,1,0:T(8,128)(2,1)S(1)}, bf16[1,592,128]{2,1,0:T(8,128)(2,1)S(1)}, u32[]{:S(2)}, u32[]{:S(2)}) collective-permute-start(bf16[1,592,128]{2,1,0:T(8,128)(2,1)S(1)} %bitcast.109), channel_id=1, source_target_pairs={{0,16},{4,20},{8,24},{12,28},{16,0},{20,4},{24,8},{28,12},{1,17},{... | collective-permute-start | bytes 454664 | tf_op jit(solution)/shard_map/ppermute | solution.py:58
  9.5 6.4 %copy-start.17 = (s32[32,48]{1,0:T(8,128)S(1)}, s32[32,48]{1,0:T(8,128)}, u32[]{:S(2)}) copy-start(s32[32,48]{1,0:T(8,128)} %param.10) | copy-start | bytes 18436
  9.5 10.7 %copy-start.20 = (s32[19]{0:T(128)S(1)}, s32[19]{0:T(128)}, u32[]{:S(2)}) copy-start(s32[19]{0:T(128)} %param.11) | copy-start | bytes 232
  12.3 19.0 %copy-start.1 = (s32[17,4]{0,1:T(4,128)S(1)}, s32[17,4]{0,1:T(4,128)}, u32[]{:S(2)}) copy-start(s32[17,4]{0,1:T(4,128)} %constant.122.clone) | copy-start | bytes 820
  12.3 85.6 %all-to-all-start = ((bf16[4,2,30720]{2,1,0:T(2,128)(2,1)}), bf16[4,2,30720]{2,1,0:T(2,128)(2,1)S(1)}, u32[]{:S(2)}, u32[]{:S(2)}) async-start(bf16[4,2,30720]{2,1,0:T(2,128)(2,1)} %reshape.365), calls=%async_computation | async-start | bytes 983040 | tf_op jit(solution)/shard_map/all_to_all | solution.py:919
  16.4 70.9 %collective-permute-start.21 = (bf16[4,3,8,128]{3,2,1,0:T(8,128)(2,1)S(1)}, bf16[4,3,8,128]{3,2,1,0:T(8,128)(2,1)S(1)}, u32[]{:S(2)}, u32[]{:S(2)}) collective-permute-start(bf16[4,3,8,128]{3,2,1,0:T(8,128)(2,1)S(1)} %broadcast_in_dim.159), channel_id=1, source_target_pairs={{0,1},{1,2},{2,3},{4,5},{5,6},{6,7},{8,9},{9,10},{10,11},{12,13},{... | collective-permute-start | bytes 73736 | tf_op jit(solution)/shard_map/ppermute | solution.py:92
  18.8 68.5 %collective-permute-start.22 = (bf16[4,3,8,128]{3,2,1,0:T(8,128)(2,1)S(1)}, bf16[4,3,8,128]{3,2,1,0:T(8,128)(2,1)S(1)}, u32[]{:S(2)}, u32[]{:S(2)}) collective-permute-start(bf16[4,3,8,128]{3,2,1,0:T(8,128)(2,1)S(1)} %broadcast_in_dim.161), channel_id=1, source_target_pairs={{1,0},{2,1},{3,2},{5,4},{6,5},{7,6},{9,8},{10,9},{11,10},{13,12},{... | collective-permute-start | bytes 73736 | tf_op jit(solution)/shard_map/ppermute | solution.py:93
  20.8 8.8 %collective-permute-start.5 = (bf16[2,592,128]{2,1,0:T(8,128)(2,1)S(1)}, bf16[2,592,128]{2,1,0:T(8,128)(2,1)S(1)}, u32[]{:S(2)}, u32[]{:S(2)}) collective-permute-start(bf16[2,592,128]{2,1,0:T(8,128)(2,1)S(1)} %pad_maximum_fusion.3), channel_id=1, source_target_pairs={{0,8},{4,12},{8,0},{12,4},{16,24},{20,28},{24,16},{28,20},{1,9},{5... | collective-permute-start | bytes 909320 | tf_op jit(solution)/shard_map/ppermute | solution.py:58
  29.7 16.4 %collective-permute-start.6 = (bf16[4,592,128]{2,1,0:T(8,128)(2,1)S(1)}, bf16[4,592,128]{2,1,0:T(8,128)(2,1)S(1)}, u32[]{:S(2)}, u32[]{:S(2)}) collective-permute-start(bf16[4,592,128]{2,1,0:T(8,128)(2,1)S(1)} %pad_maximum_fusion.2), channel_id=1, source_target_pairs={{0,4},{4,0},{8,12},{12,8},{16,20},{20,16},{24,28},{28,24},{1,5},{5... | collective-permute-start | bytes 1818632 | tf_op jit(solution)/shard_map/ppermute | solution.py:58
  46.2 28.8 %collective-permute-start.7 = (bf16[8,592,128]{2,1,0:T(8,128)(2,1)S(1)}, bf16[8,592,128]{2,1,0:T(8,128)(2,1)S(1)}, u32[]{:S(2)}, u32[]{:S(2)}) collective-permute-start(bf16[8,592,128]{2,1,0:T(8,128)(2,1)S(1)} %pad_maximum_fusion.1), channel_id=1, source_target_pairs={{0,2},{1,3},{2,0},{3,1},{4,6},{5,7},{6,4},{7,5},{8,10},{9,11},{10,... | collective-permute-start | bytes 3637256 | tf_op jit(solution)/shard_map/ppermute | solution.py:58
  76.7 83.2 %collective-permute-start.8 = (bf16[16,592,128]{2,1,0:T(8,128)(2,1)}, bf16[16,592,128]{2,1,0:T(8,128)(2,1)}, u32[]{:S(2)}, u32[]{:S(2)}) collective-permute-start(bf16[16,592,128]{2,1,0:T(8,128)(2,1)} %get-tuple-element.150), channel_id=1, source_target_pairs={{0,1},{1,0},{2,3},{3,2},{4,5},{5,4},{6,7},{7,6},{8,9},{9,8},{10,11... | collective-permute-start | bytes 7274504 | tf_op jit(solution)/shard_map/ppermute | solution.py:58
  87.7 5.1 collective-permute-start.23
  91.2 6.0 %collective-permute-start.24 = (bf16[3,30,2,128]{3,2,1,0:T(2,128)(2,1)S(1)}, bf16[3,30,2,128]{3,2,1,0:T(2,128)(2,1)S(1)}, u32[]{:S(2)}, u32[]{:S(2)}) collective-permute-start(bf16[3,30,2,128]{3,2,1,0:T(2,128)(2,1)S(1)} %bitcast.142), channel_id=1, source_target_pairs={{4,0},{8,4},{12,8},{16,12},{20,16},{24,20},{28,24},{5,1},{9,5},{13... | collective-permute-start | bytes 138248 | tf_op jit(solution)/shard_map/ppermute | solution.py:98
  97.8 18.3 %all-to-all-start.3 = ((bf16[4,2,30720]{2,1,0:T(2,128)(2,1)}), bf16[4,2,30720]{2,1,0:T(2,128)(2,1)S(1)}, u32[]{:S(2)}, u32[]{:S(2)}) async-start(bf16[4,2,30720]{2,1,0:T(2,128)(2,1)} %reshape.367), calls=%async_computation.3 | async-start | bytes 983040 | tf_op jit(solution)/shard_map/all_to_all | solution.py:920
  104.5 10.3 %copy-start.13 = (bf16[3,30,2,1,128]{4,3,2,1,0:T(2,128)(2,1)S(1)}, bf16[3,30,2,1,128]{4,3,2,1,0:T(2,128)(2,1)}, u32[]{:S(2)}) copy-start(bf16[3,30,2,1,128]{4,3,2,1,0:T(2,128)(2,1)} %copy.338) | copy-start | bytes 138244
  104.5 10.3 %copy-start.14 = (bf16[3,30,2,1,128]{4,3,2,1,0:T(2,128)(2,1)S(1)}, bf16[3,30,2,1,128]{4,3,2,1,0:T(2,128)(2,1)}, u32[]{:S(2)}) copy-start(bf16[3,30,2,1,128]{4,3,2,1,0:T(2,128)(2,1)} %copy.339) | copy-start | bytes 138244
  110.3 15.3 %collective-permute-start = (bf16[8,3,8,80]{3,1,2,0:T(4,128)(2,1)}, bf16[8,3,8,80]{3,1,2,0:T(4,128)(2,1)}, u32[]{:S(2)}, u32[]{:S(2)}) collective-permute-start(bf16[8,3,8,80]{3,1,2,0:T(4,128)(2,1)} %get-tuple-element.170), channel_id=1, source_target_pairs={{0,1},{1,2},{2,3},{4,5},{5,6},{6,7},{8,9},{9,10},{10,11},{12,13},{... | collective-permute-start | bytes 92168 | tf_op jit(solution)/shard_map/ppermute | solution.py:92
  113.3 15.4 %collective-permute-start.1 = (bf16[8,3,8,80]{3,1,2,0:T(4,128)(2,1)}, bf16[8,3,8,80]{3,1,2,0:T(4,128)(2,1)}, u32[]{:S(2)}, u32[]{:S(2)}) collective-permute-start(bf16[8,3,8,80]{3,1,2,0:T(4,128)(2,1)} %get-tuple-element.171), channel_id=1, source_target_pairs={{1,0},{2,1},{3,2},{5,4},{6,5},{7,6},{9,8},{10,9},{11,10},{13,12},{... | collective-permute-start | bytes 92168 | tf_op jit(solution)/shard_map/ppermute | solution.py:93
  132.7 8.6 %copy-start = (bf16[8,3,2,4,80]{1,0,3,2,4:T(8,128)(2,1)S(1)}, bf16[8,3,2,4,80]{1,0,3,2,4:T(8,128)(2,1)}, u32[]{:S(2)}) copy-start(bf16[8,3,2,4,80]{1,0,3,2,4:T(8,128)(2,1)} %copy.308) | copy-start | bytes 92164
  134.6 8.4 %collective-permute-start.3 = (bf16[3,54,2,80]{1,0,2,3:T(4,128)(2,1)S(1)}, bf16[3,54,2,80]{1,0,2,3:T(4,128)(2,1)S(1)}, u32[]{:S(2)}, u32[]{:S(2)}) collective-permute-start(bf16[3,54,2,80]{1,0,2,3:T(4,128)(2,1)S(1)} %get-tuple-element.138), channel_id=1, source_target_pairs={{4,0},{8,4},{12,8},{16,12},{20,16},{24,20},{28,24},{5,1},{9,5},{13... | collective-permute-start | bytes 155528 | tf_op jit(solution)/shard_map/ppermute | solution.py:98
  135.9 12.0 %collective-permute-start.2 = (bf16[3,54,2,80]{1,0,2,3:T(4,128)(2,1)S(1)}, bf16[3,54,2,80]{1,0,2,3:T(4,128)(2,1)S(1)}, u32[]{:S(2)}, u32[]{:S(2)}) collective-permute-start(bf16[3,54,2,80]{1,0,2,3:T(4,128)(2,1)S(1)} %get-tuple-element.137), channel_id=1, source_target_pairs={{0,4},{4,8},{8,12},{12,16},{16,20},{20,24},{24,28},{1,5},{5,9},{9,... | collective-permute-start | bytes 155528 | tf_op jit(solution)/shard_map/ppermute | solution.py:97
  201.9 14.9 %all-to-all-start.1 = ((f32[32,8,256]{2,1,0:T(8,128)}), f32[32,8,256]{2,1,0:T(8,128)S(1)}, u32[]{:S(2)}, u32[]{:S(2)}) async-start(f32[32,8,256]{2,1,0:T(8,128)} %broadcast_in_dim.145), calls=%async_computation.1 | async-start | bytes 524288 | tf_op jit(solution)/shard_map/all_to_all | solution.py:80
  216.8 0.7 copy-start.10
  217.6 18.1 %copy-start.5 = (bf16[14,48,8,80]{3,2,1,0:T(8,128)(2,1)S(1)}, bf16[14,48,8,80]{3,2,1,0:T(8,128)(2,1)}, u32[]{:S(2)}) copy-start(bf16[14,48,8,80]{3,2,1,0:T(8,128)(2,1)} %get-tuple-element.143) | copy-start | bytes 2580484
  233.8 23.5 %collective-permute-start.9 = (bf16[4,3,8,512]{3,0,2,1:T(4,128)(2,1)S(1)}, bf16[4,3,8,512]{3,0,2,1:T(4,128)(2,1)S(1)}, u32[]{:S(2)}, u32[]{:S(2)}) collective-permute-start(bf16[4,3,8,512]{3,0,2,1:T(4,128)(2,1)S(1)} %copy.358), channel_id=1, source_target_pairs={{0,1},{1,2},{2,3},{4,5},{5,6},{6,7},{8,9},{9,10},{10,11},{12,13},{... | collective-permute-start | bytes 294920 | tf_op jit(solution)/shard_map/ppermute | solution.py:92
  243.0 12.8 %copy-start.7 = (bf16[768,512]{1,0:T(8,128)(2,1)S(1)}, bf16[768,512]{1,0:T(8,128)(2,1)}, u32[]{:S(2)}) copy-start(bf16[768,512]{1,0:T(8,128)(2,1)} %get-tuple-element.80.refs_2_) | copy-start | bytes 2359300
  256.1 3.2 collective-permute-start.10
  259.6 6.4 %collective-permute-start.11 = (bf16[3,30,2,512]{3,2,1,0:T(2,128)(2,1)S(1)}, bf16[3,30,2,512]{3,2,1,0:T(2,128)(2,1)S(1)}, u32[]{:S(2)}, u32[]{:S(2)}) collective-permute-start(bf16[3,30,2,512]{3,2,1,0:T(2,128)(2,1)S(1)} %get-tuple-element.160), channel_id=1, source_target_pairs={{0,4},{4,8},{8,12},{12,16},{16,20},{20,24},{24,28},{1,5},{5,9},{9,... | collective-permute-start | bytes 552968 | tf_op jit(solution)/shard_map/ppermute | solution.py:97
  263.0 7.4 %collective-permute-start.12 = (bf16[3,30,2,512]{3,2,1,0:T(2,128)(2,1)S(1)}, bf16[3,30,2,512]{3,2,1,0:T(2,128)(2,1)S(1)}, u32[]{:S(2)}, u32[]{:S(2)}) collective-permute-start(bf16[3,30,2,512]{3,2,1,0:T(2,128)(2,1)S(1)} %get-tuple-element.161), channel_id=1, source_target_pairs={{4,0},{8,4},{12,8},{16,12},{20,16},{24,20},{28,24},{5,1},{9,5},{13... | collective-permute-start | bytes 552968 | tf_op jit(solution)/shard_map/ppermute | solution.py:98
  280.0 17.3 %copy-start.2 = (bf16[14,48,8,80]{3,2,1,0:T(8,128)(2,1)S(1)}, bf16[14,48,8,80]{3,2,1,0:T(8,128)(2,1)}, u32[]{:S(2)}) copy-start(bf16[14,48,8,80]{3,2,1,0:T(8,128)(2,1)} %get-tuple-element.139) | copy-start | bytes 2580484
  280.0 17.3 %copy-start.3 = (bf16[14,48,8,80]{3,2,1,0:T(8,128)(2,1)S(1)}, bf16[14,48,8,80]{3,2,1,0:T(8,128)(2,1)}, u32[]{:S(2)}) copy-start(bf16[14,48,8,80]{3,2,1,0:T(8,128)(2,1)} %get-tuple-element.140) | copy-start | bytes 2580484
  280.0 17.3 %copy-start.4 = (bf16[14,48,8,80]{3,2,1,0:T(8,128)(2,1)S(1)}, bf16[14,48,8,80]{3,2,1,0:T(8,128)(2,1)}, u32[]{:S(2)}) copy-start(bf16[14,48,8,80]{3,2,1,0:T(8,128)(2,1)} %get-tuple-element.141) | copy-start | bytes 2580484
  292.8 16.2 %collective-permute-start.17 = (bf16[4,3,8,512]{3,0,2,1:T(4,128)(2,1)}, bf16[4,3,8,512]{3,0,2,1:T(4,128)(2,1)}, u32[]{:S(2)}, u32[]{:S(2)}) collective-permute-start(bf16[4,3,8,512]{3,0,2,1:T(4,128)(2,1)} %copy.362), channel_id=1, source_target_pairs={{0,1},{1,2},{2,3},{4,5},{5,6},{6,7},{8,9},{9,10},{10,11},{12,13},{... | collective-permute-start | bytes 294920 | tf_op jit(solution)/shard_map/ppermute | solution.py:92
  300.5 7.1 %copy-start.12 = (bf16[4,3,8,512]{3,2,1,0:T(8,128)(2,1)S(1)}, bf16[4,3,8,512]{3,2,1,0:T(8,128)(2,1)}, u32[]{:S(2)}) copy-start(bf16[4,3,8,512]{3,2,1,0:T(8,128)(2,1)} %get-tuple-element.164) | copy-start | bytes 294916
  303.8 19.4 %all-to-all-start.2 = ((f32[32,8,512]{2,1,0:T(8,128)}), f32[32,8,512]{2,1,0:T(8,128)S(1)}, u32[]{:S(2)}, u32[]{:S(2)}) async-start(f32[32,8,512]{2,1,0:T(8,128)} %broadcast_in_dim.151), calls=%async_computation.2 | async-start | bytes 1048576 | tf_op jit(solution)/shard_map/all_to_all | solution.py:80
  307.7 3.2 collective-permute-start.18
  311.9 36.7 %collective-permute-start.19 = (bf16[3,30,2,512]{3,2,1,0:T(2,128)(2,1)}, bf16[3,30,2,512]{3,2,1,0:T(2,128)(2,1)S(1)}, u32[]{:S(2)}, u32[]{:S(2)}) collective-permute-start(bf16[3,30,2,512]{3,2,1,0:T(2,128)(2,1)} %get-tuple-element.152), channel_id=1, source_target_pairs={{0,4},{4,8},{8,12},{12,16},{16,20},{20,24},{24,28},{1,5},{5,9},{9,... | collective-permute-start | bytes 552968 | tf_op jit(solution)/shard_map/ppermute | solution.py:97
  315.6 33.1 %collective-permute-start.20 = (bf16[3,30,2,512]{3,2,1,0:T(2,128)(2,1)S(1)}, bf16[3,30,2,512]{3,2,1,0:T(2,128)(2,1)S(1)}, u32[]{:S(2)}, u32[]{:S(2)}) collective-permute-start(bf16[3,30,2,512]{3,2,1,0:T(2,128)(2,1)S(1)} %get-tuple-element.153), channel_id=1, source_target_pairs={{4,0},{8,4},{12,8},{16,12},{20,16},{24,20},{28,24},{5,1},{9,5},{13... | collective-permute-start | bytes 552968 | tf_op jit(solution)/shard_map/ppermute | solution.py:98
  323.2 0.8 copy-start.6
  345.8 19.0 %collective-permute-start.13 = (bf16[4,3,8,512]{3,0,2,1:T(4,128)(2,1)}, bf16[4,3,8,512]{3,0,2,1:T(4,128)(2,1)}, u32[]{:S(2)}, u32[]{:S(2)}) collective-permute-start(bf16[4,3,8,512]{3,0,2,1:T(4,128)(2,1)} %copy.360), channel_id=1, source_target_pairs={{0,1},{1,2},{2,3},{4,5},{5,6},{6,7},{8,9},{9,10},{10,11},{12,13},{... | collective-permute-start | bytes 294920 | tf_op jit(solution)/shard_map/ppermute | solution.py:92
  354.4 2.2 copy-start.8
  354.4 3.8 copy-start.19
  356.9 9.8 %collective-permute-start.14 = (bf16[4,3,8,512]{3,0,2,1:T(4,128)(2,1)S(1)}, bf16[4,3,8,512]{3,0,2,1:T(4,128)(2,1)S(1)}, u32[]{:S(2)}, u32[]{:S(2)}) collective-permute-start(bf16[4,3,8,512]{3,0,2,1:T(4,128)(2,1)S(1)} %copy.361), channel_id=1, source_target_pairs={{1,0},{2,1},{3,2},{5,4},{6,5},{7,6},{9,8},{10,9},{11,10},{13,12},{... | collective-permute-start | bytes 294920 | tf_op jit(solution)/shard_map/ppermute | solution.py:93
  359.0 29.5 %all-to-all-start.4 = ((f32[32,8,512]{2,1,0:T(8,128)}), f32[32,8,512]{2,1,0:T(8,128)S(1)}, u32[]{:S(2)}, u32[]{:S(2)}) async-start(f32[32,8,512]{2,1,0:T(8,128)} %broadcast_in_dim.154), calls=%async_computation.4 | async-start | bytes 1048576 | tf_op jit(solution)/shard_map/all_to_all | solution.py:80
  367.1 11.3 %collective-permute-start.15 = (bf16[3,30,2,512]{3,2,1,0:T(2,128)(2,1)S(1)}, bf16[3,30,2,512]{3,2,1,0:T(2,128)(2,1)S(1)}, u32[]{:S(2)}, u32[]{:S(2)}) collective-permute-start(bf16[3,30,2,512]{3,2,1,0:T(2,128)(2,1)S(1)} %get-tuple-element.156), channel_id=1, source_target_pairs={{0,4},{4,8},{8,12},{12,16},{16,20},{20,24},{24,28},{1,5},{5,9},{9,... | collective-permute-start | bytes 552968 | tf_op jit(solution)/shard_map/ppermute | solution.py:97
  370.7 9.9 %collective-permute-start.16 = (bf16[3,30,2,512]{3,2,1,0:T(2,128)(2,1)S(1)}, bf16[3,30,2,512]{3,2,1,0:T(2,128)(2,1)S(1)}, u32[]{:S(2)}, u32[]{:S(2)}) collective-permute-start(bf16[3,30,2,512]{3,2,1,0:T(2,128)(2,1)S(1)} %get-tuple-element.157), channel_id=1, source_target_pairs={{4,0},{8,4},{12,8},{16,12},{20,16},{24,20},{28,24},{5,1},{9,5},{13... | collective-permute-start | bytes 552968 | tf_op jit(solution)/shard_map/ppermute | solution.py:98
  388.5 0.8 copy-start.11
  427.6 28.3 %all-to-all-start.5 = ((f32[32,8,256]{2,1,0:T(8,128)}), f32[32,8,256]{2,1,0:T(8,128)S(1)}, u32[]{:S(2)}, u32[]{:S(2)}) async-start(f32[32,8,256]{2,1,0:T(8,128)} %broadcast_in_dim.164), calls=%async_computation.5 | async-start | bytes 524288 | tf_op jit(solution)/shard_map/all_to_all | solution.py:80
  456.0 0.7 copy-start.18
  496.6 4.8 collective-permute-start.25
  504.5 29.0 %collective-permute-start.26 = (bf16[8,592,128]{2,1,0:T(8,128)(2,1)S(1)}, bf16[8,592,128]{2,1,0:T(8,128)(2,1)S(1)}, u32[]{:S(2)}, u32[]{:S(2)}) collective-permute-start(bf16[8,592,128]{2,1,0:T(8,128)(2,1)S(1)} %slice.277), channel_id=1, source_target_pairs={{0,2},{1,3},{2,0},{3,1},{4,6},{5,7},{6,4},{7,5},{8,10},{9,11},{10,... | collective-permute-start | bytes 3637256 | tf_op jit(solution)/shard_map/ppermute | solution.py:58
  533.8 15.2 %collective-permute-start.27 = (bf16[4,592,128]{2,1,0:T(8,128)(2,1)S(1)}, bf16[4,592,128]{2,1,0:T(8,128)(2,1)S(1)}, u32[]{:S(2)}, u32[]{:S(2)}) collective-permute-start(bf16[4,592,128]{2,1,0:T(8,128)(2,1)S(1)} %slice.278), channel_id=1, source_target_pairs={{0,4},{4,0},{8,12},{12,8},{16,20},{20,16},{24,28},{28,24},{1,5},{5... | collective-permute-start | bytes 1818632 | tf_op jit(solution)/shard_map/ppermute | solution.py:58
  549.2 33.3 %copy-start.9 = (f32[72072]{0:T(1024)S(1)}, f32[72072]{0:T(1024)}, u32[]{:S(2)}) copy-start(f32[72072]{0:T(1024)} %param.12) | copy-start | bytes 864868
  549.2 33.3 %copy-start.15 = (f32[72072]{0:T(1024)S(1)}, f32[72072]{0:T(1024)}, u32[]{:S(2)}) copy-start(f32[72072]{0:T(1024)} %param.13) | copy-start | bytes 864868
  549.2 33.3 %copy-start.16 = (f32[72072]{0:T(1024)S(1)}, f32[72072]{0:T(1024)}, u32[]{:S(2)}) copy-start(f32[72072]{0:T(1024)} %param.14) | copy-start | bytes 864868
  549.2 7.8 %collective-permute-start.28 = (bf16[2,592,128]{2,1,0:T(8,128)(2,1)S(1)}, bf16[2,592,128]{2,1,0:T(8,128)(2,1)S(1)}, u32[]{:S(2)}, u32[]{:S(2)}) collective-permute-start(bf16[2,592,128]{2,1,0:T(8,128)(2,1)S(1)} %slice.279), channel_id=1, source_target_pairs={{0,8},{4,12},{8,0},{12,4},{16,24},{20,28},{24,16},{28,20},{1,9},{5... | collective-permute-start | bytes 909320 | tf_op jit(solution)/shard_map/ppermute | solution.py:58
  557.1 7.8 %collective-permute-start.29 = (bf16[1,592,128]{2,1,0:T(8,128)(2,1)S(1)}, bf16[1,592,128]{2,1,0:T(8,128)(2,1)S(1)}, u32[]{:S(2)}, u32[]{:S(2)}) collective-permute-start(bf16[1,592,128]{2,1,0:T(8,128)(2,1)S(1)} %slice.280), channel_id=1, source_target_pairs={{0,16},{4,20},{8,24},{12,28},{16,0},{20,4},{24,8},{28,12},{1,17},{... | collective-permute-start | bytes 454664 | tf_op jit(solution)/shard_map/ppermute | solution.py:58
  567.7 13.4 %all-to-all-start.6 = ((f32[32,8,128]{2,1,0:T(8,128)}), f32[32,8,128]{2,1,0:T(8,128)S(1)}, u32[]{:S(2)}, u32[]{:S(2)}) async-start(f32[32,8,128]{2,1,0:T(8,128)} %broadcast_in_dim_broadcast_in_dim_broadcast_in_dim.2), calls=%async_computation.6 | async-start | bytes 262144 | tf_op jit(solution)/shard_map/all_to_all | solution.py:80

commit v3 on v2

--- a/solution.py
+++ b/solution.py
@@ -40,10 +40,10 @@
 
 f32 = jnp.float32
 bf16 = jnp.bfloat16
-VMEM_LIMIT = 60 * 1024 * 1024
-
-
-def bit_list():
+VMEM_LIMIT = 34 * 1024 * 1024
+
+
+def plane_bits():
     bits = []
     for axis in AXES:
         count = lax.axis_size(axis)
@@ -51,32 +51,111 @@
         while step >= 1:
             bits.append((axis, count, step))
             step //= 2
-    return bits
+    across = [b for b in bits if b[0] == "lat" and b[2] > 1]
+    within = [b for b in bits if b not in across]
+    return across, within
 
 
 def exchange(values, axis, count, step):
     return lax.ppermute(values, axis, [(i, i ^ step) for i in range(count)])
 
 
-def gather_blocks(block):
-    blocks = block[None]
-    for axis, count, step in bit_list():
-        blocks = jnp.concatenate([blocks, exchange(blocks, axis, count, step)], axis=0)
-    return blocks
-
-
-def scatter_blocks(keep, send):
-    for turn, (axis, count, step) in enumerate(reversed(bit_list())):
-        if turn > 0:
-            half = keep.shape[0] // 2
-            keep, send = keep[:half], keep[half:].astype(bf16)
-        keep = keep + exchange(send, axis, count, step).astype(f32)
-    return keep[0]
-
-
-def spread(tile):
-    count = lax.axis_size(AXES)
-    copies = jnp.broadcast_to(tile[None], (count,) + tile.shape)
+def half_rows_of(tall):
+    return -(-tall // 32) * 16
+
+
+def gather_steps(near, far):
+    across, (first, second, *others) = plane_bits()
+
+    def plane_step(bit):
+        return lambda blocks: jnp.concatenate([blocks, exchange(blocks, *bit)], axis=0)
+
+    def pick(blocks):
+        planes = blocks.shape[0]
+        plane = lax.axis_index("lat") // 2
+        found = [lax.dynamic_index_in_dim(blocks, seat_of(plane, p, planes), 0, False) for p in range(planes)]
+        return [jnp.stack([found[p] for p in group]) for group in (near, far)]
+
+    return [plane_step(bit) for bit in across], pick
+
+
+def within_steps():
+    _, (first, second, *others) = plane_bits()
+
+    def halves(blocks):
+        cut = half_rows_of(blocks.shape[1])
+        left, right = blocks[:, :cut], blocks[:, cut:]
+        left = jnp.stack([left, exchange(left, *first)], axis=0)
+        right = jnp.stack([right, exchange(right, *second)], axis=0)
+        return left, right
+
+    def join(state):
+        left, right = state
+        left = jnp.stack([left, exchange(left, *second)], axis=0)
+        right = jnp.stack([right, exchange(right, *first)], axis=1)
+        both = jnp.concatenate([left, right], axis=3)
+        return both.reshape((-1,) + both.shape[3:])
+
+    def rest(both):
+        for bit in others:
+            both = jnp.concatenate([both, exchange(both, *bit)], axis=0)
+        return both
+
+    return [halves, join, rest]
+
+
+def scatter_steps(keep, send, planes):
+    _, (first, second, *others) = plane_bits()
+    cut = half_rows_of(keep.shape[1])
+
+    def inner(turn, bit):
+        def step(state):
+            keep, send = state
+            if turn > 0:
+                half = keep.shape[0] // 2
+                keep, send = keep[:half], keep[half:].astype(bf16)
+            keep = keep + exchange(send, *bit).astype(f32)
+            return keep, None
+
+        return step
+
+    def outer(state):
+        keep, _ = state
+        parts = keep.reshape((2, 2, len(planes)) + keep.shape[1:])
+        left, right = parts[:, :, :, :cut], parts[:, :, :, cut:]
+        left = left[0] + exchange(left[1].astype(bf16), *second).astype(f32)
+        right = right[:, 0] + exchange(right[:, 1].astype(bf16), *first).astype(f32)
+        return left, right
+
+    def last(state):
+        left, right = state
+        left = left[0] + exchange(left[1].astype(bf16), *first).astype(f32)
+        right = right[0] + exchange(right[1].astype(bf16), *second).astype(f32)
+        return jnp.concatenate([left, right], axis=1)
+
+    steps = [inner(turn, bit) for turn, bit in enumerate(reversed(others))]
+    return (keep, send), steps + [outer, last, lambda sums: scatter_planes(sums, planes)]
+
+
+def tie(first, second):
+    return lax.optimization_barrier((first, second))
+
+
+def scatter_planes(sums, planes):
+    count = lax.axis_size("lat")
+    total = count // 2
+    plane = lax.axis_index("lat") // 2
+    empty = jnp.zeros(sums.shape[1:], f32)
+    rows = jnp.stack([sums[planes.index(p)] if p in planes else empty for p in range(total)])
+    mine = lax.dynamic_index_in_dim(rows, plane, 0, False)
+    for away in range(1, total):
+        pairs = [(i, i ^ (2 * away)) for i in range(count) if (i // 2) ^ away in planes]
+        part = lax.dynamic_index_in_dim(rows, plane ^ away, 0, False).astype(bf16)
+        mine = mine + lax.ppermute(part, "lat", pairs).astype(f32)
+    return mine
+
+
+def swap(copies):
     return lax.all_to_all(copies, AXES, 0, 0, tiled=True)
 
 
@@ -85,29 +164,17 @@
     return [(i, i + 1) for i in range(ends)], [(i + 1, i) for i in range(ends)]
 
 
-def with_halo(cells):
-    rows, cols, blocks, chans = cells.shape
-    bands = blocks // 2
+def columns_out(cells, rows, cols):
+    split = cells.reshape(rows, cols, 8, cells.shape[-1])
     onward, back = neighbours("lvl")
-    left = lax.ppermute(cells[:, cols - REACH :], "lvl", onward)
-    right = lax.ppermute(cells[:, :REACH], "lvl", back)
-    cells = jnp.concatenate([left, cells, right], axis=1)
-    cells = cells.reshape(rows, cols + 2 * REACH, 2, bands, chans)
+    left = lax.ppermute(split[:, cols - REACH :].reshape(-1, cells.shape[-1]), "lvl", onward)
+    right = lax.ppermute(split[:, :REACH].reshape(-1, cells.shape[-1]), "lvl", back)
+    return left, right
+
+
+def lines_out(lower, upper):
     onward, back = neighbours("lat")
-    above = lax.ppermute(cells[rows - REACH :, :, :, bands - 1], "lat", onward)
-    below = lax.ppermute(cells[:REACH, :, :, 0], "lat", back)
-    top = jnp.concatenate([above[:, :, :, None], cells[rows - REACH :, :, :, : bands - 1]], axis=3)
-    bottom = jnp.concatenate([cells[:REACH, :, :, 1:], below[:, :, :, None]], axis=3)
-    return jnp.concatenate([top, cells, bottom], axis=0).reshape(
-        rows + 2 * REACH, cols + 2 * REACH, blocks, chans
-    )
-
-
-def to_cells(grid):
-    chans, batch, rows, cols = grid.shape
-    bands = BLOCKS // batch
-    split = grid.reshape(chans, batch, bands, rows // bands, cols)
-    return split.transpose(3, 4, 1, 2, 0).reshape(rows // bands, cols, BLOCKS, chans)
+    return lax.ppermute(lower, "lat", onward), lax.ppermute(upper, "lat", back)
 
 
 def depth_cells(depth, batch):
@@ -213,7 +280,7 @@
     return jnp.stack(lines, axis=1).reshape(rows * cols * 8, chans)
 
 
-def call(kernel, outs, grid=(), ins=None, out_specs=None, scratch=(), flops=0, name=None):
+def call(kernel, outs, grid=(), ins=None, out_specs=None, scratch=(), micros=5, name=None):
     params = dict(out_shape=[jax.ShapeDtypeStruct(s, t) for s, t in outs])
     if ins:
         params.update(in_specs=ins)
@@ -223,7 +290,7 @@
         kernel,
         scratch_shapes=list(scratch),
         compiler_params=pltpu.CompilerParams(vmem_limit_bytes=VMEM_LIMIT),
-        cost_estimate=pl.CostEstimate(flops=flops, bytes_accessed=1000000, transcendentals=0),
+        cost_estimate=pl.CostEstimate(flops=int(micros * 1.1e9), bytes_accessed=100000, transcendentals=0),
         name=name,
         **params,
     )
@@ -241,44 +308,231 @@
     return pl.BlockSpec((rows, LANES), lambda i: (0, i))
 
 
+def stats_tile(devices):
+    return pl.BlockSpec((devices, 8, LANES), lambda i: (0, 0, i))
+
+
 TAP_TILE = pl.BlockSpec((TAPS, 8, LANES), lambda i: (0, 0, i))
 
 
 def conv_sums(source, taps, depth, counts, out, stats, rows, cols, masked=None):
+    lane = lax.broadcasted_iota(jnp.int32, (64, LANES), 1)
+    mark = jnp.where(pl.program_id(0) == WIDTH2 // LANES, WIDTH2 % LANES, -1)
+
     def emit(place, total, carry):
         flat = total.reshape(64, LANES)
         out[place, :] = flat
-        kept = jnp.where(depth[place, :] > 0.0, flat, 0.0)
+        ocean = depth[place, :] > 0.0
+        kept = jnp.where(ocean, flat, 0.0)
         if masked is not None:
-            masked[place, :] = kept.astype(bf16)
+            masked[place, :] = jnp.where(lane == mark, jnp.where(ocean, 1.0, 0.0), kept).astype(bf16)
         kept_cells = kept.reshape(8, 8, LANES)
         return (carry[0] + jnp.sum(kept_cells, axis=0), carry[1] + jnp.sum(kept_cells * total, axis=0))
 
     zero = jnp.zeros((8, LANES), f32)
     first, second = convolve(source, taps, rows, cols, emit, (zero, zero))
-    stats[...] = counts[...]
-    stats[0:1, :] = row_sum(first)
-    stats[1:2, :] = row_sum(second)
-
-
-def stem_kernel(rows, cols, fields, stem, taps, depth, counts, hzero, out, stats, source):
+    index = lax.broadcasted_iota(jnp.int32, (8, LANES), 0)
+    tile = jnp.where(index == 0, row_sum(first), jnp.where(index == 1, row_sum(second), counts[...]))
+    stats[...] = jnp.broadcast_to(tile[None], stats.shape)
+
+
+def lay_border(rows, cols, source, held, centre, left, right, above, below):
     width = cols + 2 * REACH
+    sides = [part[...].astype(f32) for part in (left, right)]
+    for row in range(rows):
+        start = (row + REACH) * width
+        source[rows8(start + REACH, cols), :] = centre[rows8(row * cols, cols), :].astype(f32)
+        for side, place in zip(sides, (0, cols + REACH)):
+            source[rows8(start + place, REACH), :] = side[row * REACH * 8 : (row + 1) * REACH * 8]
+    for t in range(REACH):
+        for start, target, way in ((rows + t, t, 1), (REACH + t, rows + REACH + t, 7)):
+            line = source[rows8(start * width, width), :].reshape(width, 8, LANES)
+            source[rows8(target * width, width), :] = pltpu.roll(line, way, 1).reshape(width * 8, LANES)
+    amount = REACH * width
+    for part, base in ((above, 0), (below, (rows + REACH) * width * 8 + BLOCKS // 2 - 1)):
+        held[...] = part[...].astype(f32)
+        for b in range(2):
+            values = held[pl.ds(b, amount, stride=2), :]
+            source[pl.ds(base + b * (BLOCKS // 2), amount, stride=8), :] = values
+
+
+def pack_kernel(parts, cols, reach, values, out, tiles, turned, flat):
+    total = values.shape[1]
+    width = cols + 2 * reach
+    lanes = out.shape[2]
+    for k in range(-(-total // LANES)):
+        size = min(LANES, total - k * LANES)
+        tiles[k, :, :size] = values[:, k * LANES : k * LANES + size].astype(f32)
+    turned[...] = jnp.zeros(turned.shape, f32)
+    depth = values.shape[0] // lanes
+    for row in range(depth):
+        for k in range(-(-total // LANES)):
+            size = min(LANES, total - k * LANES)
+            piece = tiles[k, pl.ds(row, lanes, stride=depth), :].T
+            turned[8 + k * LANES : 8 + k * LANES + size, :] = piece[:size]
+        for part in range(parts):
+            start = 8 + part * cols - reach
+            flat[part, row * width : (row + 1) * width, :] = turned[start : start + width, :]
+    for part in range(parts):
+        out[part] = flat[part].astype(bf16)
+
+
+def unpack_cells(packed, parts, cells):
+    lanes = packed.shape[2]
+    chans = lanes // BLOCKS
+    amount = packed.shape[1]
+    source = lax.broadcasted_iota(jnp.int32, (lanes, LANES), 0)
+    target = lax.broadcasted_iota(jnp.int32, (lanes, LANES), 1)
+    for s in range(BLOCKS):
+        total = jnp.zeros((amount, LANES), f32)
+        for part in range(parts):
+            pick = ((target - part * chans) * BLOCKS + s == source).astype(bf16)
+            total = total + nn(packed[part], pick)
+        cells[pl.ds(s, amount, stride=BLOCKS), :] = total
+
+
+def targets_kernel(parts, packed, out, cells):
+    unpack_cells(packed, parts, cells)
+    out[...] = cells[...].astype(bf16)
+
+
+def fields_kernel(parts, rows, cols, packed, cells, lower, upper, held):
+    unpack_cells(packed, parts, cells)
+    width = cols + 2 * REACH
+    room = -(-width // 8) * 8
+    held[...] = jnp.zeros(held.shape, f32)
+    for out, low, band in ((lower, rows - REACH, BLOCKS // 2 - 1), (upper, 0, 0)):
+        for b in range(2):
+            for t in range(REACH):
+                start = (low + t) * width * 8 + band + b * (BLOCKS // 2)
+                at = (b * REACH + t) * room
+                held[at : at + width, :] = cells[pl.ds(start, width, stride=8), :]
+        out[...] = held[...].astype(bf16)
+
+
+def shift_kernel(rows, cols, cells, above, below, first, second, third, ends, far, farther):
+    width = cols + 2 * REACH
+    room = -(-width // 8) * 8
+    line = width * 8
+    for t in range(REACH):
+        for k, row, way in ((t, rows - REACH + t, 1), (REACH + t, t, 7)):
+            values = cells[row * line : (row + 1) * line, :].reshape(width, 8, LANES)
+            ends[k * line : (k + 1) * line, :] = pltpu.roll(values, way, 1).reshape(line, LANES)
+    for part, base, band in ((above, 0, 0), (below, REACH, BLOCKS // 2 - 1)):
+        values = part[...].astype(f32)
+        for b in range(2):
+            for t in range(REACH):
+                at = (b * REACH + t) * room
+                start = (base + t) * line + band + b * (BLOCKS // 2)
+                ends[pl.ds(start, width, stride=8), :] = values[at : at + width]
+
+    def row_values(row):
+        if row < REACH:
+            return ends, row * line
+        if row < REACH + rows:
+            return cells, (row - REACH) * line
+        return ends, (row - rows) * line
+
+    total = rows + 2 * REACH
+    for row in range(total):
+        ref, start = row_values(row)
+        values = ref[start : start + line, :]
+        far[row * line : (row + 1) * line, :] = pltpu.roll(values, CIN, 1)
+        farther[row * line : (row + 1) * line, :] = pltpu.roll(values, 2 * CIN - LANES, 1)
+    for k in range(2):
+        far[(total + k) * line : (total + k + 1) * line, :] = jnp.zeros((line, LANES), f32)
+        farther[(total + k) * line : (total + k + 1) * line, :] = jnp.zeros((line, LANES), f32)
+    amount = cols * 8
+    lane = lax.broadcasted_iota(jnp.int32, (amount, LANES), 1)
+    for row in range(total):
+        ref, start = row_values(row)
+        for out, near, middle, last in (
+            (first, 0, row * line + 8, row * line + 16),
+            (second, 24, row * line + 32, row * line + 40),
+            (third, 48, (row + 1) * line + 48, (row + 2) * line + 48),
+        ):
+            mid = far[middle : middle + amount, :]
+            place = slice(row * amount, (row + 1) * amount)
+            out[place, :LANES] = jnp.where(lane < CIN, ref[start + near : start + near + amount, :], mid).astype(bf16)
+            out[place, LANES:] = jnp.where(lane < 2 * CIN - LANES, mid, farther[last : last + amount, :]).astype(bf16)
+
+
+def wide_stem(stem):
+    return jnp.concatenate([stem.astype(f32), jnp.zeros((C1, C1 - CI), f32)], axis=1)
+
+
+def triple_stem(stem):
+    wide = wide_stem(stem)
+    return wide + pltpu.roll(wide, CIN, 1) + pltpu.roll(wide, 2 * CIN, 1)
+
+
+def stem_kernel(
+    rows, cols, first, second, third, near, stem, pick, depth, counts, hzero, out, stats, weights, stem3, sums
+):
+    amount = cols * 8
+    stem3[...] = triple_stem(stem[...])
+
+    def weight(index, carry):
+        both = nt(near[...], pick[index]) * stem3[...]
+        weights[pl.ds(pl.multiple_of(index * C1, C1), C1), :] = both.astype(bf16)
+        return carry
+
+    lax.fori_loop(0, GROUPS, weight, 0)
+    wide = wide_stem(stem[...]).astype(bf16)
+    sums[...] = jnp.zeros(sums.shape, f32)
 
     def line(row, carry):
-        place = rows8(row * width, width)
-        source[place, :] = nt(fields[place, :], stem[...]).astype(bf16).astype(f32)
+        def place(shift):
+            return pl.ds(pl.multiple_of((row + shift) * amount, amount), amount)
+
+        total = jnp.zeros((amount, C1), f32)
+        for p in range(KSIZE):
+            total = total + nt(first[place(p), :], weights[p * C1 : (p + 1) * C1, :])
+            total = total + nt(second[place(p), :], weights[(KSIZE + p) * C1 : (KSIZE + p + 1) * C1, :])
+        for k in range(3):
+            at = (2 * KSIZE + k) * C1
+            total = total + nt(third[place(3 * k), :], weights[at : at + C1, :])
+        out[place(0), :] = total
+        hzero[place(0), :] = nt(second[place(REACH), :], wide).astype(bf16)
+        ocean = depth[place(0), :] > 0.0
+        kept = jnp.where(jnp.concatenate([ocean, ocean], axis=1), total, 0.0)
+        sums[0:1, :] += row_sum(kept)
+        sums[1:2, :] += row_sum(kept * total)
         return carry
 
-    lax.fori_loop(0, rows + 2 * REACH, line, 0)
-    for row in range(rows):
-        hzero[rows8(row * cols, cols), :] = source[
-            rows8((row + REACH) * width + REACH, cols), :
-        ].astype(bf16)
-    conv_sums(source, taps, depth, counts, out, stats, rows, cols)
-
-
-def coarse_conv_kernel(rows, cols, border, taps, depth, counts, out, masked, stats, source):
-    source[...] = border[...].astype(f32)
+    lax.fori_loop(0, rows, line, 0)
+    stats[...] = jnp.broadcast_to((sums[...] + counts[...])[None], stats.shape)
+
+
+def edge_kernel(rows, cols, count, *refs):
+    inputs, (lower, upper, held, edge) = refs[: 3 * count], refs[3 * count :]
+    width = cols + 2 * REACH
+    lines = edge_lines(cols)
+    amount = rows * cols * 8
+    side = rows * REACH * 8
+    for k in range(count):
+        for tile in range(C2 // LANES):
+            lanes = slice(tile * LANES, (tile + 1) * LANES)
+            for ref, start, size in zip(inputs[3 * k : 3 * k + 3], (0, amount, amount + side), (amount, side, side)):
+                held[start : start + size, :] = ref[:, lanes].astype(f32)
+            for out, low, band in ((lower, rows - REACH, BLOCKS // 2 - 1), (upper, 0, 0)):
+                edge[lines - 16 :, :] = jnp.zeros((16, LANES), f32)
+                for t in range(REACH):
+                    for b in range(2):
+                        s = band + b * (BLOCKS // 2)
+                        at = t * width * 2 + b
+                        for start, wide, col in ((amount, REACH, 0), (0, cols, REACH), (amount + side, REACH, REACH + cols)):
+                            values = held[pl.ds(start + (low + t) * wide * 8 + s, wide, stride=8), :]
+                            edge[pl.ds(at + 2 * col, wide, stride=2), :] = values
+                out[k * lines : (k + 1) * lines, lanes] = edge[...].astype(bf16)
+
+
+def edge_lines(cols):
+    return -(-REACH * (cols + 2 * REACH) * 2 // 16) * 16
+
+
+def coarse_conv_kernel(rows, cols, centre, left, right, above, below, taps, depth, counts, out, masked, stats, source, held):
+    lay_border(rows, cols, source, held, centre, left, right, above, below)
     conv_sums(source, taps, depth, counts, out, stats, rows, cols, masked)
 
 
@@ -309,8 +563,8 @@
 
 def middle_kernel(
     cols, got, conv, cells, vecs, up, up_bias, down, ups, fine_rows, head, last_rows, tables, hone, targets, depth,
-    skip_out, top_out, dy_out, ds_out, du_out, dtop_out, dv_out, gated_out, da_out, normal_out, dn_out, dx_out,
-    sums, hidden_sums,
+    skip_out, top_out, dy_out, ds_out, du_out, dtop_out, dv_out, gated_out, da_out, normal_out, dx_out,
+    sums, hidden_sums, copies,
 ):
     mean, inverse, _, ocean_count = norm_rows(got)
     scale = inverse * vecs[0:1]
@@ -351,7 +605,6 @@
     da = (nn(dv, down[...]) * bend).astype(bf16)
     da_out[...] = da
     dn = nn(da, up[...])
-    dn_out[...] = dn
     dx_out[...] = (dn * vecs[0:1]).astype(bf16)
 
     @pl.when(pl.program_id(0) == 0)
@@ -366,6 +619,10 @@
     sums[4:5, :CI] += row_sum(dy.astype(f32))
     sums[5:6, :LANES] += loss
     hidden_sums[0:1, :] += row_sum(da.astype(f32))
+
+    @pl.when(pl.program_id(0) == pl.num_programs(0) - 1)
+    def _():
+        copies[...] = jnp.broadcast_to(sums[...][None], copies.shape)
 
 
 def coarse_weights_kernel(da, normal, dv, gated, du, top, dy, skip, up_out, down_out, ups_out, head_out):
@@ -387,20 +644,23 @@
     return inverse, first, second
 
 
-def coarse_conv_back_kernel(
-    rows, cols, got, back, vecs, border, dx, masked, mask, taps, dtop, dcells, taps_out, source, slope
-):
+def coarse_conv_back_kernel(rows, cols, *refs):
+    got, back, vecs = refs[:3]
+    border, dx, masked, mask = refs[3:8], refs[8:13], refs[13:18], refs[18:23]
+    taps, dtop, dcells, taps_out, source, slope, held, ocean = refs[23:]
+
+    @pl.when(pl.program_id(0) == 0)
+    def _():
+        lay_border(rows, cols, source, held, *mask)
+        at = WIDTH2 % LANES
+        ocean[...] = jnp.broadcast_to(source[:, at : at + 1], ocean.shape)
+
     inverse, first, second = backward_rows(got, back, vecs[0:1])
-    source[...] = border[...].astype(f32)
-    slope[...] = (
-        (
-            dx[...].astype(f32) * inverse
-            + jnp.where(mask[...] > 0.0, first, 0.0)
-            + masked[...].astype(f32) * second
-        )
-        .astype(bf16)
-        .astype(f32)
-    )
+    lay_border(rows, cols, source, held, *dx)
+    slope[...] = source[...] * inverse + ocean[...] * first
+    lay_border(rows, cols, source, held, *masked)
+    slope[...] = (slope[...] + source[...] * second).astype(bf16).astype(f32)
+    lay_border(rows, cols, source, held, *border)
 
     def emit(place, total, carry):
         dcells[place, :] = (dtop[place, :] + total.reshape(64, LANES)).astype(bf16)
@@ -426,7 +686,7 @@
 
 
 def fine_back_kernel(
-    cols, got, dcells, downs, ds, vecs, conv, slope, up, down, dv_out, da_out, dn_out, normal_out, sums, hidden_sums, coarse_sums
+    cols, got, dcells, downs, ds, vecs, conv, slope, up, down, dv_out, da_out, dn_out, normal_out, sums, hidden_sums, coarse_sums, copies
 ):
     mean, inverse, _, _ = norm_rows(got)
     dlow = dcells[...]
@@ -454,6 +714,10 @@
         sums[0:1, :] += row_sum(dn)
         sums[1:2, :] += row_sum(dn * centred)
 
+    @pl.when(pl.program_id(0) == pl.num_programs(0) - 1)
+    def _():
+        copies[...] = jnp.broadcast_to(sums[...][None], copies.shape)
+
 
 def fine_weights_kernel(da, normal, dv, gated, dcells, patches, up_out, down_out, downs_out):
     up_out[...] = tn(da[...], normal[...])
@@ -462,8 +726,8 @@
 
 
 def stem_back_kernel(
-    rows, cols, got, back, vecs, dn, conv, depth, dv, first_cells, second_cells, third_cells, near, stem, pick,
-    stem_out, taps_out, turned, acc, tap_acc, stem3,
+    rows, cols, got, back, vecs, dn, conv, depth, dv, first_cells, second_cells, third_cells, near, stem, pick, sums,
+    tail, turned, acc, tap_acc, stem3, lines, held,
 ):
     inverse, first, second = backward_rows(got, back, vecs[0:1])
     scale = inverse * vecs[0:1]
@@ -482,8 +746,7 @@
     lane = lax.broadcasted_iota(jnp.int32, acc.shape, 1)
     acc[...] = jnp.where(lane < CIN, acc[...], 0.0)
     tap_acc[...] = jnp.zeros(tap_acc.shape, f32)
-    wide = jnp.concatenate([stem[...].astype(f32), jnp.zeros((C1, C1 - CI), f32)], axis=1)
-    stem3[...] = wide + pltpu.roll(wide, CIN, 1) + pltpu.roll(wide, 2 * CIN, 1)
+    stem3[...] = triple_stem(stem[...])
 
     def group(index, cells, row):
         place = pl.ds(pl.multiple_of(row * amount, amount), rows * amount)
@@ -504,12 +767,17 @@
 
     lax.fori_loop(0, 3, triple, 0)
     full = acc[...]
-    stem_out[...] = (
+    acc[:, :LANES] = (
         full[:, :LANES]
         + pltpu.roll(full, C1 - CIN, 1)[:, :LANES]
         + pltpu.roll(full, C1 - 2 * CIN, 1)[:, :LANES]
     )
-    taps_out[...] = tap_acc[...]
+    lines[...] = jnp.zeros(lines.shape, f32)
+    write_matrix(lines, 0, STEM, held, acc)
+    write_short(lines, offsets()[TAPS1], WIDTH, TAPS, lambda r: tap_acc[r : r + 1, :])
+    write_row(lines, 0, GAIN1, norm_row(got, sums))
+    write_row(lines, 0, SHIFT1, row_of(sums, 0))
+    tail[...] = lines[...].reshape(tail.shape)
 
 
 def period(length):
@@ -661,14 +929,22 @@
 TAPS2, GAIN2, SHIFT2, UP2, UPB2, DOWN2, DOWNB2, UPS, UPSB, HEAD, HEADB = range(10, 21)
 
 
-def collect(devices, shard_len, me, blocks, lines, low, high):
+def planes_of(devices, shard_len, low, high, plane_size):
+    firsts, tall = shard_places(devices, shard_len)
+    found = {e // plane_size for e in range(devices) if firsts[e] < high and firsts[e] + tall > low}
+    return sorted(found)
+
+
+def collect(devices, shard_len, plane_size, place, parts, lines, low, high):
     firsts, tall = shard_places(devices, shard_len)
     started = False
     for e in range(devices):
         end = firsts[e + 1] + 16 if e + 1 < devices else firsts[e] + tall
         if end <= low or firsts[e] >= high:
             continue
-        seat = seat_of(me, e, devices)
+        plane, blocks = next((p.index(e // plane_size), b) for p, b in parts if e // plane_size in p)
+        planes = next(len(p) for p, b in parts if e // plane_size in p)
+        seat = seat_of(place, e % plane_size, plane_size) * planes + plane
         first = firsts[e] - low
         skip = max(0, -first)
         take = min(tall, high - firsts[e])
@@ -721,6 +997,8 @@
     rows = shapes_of()[piece][0]
     read_short(lines, offsets()[piece] - shift, rows, TAPS, put)
     held[rows:tall, :] = jnp.zeros((tall - rows, LANES), f32)
+    if out is None:
+        return
     across = held[:tall, :].T
     for t in range(TAPS):
         out[t] = jnp.broadcast_to(across[t : t + 1, :], (8, tall))
@@ -738,12 +1016,12 @@
     return -(-(offsets()[HEADB] + CIN) // 2048) * 16
 
 
-def first_params_kernel(devices, shard_len, me, blocks, perm, stem, taps1, near1, vecs1, up1, bias1, down1, downs, downs_four, down_rows, lines, held):
-    collect(devices, shard_len, me[0], blocks, lines, 0, first_end())
+def first_params_kernel(devices, shard_len, plane_size, planes, place, blocks, perm, stem, near1, vecs1, up1, bias1, down1, downs, downs_four, down_rows, lines, held):
+    collect(devices, shard_len, plane_size, place[0], [(planes, blocks)], lines, 0, first_end())
     vecs1[...] = jnp.zeros(vecs1.shape, f32)
     down_rows[...] = jnp.zeros(down_rows.shape, f32)
     bias1[...] = jnp.zeros(bias1.shape, f32)
-    read_taps(lines, 0, TAPS1, held, taps1, C1)
+    read_taps(lines, 0, TAPS1, held, None, C1)
     near1[...] = held[:C1, :].astype(bf16)
     read_matrix(lines, 0, STEM, held, stem)
     read_row(lines, 0, GAIN1, vecs1, 0)
@@ -758,9 +1036,10 @@
         downs_four[k] = nt(downs[...], perm[k]).astype(bf16)
 
 
-def rest_params_kernel(devices, shard_len, me, blocks, taps2, vecs2, up2, bias2, down2, ups_four, vecs1, head, last, lines, held):
+def rest_params_kernel(devices, shard_len, plane_size, planes, others, place, blocks, more, taps2, vecs2, up2, bias2, down2, ups_four, vecs1, head, last, lines, held):
     shift = rest_start() * LANES
-    collect(devices, shard_len, me[0], blocks, lines, rest_start(), rest_end())
+    parts = [(planes, blocks), (others, more)]
+    collect(devices, shard_len, plane_size, place[0], parts, lines, rest_start(), rest_end())
     for out in (vecs1, vecs2, bias2, last):
         out[...] = jnp.zeros(out.shape, f32)
     read_taps(lines, shift, TAPS2, held, taps2, C2)
@@ -831,35 +1110,57 @@
     return get
 
 
-def flatten_kernel(
-    devices, shard_len, me, got1, got2, g_stem, g_taps1, sums1, hidden1, g_up1, g_down1, g_downs, sums_low, g_taps2,
-    sums2, hidden2, g_up2, g_down2, g_ups, g_head, keep, send, lines, held,
+def scatter_out(devices, shard_len, plane_size, planes, place, lines, low, keep, send):
+    firsts, tall = shard_places(devices, shard_len)
+    half = plane_size // 2
+    for k, plane in enumerate(planes):
+        for r in range(plane_size):
+            first = firsts[plane * plane_size + r] - low
+            start, end = max(first, 0), min(first + tall, lines.shape[0])
+            seat = seat_of(place, r, plane_size)
+
+            def put(out, index, kind):
+                if end <= start:
+                    out[index] = jnp.zeros((tall, LANES), kind)
+                    return
+                if start > first:
+                    out[index, : start - first] = jnp.zeros((start - first, LANES), kind)
+                out[index, start - first : end - first] = lines[start:end, :].astype(kind)
+                if end < first + tall:
+                    out[index, end - first :] = jnp.zeros((first + tall - end, LANES), kind)
+
+            @pl.when(seat < half)
+            def _():
+                put(keep, seat * len(planes) + k, f32)
+
+            @pl.when(seat >= half)
+            def _():
+                put(send, (seat - half) * len(planes) + k, bf16)
+
+
+def span(first, last):
+    end = offsets()[last] + math.prod(shapes_of()[last])
+    return offsets()[first] // 2048 * 16, -(-end // 2048) * 16
+
+
+def clear_ends(lines, low, first, last):
+    start = offsets()[first] // LANES - low + 1
+    lines[:start, :] = jnp.zeros((start, LANES), f32)
+    end = -(-(offsets()[last] + math.prod(shapes_of()[last])) // LANES) - low
+    if end < lines.shape[0]:
+        lines[end:, :] = jnp.zeros((lines.shape[0] - end, LANES), f32)
+
+
+def late_flat_kernel(
+    devices, shard_len, plane_size, planes, place, sums2, hidden2, g_up2, g_down2, g_ups, g_head, keep, send, lines, held
 ):
-    def matrix(piece, source):
-        write_matrix(lines, 0, piece, held, source)
-
-    def row(piece, get):
-        write_row(lines, 0, piece, get)
-
-    matrix(STEM, g_stem)
-    write_short(lines, offsets()[TAPS1], WIDTH, TAPS, lambda r: g_taps1[r : r + 1, :])
-    row(GAIN1, norm_row(got1, sums1))
-    row(SHIFT1, row_of(sums1, 0))
-    matrix(UP1, g_up1)
-    row(UPB1, row_of(hidden1, 0))
-    matrix(DOWN1, g_down1)
-    row(DOWNB1, row_of(sums1, 2))
-    matrix(DOWNS, g_downs)
-    row(DOWNSB, row_of(sums_low, 0))
-    across = jnp.concatenate([g_taps2[...], jnp.zeros((LANES - g_taps2.shape[0], C2), f32)], axis=0).T
-    held[:C2, :] = across
-    write_short(lines, offsets()[TAPS2], WIDTH2, TAPS, lambda r: held[r : r + 1, :])
-    row(GAIN2, norm_row(got2, sums2))
-    row(SHIFT2, row_of(sums2, 0))
-    matrix(UP2, g_up2)
-    row(UPB2, row_of(hidden2, 0))
-    matrix(DOWN2, g_down2)
-    row(DOWNB2, row_of(sums2, 2))
+    low, _ = span(UP2, HEADB)
+    shift = low * LANES
+    clear_ends(lines, low, UP2, HEADB)
+    write_matrix(lines, shift, UP2, held, g_up2)
+    write_row(lines, shift, UPB2, row_of(hidden2, 0))
+    write_matrix(lines, shift, DOWN2, held, g_down2)
+    write_row(lines, shift, DOWNB2, row_of(sums2, 2))
     rows, length = shapes_of()[UPS]
     tiles = C2 // LANES
     tall = WIDTH + 2 * FRONT
@@ -871,29 +1172,35 @@
             held[at + FRONT + WIDTH : at + tall, :] = jnp.zeros((FRONT, LANES), f32)
 
     def get(first, stride, count, tile):
-        place = ((first % 4) * tiles + tile) * tall + FRONT + first // 4
-        return held[pl.ds(place, count, stride=stride // 4), :]
-
-    write_rows(lines, offsets()[UPS], rows, length, get)
-    row(UPSB, row_of(sums2, 3))
-    matrix(HEAD, g_head)
-    row(HEADB, row_of(sums2, 4))
-    end = offsets()[HEADB] + CIN
-    last = -(-end // LANES)
-    lines[last:, :] = jnp.zeros((lines.shape[0] - last, LANES), f32)
-
-    firsts, tall = shard_places(devices, shard_len)
-    half = devices // 2
-    for e in range(devices):
-        seat = seat_of(me[0], e, devices)
-
-        @pl.when(seat < half)
-        def _():
-            keep[seat] = lines[firsts[e] : firsts[e] + tall, :]
-
-        @pl.when(seat >= half)
-        def _():
-            send[seat - half] = lines[firsts[e] : firsts[e] + tall, :].astype(bf16)
+        at = ((first % 4) * tiles + tile) * tall + FRONT + first // 4
+        return held[pl.ds(at, count, stride=stride // 4), :]
+
+    write_rows(lines, offsets()[UPS] - shift, rows, length, get)
+    write_row(lines, shift, UPSB, row_of(sums2, 3))
+    write_matrix(lines, shift, HEAD, held, g_head)
+    write_row(lines, shift, HEADB, row_of(sums2, 4))
+    scatter_out(devices, shard_len, plane_size, planes, place[0], lines, low, keep, send)
+
+
+def early_flat_kernel(
+    devices, shard_len, plane_size, planes, place, got2, sums1, hidden1, g_up1, g_down1, g_downs, sums_low, g_taps2, sums2,
+    keep, send, lines, held,
+):
+    low, _ = span(UP1, SHIFT2)
+    shift = low * LANES
+    clear_ends(lines, low, UP1, SHIFT2)
+    write_matrix(lines, shift, UP1, held, g_up1)
+    write_row(lines, shift, UPB1, row_of(hidden1, 0))
+    write_matrix(lines, shift, DOWN1, held, g_down1)
+    write_row(lines, shift, DOWNB1, row_of(sums1, 2))
+    write_matrix(lines, shift, DOWNS, held, g_downs)
+    write_row(lines, shift, DOWNSB, row_of(sums_low, 0))
+    across = jnp.concatenate([g_taps2[...], jnp.zeros((LANES - g_taps2.shape[0], C2), f32)], axis=0).T
+    held[:C2, :] = across
+    write_short(lines, offsets()[TAPS2] - shift, WIDTH2, TAPS, lambda r: held[r : r + 1, :])
+    write_row(lines, shift, GAIN2, norm_row(got2, sums2))
+    write_row(lines, shift, SHIFT2, row_of(sums2, 0))
+    scatter_out(devices, shard_len, plane_size, planes, place[0], lines, low, keep, send)
 
 
 def group_taps():
@@ -909,41 +1216,96 @@
 def body(fields, targets, ocean_depth, thickness_class, params, moment1, moment2):
     shard_len = params.shape[0]
     devices = lax.axis_size(AXES)
+    plane_size = 2 * lax.axis_size("lvl")
     me = lax.axis_index(AXES)
     _, tall = shard_places(devices, shard_len)
     at = (me * (shard_len % 2048)) % 2048
     block = lax.dynamic_update_slice(jnp.zeros((tall * LANES,), bf16), params.astype(bf16), (at,))
-    blocks = gather_blocks(block.reshape(tall, LANES))
-    me_row = jnp.broadcast_to(me, (1,)).astype(jnp.int32)
-
-    inputs = to_cells(lax.all_to_all(fields, "lvl", split_axis=3, concat_axis=0, tiled=True))
-    goal = to_cells(lax.all_to_all(targets, "lvl", split_axis=3, concat_axis=0, tiled=True))
-    rows, cols, _, _ = inputs.shape
-    batch = fields.shape[1]
+    near_planes = planes_of(devices, shard_len, 0, first_end(), plane_size)
+    far_planes = [p for p in range(devices // plane_size) if p not in near_planes]
+    plane_steps, pick_planes = gather_steps(near_planes, far_planes)
+    blocks = block.reshape(1, tall, LANES)
+    place_row = jnp.broadcast_to(me % plane_size, (1,)).astype(jnp.int32)
+
+    smem = pl.BlockSpec(memory_space=pltpu.SMEM)
+    vmem = pl.BlockSpec(memory_space=pltpu.VMEM)
+    parts = lax.axis_size("lvl")
+    chans, batch, all_rows, all_cols = fields.shape
+    bands = BLOCKS // batch
+    rows, cols = all_rows // bands, all_cols // parts
     half_rows, half_cols = rows // 2, cols // 2
     cells, low_cells = rows * cols * 8, half_rows * half_cols * 8
-    wide = with_halo(inputs)
-    wide_rows, wide_cols = rows + 2 * REACH, cols + 2 * REACH
-    border_cells = wide_rows * wide_cols * 8
+    wide_cols = cols + 2 * REACH
     low_border = (half_rows + 2 * REACH) * (half_cols + 2 * REACH) * 8
-    fields_in = fill(wide, wide_rows, wide_cols, 8, CI).reshape(border_cells, CI)
-    later = jnp.pad(wide, ((0, 2), (0, 0), (0, 0), (0, 0)))
-
-    def three(parts):
-        joined = jnp.concatenate(parts, axis=3)
-        return fill(joined, wide_rows, cols, 8, C1).reshape(wide_rows * cols * 8, C1)
-
-    first_cells = three([wide[:, k : k + cols] for k in range(3)])
-    second_cells = three([wide[:, k : k + cols] for k in range(3, 6)])
-    third_cells = three([later[k : k + wide_rows, 6 : 6 + cols] for k in range(3)])
-    goal = fill(goal, rows, cols, 8, CI).reshape(cells, CI)
+
+    def packed(values, reach):
+        width = cols + 2 * reach
+        lanes = chans * BLOCKS
+        copies = call(
+            lambda *refs: pack_kernel(parts, cols, reach, *refs),
+            [((parts, rows * width, lanes), bf16)],
+            scratch=[
+                pltpu.VMEM((-(-all_cols // LANES), chans * batch * all_rows, LANES), f32),
+                pltpu.VMEM((16 + -(-all_cols // LANES) * LANES, lanes), f32),
+                pltpu.VMEM((parts, rows * width, lanes), f32),
+            ],
+            micros=3,
+            name="pack",
+        )(values.reshape(-1, all_cols))[0]
+        return copies
+
+    def given(copies):
+        return lax.all_to_all(copies, "lvl", 0, 0, tiled=True)
+
+    field_copies = packed(fields, REACH)
+    goal_copies = packed(targets, 0)
+    for step in plane_steps[:-1]:
+        blocks = step(blocks)
+    goal_copies, blocks = tie(goal_copies, blocks)
+    blocks = plane_steps[-1](blocks)
+    send_room = 2 * REACH * -(-wide_cols // 8) * 8
+    field_cells, lower, upper = call(
+        lambda *refs: fields_kernel(parts, rows, cols, *refs),
+        [((rows * wide_cols * 8, LANES), f32), ((send_room, LANES), bf16), ((send_room, LANES), bf16)],
+        scratch=[pltpu.VMEM((send_room, LANES), f32)],
+        micros=4,
+        name="fields",
+    )(given(field_copies))
+    (field_cells, lower, upper), blocks = tie((field_cells, lower, upper), blocks)
+    above, below = lines_out(lower, upper)
+    near_blocks, far_blocks = pick_planes(blocks)
+    near_steps = within_steps()
+    state = near_steps[0](near_blocks)
+    (field_cells, above, below), state = tie((field_cells, above, below), state)
+    state = near_steps[1](state)
+    shifted_rows = (rows + 2 * REACH) * cols * 8
+    first_cells, second_cells, third_cells = call(
+        lambda *refs: shift_kernel(rows, cols, *refs),
+        [((shifted_rows, C1), bf16)] * 3,
+        scratch=[
+            pltpu.VMEM((2 * REACH * wide_cols * 8, LANES), f32),
+            pltpu.VMEM(((rows + 2 * REACH + 2) * wide_cols * 8, LANES), f32),
+            pltpu.VMEM(((rows + 2 * REACH + 2) * wide_cols * 8, LANES), f32),
+        ],
+        micros=6,
+        name="shift",
+    )(field_cells, above, below)
+    (first_cells, second_cells, third_cells), state = tie((first_cells, second_cells, third_cells), state)
+    blocks = near_steps[2](state)
+    goal = call(
+        lambda *refs: targets_kernel(parts, *refs),
+        [((cells, LANES), bf16)],
+        scratch=[pltpu.VMEM((cells, LANES), f32)],
+        micros=4,
+        name="targets",
+    )(given(goal_copies))[0]
+    more_blocks = far_blocks
+    for step in within_steps():
+        more_blocks = step(more_blocks)
 
     deep = depth_cells(ocean_depth, batch)
     depth_rows = jnp.broadcast_to(deep.astype(f32)[..., None], deep.shape + (LANES,)).reshape(cells, LANES)
     low = jnp.max(deep.reshape(half_rows, 2, half_cols, 2, 8), axis=(1, 3))
-    low_mask = (low > 0).astype(bf16)[..., None]
-    low_wide = with_halo(jnp.broadcast_to(low_mask, low_mask.shape[:3] + (LANES,)))
-    low_wide = low_wide.reshape(low_border, LANES)
     low_rows = jnp.broadcast_to(low.astype(f32)[..., None], low.shape + (LANES,)).reshape(low_cells, LANES)
     channel = jnp.arange(CI, dtype=jnp.int32)
     level = jnp.where(channel < 4 * LEVELS, channel // 4, 0)
@@ -971,47 +1333,38 @@
     third_at = jnp.arange(C1, dtype=jnp.int32) // CIN
     wanted = jnp.array([line + [-1] for line in table], dtype=jnp.int32)[:, third_at]
     pick = (wanted[:, :, None] == jnp.arange(LANES, dtype=jnp.int32)[None, None, :]).astype(bf16)
-    smem = pl.BlockSpec(memory_space=pltpu.SMEM)
-    vmem = pl.BlockSpec(memory_space=pltpu.VMEM)
     held_room = pltpu.VMEM((4 * H2, LANES), f32)
-    stem_in, taps_in1, near1, vecs1, up_in1, bias_in1, down_in1, downs_in, downs_four, down_rows = call(
-        lambda *refs: first_params_kernel(devices, shard_len, *refs),
+    stem_in, near1, vecs1, up_in1, bias_in1, down_in1, downs_in, downs_four, down_rows = call(
+        lambda *refs: first_params_kernel(devices, shard_len, plane_size, near_planes, *refs),
         [
-            ((C1, CI), bf16), ((TAPS, 8, C1), f32), ((C1, LANES), bf16), ((8, C1), f32), ((H1, C1), bf16),
+            ((C1, CI), bf16), ((C1, LANES), bf16), ((8, C1), f32), ((H1, C1), bf16),
             ((1, H1), f32), ((C1, H1), bf16), ((C2, H1), bf16), ((4, C2, C1), bf16), ((8, C2), f32),
         ],
         ins=[smem, vmem, vmem],
         scratch=[pltpu.VMEM((first_end(), LANES), f32), held_room],
+        micros=8,
         name="first_params",
-    )(me_row, blocks, perm)
+    )(place_row, blocks, perm)
     taps_in2, vecs2, up_in2, bias_in2, down_in2, ups_four, fine_rows, head_in, last_rows = call(
-        lambda *refs: rest_params_kernel(devices, shard_len, *refs),
+        lambda *refs: rest_params_kernel(devices, shard_len, plane_size, near_planes, far_planes, *refs),
         [
             ((TAPS, 8, C2), f32), ((8, C2), f32), ((H2, C2), bf16), ((1, H2), f32), ((C2, H2), bf16),
             ((4, C1, C2), bf16), ((8, C1), f32), ((CI, C1), bf16), ((8, CI), f32),
         ],
-        ins=[smem, vmem],
+        ins=[smem, vmem, vmem],
         scratch=[pltpu.VMEM((rest_end() - rest_start(), LANES), f32), held_room],
+        micros=13,
         name="rest_params",
-    )(me_row, blocks)
+    )(place_row, blocks, more_blocks)
 
     hzero, conv1, stats1 = call(
         lambda *refs: stem_kernel(rows, cols, *refs),
-        [((cells, C1), bf16), ((cells, C1), f32), ((8, C1), f32)],
-        grid=(C1 // LANES,),
-        ins=[
-            whole(border_cells, CI),
-            pl.BlockSpec((LANES, CI), lambda i: (i, 0)),
-            TAP_TILE,
-            whole(cells, LANES),
-            lane_tile(8),
-        ],
-        out_specs=[lane_tile(cells), lane_tile(cells), lane_tile(8)],
-        scratch=[pltpu.VMEM((border_cells, LANES), f32)],
-        flops=cells * C1 * TAPS * 100,
+        [((cells, C1), bf16), ((cells, C1), f32), ((devices, 8, C1), f32)],
+        scratch=[pltpu.VMEM((GROUPS * C1, C1), bf16), pltpu.VMEM((C1, C1), f32), pltpu.VMEM((8, C1), f32)],
+        micros=16,
         name="stem_conv",
-    )(fields_in, stem_in, taps_in1, depth_rows, counts1)
-    got1 = spread(stats1)
+    )(first_cells, second_cells, third_cells, near1, stem_in, pick, depth_rows, counts1)
+    got1 = swap(stats1)
     chunk, low_chunk = 2 * cols * 8, half_cols * 8
     hone, gated1, slope1, patches, coarse = call(
         lambda *refs: fine_kernel(cols, *refs),
@@ -1031,32 +1384,56 @@
             band(chunk, C1), band(chunk, H1), band(chunk, H1), band(low_chunk, H1), band(low_chunk, C2),
         ],
         scratch=[pltpu.VMEM((chunk, C1), f32)],
-        flops=cells * C1 * H1 * 8,
+        micros=15,
         name="fine_forward",
     )(got1, conv1, hzero, vecs1, up_in1, bias_in1, down_in1, perm, downs_in, down_rows)
 
-    border2 = with_halo(coarse.reshape(half_rows, half_cols, 8, C2)).reshape(low_border, C2)
+    edge = edge_lines(half_cols)
+    side = half_rows * REACH * 8
+
+    def halo(*arrays):
+        count = len(arrays)
+        joined = [columns_out(values, half_rows, half_cols) for values in arrays]
+        lower, upper = call(
+            lambda *refs: edge_kernel(half_rows, half_cols, count, *refs),
+            [((count * edge, C2), bf16)] * 2,
+            scratch=[pltpu.VMEM((low_cells + 2 * side, LANES), f32), pltpu.VMEM((edge, LANES), f32)],
+            micros=3,
+            name="edge",
+        )(*[ref for values, sides in zip(arrays, joined) for ref in (values, *sides)])
+        above, below = lines_out(lower, upper)
+        return [
+            [values, *sides, above[k * edge : (k + 1) * edge], below[k * edge : (k + 1) * edge]]
+            for k, (values, sides) in enumerate(zip(arrays, joined))
+        ]
+
+    def border_tiles(tile):
+        return [tile(low_cells), tile(side), tile(side), tile(edge), tile(edge)]
+
+    def edge_tile(rows):
+        return pl.BlockSpec((rows, LANES), lambda i: (0, WIDTH2 // LANES))
+
+    (border2,) = halo(coarse)
     conv2, masked2, stats2 = call(
         lambda *refs: coarse_conv_kernel(half_rows, half_cols, *refs),
-        [((low_cells, C2), f32), ((low_cells, C2), bf16), ((8, C2), f32)],
+        [((low_cells, C2), f32), ((low_cells, C2), bf16), ((devices, 8, C2), f32)],
         grid=(C2 // LANES,),
-        ins=[lane_tile(low_border), TAP_TILE, whole(low_cells, LANES), lane_tile(8)],
-        out_specs=[lane_tile(low_cells), lane_tile(low_cells), lane_tile(8)],
-        scratch=[pltpu.VMEM((low_border, LANES), f32)],
-        flops=low_cells * C2 * TAPS * 100,
+        ins=border_tiles(lane_tile) + [TAP_TILE, whole(low_cells, LANES), lane_tile(8)],
+        out_specs=[lane_tile(low_cells), lane_tile(low_cells), stats_tile(devices)],
+        scratch=[pltpu.VMEM((low_border, LANES), f32), pltpu.VMEM((edge, LANES), f32)],
+        micros=11,
         name="coarse_conv",
-    )(border2, taps_in2, low_rows, counts2)
-    got2 = spread(stats2)
-    masked_wide = with_halo(masked2.reshape(half_rows, half_cols, 8, C2)).reshape(low_border, C2)
+    )(*border2, taps_in2, low_rows, counts2)
+    got2 = swap(stats2)
     (
-        skip, top, dy, ds, du, dtop, dv2, gated2, da2, normal2, dn2, dx2, sums2, hidden2,
+        skip, top, dy, ds, du, dtop, dv2, gated2, da2, normal2, dx2, sums2, hidden2, copies2,
     ) = call(
         lambda *refs: middle_kernel(cols, *refs),
         [
             ((cells, C1), bf16), ((low_cells, C2), bf16), ((cells, CI), bf16), ((cells, C1), f32),
             ((4, low_cells, C1), bf16), ((low_cells, C2), f32), ((low_cells, C2), bf16), ((low_cells, H2), bf16),
-            ((low_cells, H2), bf16), ((low_cells, C2), bf16), ((low_cells, C2), f32), ((low_cells, C2), bf16),
-            ((8, C2), f32), ((8, H2), f32),
+            ((low_cells, H2), bf16), ((low_cells, C2), bf16), ((low_cells, C2), bf16),
+            ((8, C2), f32), ((8, H2), f32), ((devices, 8, C2), f32),
         ],
         grid=(half_rows,),
         ins=[
@@ -1067,44 +1444,62 @@
         out_specs=[
             band(chunk, C1), band(low_chunk, C2), band(chunk, CI), band(chunk, C1),
             pl.BlockSpec((4, low_chunk, C1), lambda i: (0, i, 0)), band(low_chunk, C2), band(low_chunk, C2),
-            band(low_chunk, H2), band(low_chunk, H2), band(low_chunk, C2), band(low_chunk, C2), band(low_chunk, C2),
-            whole(8, C2), whole(8, H2),
+            band(low_chunk, H2), band(low_chunk, H2), band(low_chunk, C2), band(low_chunk, C2),
+            whole(8, C2), whole(8, H2), whole(devices, 8, C2),
         ],
-        flops=low_cells * C2 * H2 * 16,
+        micros=20,
         name="middle",
     )(
         got2, conv2, coarse, vecs2, up_in2, bias_in2, down_in2, ups_four, fine_rows, head_in, last_rows, tables, hone, goal,
         depth_rows,
     )
-    back2 = spread(sums2)
-    dx_wide = with_halo(dx2.reshape(half_rows, half_cols, 8, C2)).reshape(low_border, C2)
+    back2 = swap(copies2)
+    dx_halo, masked_halo = halo(dx2, masked2)
+    da2, dx_halo[1] = tie(da2, dx_halo[1])
     g_up2, g_down2, g_ups, g_head = call(
         coarse_weights_kernel,
         [((H2, C2), f32), ((C2, H2), f32), ((4, C1, C2), f32), ((CI, C1), f32)],
-        flops=low_cells * C2 * H2 * 8,
+        micros=10,
         name="coarse_weights",
     )(da2, normal2, dv2, gated2, du, top, dy, skip)
+    late_planes = planes_of(devices, shard_len, *span(UP2, HEADB), plane_size)
+    half_seats = plane_size // 2
+    late_keep, late_send = call(
+        lambda *refs: late_flat_kernel(devices, shard_len, plane_size, late_planes, *refs),
+        [((half_seats * len(late_planes), tall, LANES), kind) for kind in (f32, bf16)],
+        ins=[smem] + [vmem] * 6,
+        scratch=[pltpu.VMEM((span(UP2, HEADB)[1] - span(UP2, HEADB)[0], LANES), f32), held_room],
+        micros=9,
+        name="late_flat",
+    )(place_row, sums2, hidden2, g_up2, g_down2, g_ups, g_head)
     dcells, g_taps2 = call(
         lambda *refs: coarse_conv_back_kernel(half_rows, half_cols, *refs),
         [((low_cells, C2), bf16), ((56, C2), f32)],
         grid=(C2 // LANES,),
-        ins=[
-            pl.BlockSpec((devices, 8, LANES), lambda i: (0, 0, i)),
-            pl.BlockSpec((devices, 8, LANES), lambda i: (0, 0, i)),
-            lane_tile(8), lane_tile(low_border), lane_tile(low_border), lane_tile(low_border),
-            whole(low_border, LANES), TAP_TILE, lane_tile(low_cells),
+        ins=[stats_tile(devices), stats_tile(devices), lane_tile(8)]
+        + border_tiles(lane_tile) * 3
+        + border_tiles(edge_tile)
+        + [TAP_TILE, lane_tile(low_cells)],
+        out_specs=[lane_tile(low_cells), lane_tile(56)],
+        scratch=[
+            pltpu.VMEM((low_border, LANES), f32),
+            pltpu.VMEM((low_border, LANES), f32),
+            pltpu.VMEM((edge, LANES), f32),
+            pltpu.VMEM((low_border, LANES), f32),
         ],
-        out_specs=[lane_tile(low_cells), lane_tile(56)],
-        scratch=[pltpu.VMEM((low_border, LANES), f32), pltpu.VMEM((low_border, LANES), f32)],
-        flops=low_cells * C2 * TAPS * 200,
+        micros=25,
         name="coarse_conv_back",
-    )(got2, back2, vecs2, border2, dx_wide, masked_wide, low_wide, taps_in2, dtop)
-
-    dv1, da1, dn1, normal1, sums1, hidden1, sums_low = call(
+    )(got2, back2, vecs2, *border2, *dx_halo, *masked_halo, *masked_halo, taps_in2, dtop)
+
+    state, late_steps = scatter_steps(late_keep, late_send, late_planes)
+    dcells, state = tie(dcells, late_steps[0](state))
+    for step in late_steps[1:-3]:
+        state = step(state)
+    dv1, da1, dn1, normal1, sums1, hidden1, sums_low, copies1 = call(
         lambda *refs: fine_back_kernel(cols, *refs),
         [
             ((cells, C1), bf16), ((cells, H1), bf16), ((cells, C1), f32), ((cells, C1), bf16),
-            ((8, C1), f32), ((8, H1), f32), ((8, C2), f32),
+            ((8, C1), f32), ((8, H1), f32), ((8, C2), f32), ((devices, 8, C1), f32),
         ],
         grid=(half_rows,),
         ins=[
@@ -1113,47 +1508,65 @@
         ],
         out_specs=[
             band(chunk, C1), band(chunk, H1), band(chunk, C1), band(chunk, C1), whole(8, C1), whole(8, H1), whole(8, C2),
+            whole(devices, 8, C1),
         ],
-        flops=cells * C1 * H1 * 8,
+        micros=13,
         name="fine_backward",
     )(got1, dcells, downs_four, ds, vecs1, conv1, slope1, up_in1, down_in1)
-    back1 = spread(sums1)
+    da1, state = tie(da1, late_steps[-3](state))
+    back1 = swap(copies1)
     g_up1, g_down1, g_downs = call(
         fine_weights_kernel,
         [((H1, C1), f32), ((C1, H1), f32), ((C2, H1), f32)],
-        flops=cells * C1 * H1 * 6,
+        micros=11,
         name="fine_weights",
     )(da1, normal1, dv1, gated1, dcells, patches)
-    g_stem, g_taps1 = call(
+    early_planes = planes_of(devices, shard_len, *span(UP1, SHIFT2), plane_size)
+    early_keep, early_send = call(
+        lambda *refs: early_flat_kernel(devices, shard_len, plane_size, early_planes, *refs),
+        [((half_seats * len(early_planes), tall, LANES), kind) for kind in (f32, bf16)],
+        ins=[smem] + [vmem] * 9,
+        scratch=[pltpu.VMEM((span(UP1, SHIFT2)[1] - span(UP1, SHIFT2)[0], LANES), f32), held_room],
+        micros=6,
+        name="early_flat",
+    )(place_row, got2, sums1, hidden1, g_up1, g_down1, g_downs, sums_low, g_taps2, sums2)
+    early_keep, state = tie(early_keep, late_steps[-2](state))
+    early_state, early_steps = scatter_steps(early_keep, early_send, early_planes)
+    early_state = early_steps[0](early_state)
+    dn1, early_state = tie(dn1, early_state)
+    late = late_steps[-1](state)
+    for step in early_steps[1:]:
+        early_state = step(early_state)
+    early = early_state
+    tail_lines = -(-span(STEM, SHIFT1)[1] // (8 * devices)) * 8
+    tail = call(
         lambda *refs: stem_back_kernel(rows, cols, *refs),
-        [((C1, LANES), f32), ((C1, LANES), f32)],
-        scratch=[pltpu.VMEM((C1, cells), bf16), pltpu.VMEM((C1, C1), f32), pltpu.VMEM((C1, LANES), f32), pltpu.VMEM((C1, C1), f32)],
-        flops=cells * C1 * C1 * GROUPS * 2,
+        [((devices, tail_lines, LANES), f32)],
+        scratch=[
+            pltpu.VMEM((C1, cells), bf16), pltpu.VMEM((C1, C1), f32), pltpu.VMEM((C1, LANES), f32), pltpu.VMEM((C1, C1), f32),
+            pltpu.VMEM((devices * tail_lines, LANES), f32), pltpu.VMEM((C1, LANES), f32),
+        ],
+        micros=26,
         name="stem_back",
     )(
-        got1, back1, vecs1, dn1, conv1, depth_rows, dv1, first_cells, second_cells, third_cells, near1, stem_in,
-        pick,
-    )
-
-    keep, send = call(
-        lambda *refs: flatten_kernel(devices, shard_len, *refs),
-        [((devices // 2, tall, LANES), f32), ((devices // 2, tall, LANES), bf16)],
-        ins=[smem] + [vmem] * 17,
-        scratch=[pltpu.VMEM((rest_end() + tall, LANES), f32), held_room],
-        name="flatten",
-    )(
-        me_row, got1, got2, g_stem, g_taps1, sums1, hidden1, g_up1, g_down1, g_downs, sums_low, g_taps2, sums2, hidden2,
-        g_up2, g_down2, g_ups, g_head,
-    )
-    mine = scatter_blocks(keep, send).reshape(-1)
-    mine = lax.dynamic_slice_in_dim(mine, at, shard_len)
+        got1, back1, vecs1, dn1, conv1, depth_rows, dv1, first_cells, second_cells, third_cells, near1, stem_in, pick, sums1,
+    )[0]
+
+    chunk_sum = jnp.sum(swap(tail), axis=0)
+    mine = lax.dynamic_slice_in_dim((late + early).reshape(-1), at, shard_len)
+    squares = jnp.sum(mine * mine) + jnp.sum(chunk_sum * chunk_sum)
     loss_part = jnp.sum(sums2[5, :LANES])
-    last = jnp.broadcast_to(
-        jnp.where(index8 == 0, loss_part, jnp.where(index8 == 1, jnp.sum(mine * mine), 0.0)), (8, LANES)
-    )
-    last = jnp.sum(spread(last), axis=0)
-    loss_total, norm = last[0, 0], jnp.sqrt(last[1, 0])
+    stats = jnp.where(index8 == 0, loss_part, jnp.where(index8 == 1, squares, 0.0))
+    last = jnp.concatenate([chunk_sum, jnp.broadcast_to(stats, (8, LANES))], axis=0)
+    last = swap(jnp.broadcast_to(last[None], (devices,) + last.shape))
+    tail_flat = last[:, :tail_lines].reshape(devices * tail_lines, LANES)
+    totals = jnp.sum(last[:, tail_lines:, 0], axis=0)
+    loss_total, norm = totals[0], jnp.sqrt(totals[1])
     count = jnp.sum(got1[:, 3, 0])
+    tail_flat = jnp.pad(tail_flat, ((0, tall), (0, 0)))
+    line = jnp.minimum(me * shard_len // 2048 * 16, devices * tail_lines)
+    mine_tail = lax.dynamic_slice_in_dim(tail_flat, line, tall).reshape(-1)
+    mine = mine + lax.dynamic_slice_in_dim(mine_tail, at, shard_len)
     clipped = mine * jnp.minimum(1.0, CLIP / norm)
     first = BETA_ONE * moment1 + (1.0 - BETA_ONE) * clipped
     second = BETA_TWO * moment2 + (1.0 - BETA_TWO) * clipped * clipped

time: 594 us -> 465 us (0.78)
  waiting for transfers between devices: 138 us -> 67 us
  Pallas kernels: 192 us -> 144 us
  other arithmetic: 51.2 us -> 30.9 us
  starting transfers between devices: 96.3 us -> 111 us
    ppermute x10 -> x22, waiting for transfers between devices: 97.6 us -> 33 us  [exchange(): return lax.ppermute(values, axis, [(i, i ^ step) for i in range(count)])]
    unnamed x66 -> x239, local copies, waits for them, and re-layouts: 29.2 us -> 81.7 us
    concatenate x12 -> x8, other arithmetic: 29.7 us -> 4.58 us  [the longest x2 2.43 us: join(): both = jnp.concatenate([left, right], axis=3)]
    concatenate x13 -> x2, local copies, waits for them, and re-layouts: 20.2 us -> 0.23 us  [the longest x1 0.16 us: rest(): both = jnp.concatenate([both, exchange(both, *bit)], axis=0)]
    ppermute x10 -> x22, starting transfers between devices: 15.5 us -> 32 us  [exchange(): return lax.ppermute(values, axis, [(i, i ^ step) for i in range(count)])]
    pallas_call x4 -> x12, Pallas kernels: 62.3 us -> 49.2 us  [the longest x1 20.6 us: body(): call(lambda *refs: stem_back_kernel(rows, cols, *refs), [((devices, tail_...]
    pallas_call x1, Pallas kernels: 25.4 us -> 12.5 us  [body(): call(lambda *refs: stem_kernel(rows, cols, *refs), [((cells, C1), bf16),...]
    slice x17 -> x6, local copies, waits for them, and re-layouts: 13.4 us -> 2.98 us  [the longest x3 2.34 us: columns_out(): split[:, :REACH].reshape(-1, cells.shape[-1])]
  transfers between devices with their start and end apart: 37 -> 48, of which waited for: 21 -> 16; matrix products, arithmetic and copies ran while one was open for 20% -> 8% of each run, Pallas kernels for 9% -> 31%
where the time goes in v3:
time: 465 us; the launch traced here: 457 us
  Pallas kernels  144 us (31%)
  starting transfers between devices  111 us (24%)
  local copies, waits for them, and re-layouts  98.2 us (21%)
  waiting for transfers between devices  67 us (14%)
  other arithmetic  30.9 us (7%)
  between operations  6.49 us (1%)
    unnamed x239, local copies, waits for them, and re-layouts  81.7 us
    ppermute x22, waiting for transfers between devices, exchange(): return lax.ppermute(values, axis, [(i, i ^ step) for i in range(count)])  33 us
    ppermute x22, starting transfers between devices, exchange(): return lax.ppermute(values, axis, [(i, i ^ step) for i in range(count)])  32 us
    all_to_all x6, starting transfers between devices, swap(): return lax.all_to_all(copies, AXES, 0, 0, tiled=True)  28.6 us
    pallas_call x1, Pallas kernels, body(): call(lambda *refs: coarse_conv_back_kernel(half_rows, half_cols, *refs),...  24.9 us
    pallas_call x1, Pallas kernels, body(): call(lambda *refs: stem_back_kernel(rows, cols, *refs), [((devices, tail_...  20.6 us
    pallas_call x1, Pallas kernels, body(): call(lambda *refs: middle_kernel(cols, *refs), [((cells, C1), bf16), ((lo...  16.4 us
    ppermute x6, starting transfers between devices, scatter_planes(): mine = mine + lax.ppermute(part, 'lat', pairs).astype(f32)  15.9 us
  transfers between devices with their start and end apart: 48, of which 16 were waited for; matrix products, arithmetic and copies ran while one was open for 8% of the time, Pallas kernels for 31%

profile of v3, /device:TPU:0, one launch (start us, length us, event | category | flops | bytes accessed | tf_op | source)
XLA Modules:
  0.0 457.5 jit_solution(15649805748152321236)
XLA Ops:
  3.7 4.2 all-to-all-start
  9.4 3.4 collective-permute-start
  23.2 2.1 fields.1
  25.2 5.3 %collective-permute-done.1 = bf16[2,592,128]{2,1,0:T(8,128)(2,1)S(1)} collective-permute-done((bf16[2,592,128]{2,1,0:T(8,128)(2,1)S(1)}, bf16[2,592,128]{2,1,0:T(8,128)(2,1)S(1)}, u32[]{:S(2)}, u32[]{:S(2)}) %collective-permute-start.1) | collective-permute-done | bytes 303136 | tf_op jit(solution)/shard_map/ppermute | solution.py:60
  34.0 2.4 collective-permute-start.2
  38.5 4.8 %collective-permute-done.3.refs_2_ = bf16[336,128]{1,0:T(8,128)(2,1)S(1)} collective-permute-done((bf16[336,128]{1,0:T(8,128)(2,1)S(1)}, bf16[336,128]{1,0:T(8,128)(2,1)S(1)}, u32[]{:S(2)}, u32[]{:S(2)}) %collective-permute-start.3) | collective-permute-done | bytes 86048 | tf_op jit(solution)/shard_map/ppermute | solution.py:177
  43.7 2.9 collective-permute-start.7
  48.1 3.2 collective-permute-done.7
  54.6 2.1 collective-permute-start.13
  59.4 2.0 collective-permute-start.16
  61.7 5.0 %first_params.1 = (bf16[256,128]{1,0:T(8,128)(2,1)S(1)}, bf16[256,128]{1,0:T(8,128)(2,1)S(1)}, f32[8,256]{1,0:T(8,128)S(1)}, bf16[896,256]{1,0:T(8,128)(2,1)S(1)...) custom-call(s32[1]{0:T(128)} %bitcast.12.refs_0_, ...), custom_call_target="tpu_custom_call" | custom-call | flops 8800000000 | bytes 100000 | tf_op jit(solution)/shard_map/first_params/pallas_call | solution.py:1337
  69.6 12.5 %stem_conv.1 = (bf16[3072,256]{1,0:T(8,128)(2,1)S(1)}, f32[3072,256]{1,0:T(8,128)S(1)}, f32[32,8,256]{2,1,0:T(8,128)S(1)}) custom-call(bf16[5376,256]{1,0:T(8,128)(2,1)S(1)} %get-tuple-element.122.refs_0_.refs_7_, bf16[5376,256]{1,0:T(8,128)(2,1)S(1)} %get-tuple-element.123.refs_1_.refs_8_, bf16[5376,256]{1,0:T(8,128)(2,1)S(1)} %get-tuple-element.124.refs_2_.refs_9_, ...), custom_call_target="tpu_custom_call" | custom-call | flops 17600000000 | bytes 100000 | tf_op jit(solution)/shard_map/stem_conv/pallas_call | solution.py:1360
  85.6 3.5 all-to-all-start.1
  89.1 1.8 fusion.39
  94.0 2.2 copy.74
  96.2 6.1 %collective-permute-done.14 = bf16[2,2,304,128]{3,2,1,0:T(8,128)(2,1)} collective-permute-done((bf16[2,2,304,128]{3,2,1,0:T(8,128)(2,1)}, bf16[2,2,304,128]{3,2,1,0:T(8,128)(2,1)}, u32[]{:S(2)}, u32[]{:S(2)}) %collective-permute-start.14) | collective-permute-done | bytes 311328 | tf_op jit(solution)/shard_map/ppermute | solution.py:60
  102.3 2.3 maximum_maximum_fusion
  104.6 4.1 all-to-all-start.3
  108.8 1.9 copy-done.41
  115.3 13.6 %fine_forward.1 = (bf16[3072,256]{1,0:T(8,128)(2,1)S(1)}, bf16[3072,896]{1,0:T(8,128)(2,1)S(1)}, bf16[3072,896]{1,0:T(8,128)(2,1)}, bf16[768,896]{1,0:T(8,128)(2,1)S(1)}, bf16[768,512]{1,0:T(8,128)(2,1)S(1)}) custom-call(f32[32,8,256]{2,1,0:T(8,128)} %all-to-all-done.1.refs_0_, f32[3072,256]{1,0:T(8,128)S(1)} %copy-done.41, ...), custom_call_target="tpu_custom_call" | custom-call | flops 16499999744 | bytes 100000 | tf_op jit(solution)/shard_map/fine_forward/pallas_call | solution.py:1369
  128.8 2.4 copy-done.25
  131.3 2.4 collective-permute-start.9
  135.0 1.9 pad_maximum_fusion.refs_2_
  138.4 3.4 collective-permute-start.11
  143.3 8.1 %rest_params.1 = (f32[49,8,512]{2,1,0:T(8,128)S(1)}, f32[8,512]{1,0:T(8,128)S(1)}, bf16[1664,512]{1,0:T(8,128)(2,1)S(1)}, f32[1,1664]{1,0:T(1,128)S(1)}, bf16[51...) custom-call(s32[1]{0:T(128)} %bitcast.12.refs_0_, ...), custom_call_target="tpu_custom_call" | custom-call | flops 14300000256 | bytes 100000 | tf_op jit(solution)/shard_map/rest_params/pallas_call | solution.py:1348
  156.2 10.3 %coarse_conv.1 = (f32[768,512]{1,0:T(8,128)S(1)}, bf16[768,512]{1,0:T(8,128)(2,1)S(1)}, f32[32,8,512]{2,1,0:T(8,128)}) custom-call(bf16[768,512]{1,0:T(8,128)(2,1)S(1)} %get-tuple-element.137.refs_0_.refs_2_.refs_3_, bf16[96,512]{1,0:T(8,128)(2,1)S(1)} %collective-permute-done.9.refs_1_.refs_4_, bf16[96,512]{1,0:T(8,128)(2,1)S(1)} %collective-permute-done.10.refs_2_.refs_5_, ...), custom_call_target="tpu_custom_call" | custom-call | flops 12099999744 | bytes 100000 | tf_op jit(solution)/shard_map/coarse_conv/pallas_call | solution.py:1417
  169.5 7.8 %all-to-all-start.2 = ((f32[32,8,512]{2,1,0:T(8,128)}), f32[32,8,512]{2,1,0:T(8,128)S(1)}, u32[]{:S(2)}, u32[]{:S(2)}) async-start(f32[32,8,512]{2,1,0:T(8,128)} %get-tuple-element.141), calls=%async_computation.2 | async-start | bytes 1048576 | tf_op jit(solution)/shard_map/all_to_all | solution.py:159
  179.3 1.8 targets.1.refs_13_
  183.7 2.8 collective-permute-start.20
  186.5 6.4 %all-to-all-done.2.refs_0_.refs_1_ = f32[32,8,512]{2,1,0:T(8,128)S(1)} async-done(((f32[32,8,512]{2,1,0:T(8,128)}), f32[32,8,512]{2,1,0:T(8,128)S(1)}, u32[]{:S(2)}, u32[]{:S(2)}) %all-to-all-start.2) | async-done | bytes 524320 | tf_op jit(solution)/shard_map/all_to_all | solution.py:159
  204.3 16.4 %middle.1 = (bf16[3072,256]{1,0:T(8,128)(2,1)S(1)}, bf16[768,512]{1,0:T(8,128)(2,1)S(1)}, bf16[3072,128]{1,0:T(8,128)(2,1)S(1)}, f32[3072,256]{1,0:T(8,128)}, bf...) custom-call(f32[32,8,512]{2,1,0:T(8,128)S(1)} %all-to-all-done.2.ref, ...), custom_call_target="tpu_custom_call" | custom-call | flops 22000001024 | bytes 100000 | tf_op jit(solution)/shard_map/middle/pallas_call | solution.py:1430
  229.3 2.4 collective-permute-start.18
  234.3 6.2 %all-to-all-start.4 = ((f32[32,8,512]{2,1,0:T(8,128)}), f32[32,8,512]{2,1,0:T(8,128)S(1)}, u32[]{:S(2)}, u32[]{:S(2)}) async-start(f32[32,8,512]{2,1,0:T(8,128)} %get-tuple-element.153), calls=%async_computation.4 | async-start | bytes 1048576 | tf_op jit(solution)/shard_map/all_to_all | solution.py:159
  241.8 1.9 edge.3
  243.7 4.0 collective-permute-start.22
  249.3 4.0 coarse_weights.1
  255.1 2.0 copy-done.35
  257.0 4.2 late_flat.1
  261.2 1.8 copy-done
  263.1 3.3 collective-permute-done.22
  275.1 24.9 %coarse_conv_back.1 = (bf16[768,512]{1,0:T(8,128)(2,1)S(1)}, f32[56,512]{1,0:T(8,128)S(1)}) custom-call(f32[32,8,512]{2,1,0:T(8,128)S(1)} %all-to-all-done.2.refs_0_.refs_1_, f32[32,8,512]{2,1,0:T(8,128)S(1)} %all-to-all-done.4.refs_1_, f32[8,512]{1,0:T(8,128)S(1)} %get-tuple-element.143.refs_3_.refs_2_, bf16[768,512]{1,0:T(8,128)(2,1)S(1)} %copy-done.10, ...), custom_call_target="tpu_custom_call" | custom-call | flops 27499999232 | bytes 100000 | tf_op jit(solution)/shard_map/coarse_conv_back/pallas_call | solution.py:1475
  300.2 2.1 convert_add_fusion
  304.5 2.5 collective-permute-start.26
  307.1 9.2 %fine_backward.1 = (bf16[3072,256]{1,0:T(8,128)(2,1)S(1)}, bf16[3072,896]{1,0:T(8,128)(2,1)}, f32[3072,256]{1,0:T(8,128)S(1)}, bf16[3072,256]{1,0:T(8,128)(2,1)S...) custom-call(f32[32,8,256]{2,1,0:T(8,128)} %all-to-all-done.1.refs_0_, ...), custom_call_target="tpu_custom_call" | custom-call | flops 14300000256 | bytes 100000 | tf_op jit(solution)/shard_map/fine_backward/pallas_call | solution.py:1498
  320.3 5.9 %all-to-all-start.5 = ((f32[32,8,256]{2,1,0:T(8,128)}), f32[32,8,256]{2,1,0:T(8,128)S(1)}, u32[]{:S(2)}, u32[]{:S(2)}) async-start(f32[32,8,256]{2,1,0:T(8,128)} %get-tuple-element.182), calls=%async_computation.5 | async-start | bytes 524288 | tf_op jit(solution)/shard_map/all_to_all | solution.py:159
  329.3 2.6 copy-done.26
  331.8 2.6 copy-done.27
  335.5 4.1 fine_weights.1
  339.6 2.2 early_flat.1
  345.5 4.4 collective-permute-done.28
  352.8 5.9 %collective-permute-start.32 = (bf16[592,128]{1,0:T(8,128)(2,1)}, bf16[592,128]{1,0:T(8,128)(2,1)}, u32[]{:S(2)}, u32[]{:S(2)}) collective-permute-start(bf16[592,128]{1,0:T(8,128)(2,1)} %get-tuple-element.214), channel_id=1, source_target_pairs={{0,24},{4,28},{8,16},{12,20},{16,8},{20,12},{1,25},{5,29},{9,17},{... | collective-permute-start | bytes 454664 | tf_op jit(solution)/shard_map/ppermute | solution.py:154
  358.7 1.9 collective-permute-start.31
  360.6 2.1 collective-permute-start.30
  371.3 1.9 copy-done.43
  373.2 1.9 copy-done.46
  376.5 20.6 %stem_back.1 = f32[32,8,128]{2,1,0:T(8,128)} custom-call(f32[32,8,256]{2,1,0:T(8,128)} %all-to-all-done.1.refs_0_, f32[32,8,256]{2,1,0:T(8,128)S(1)} %all-to-all-done.5.refs_1_, f32[8,256]{1,0:T(8,128)S(1)} %get-tuple-element.131.refs_3_.refs_4_.refs_2_, f32[3072,256]{1,0:T(8,128)S(1)} %copy-done.46, f32[3072,256]{1,0:T(8,128)S(1)} %copy-done.43, ...), custom_call_target="tpu_custom_call" | custom-call | flops 28600000512 | bytes 100000 | tf_op jit(solution)/shard_map/stem_back/pallas_call | solution.py:1542
  397.1 2.6 all-to-all-start.6
  404.2 7.6 %collective-permute-done.33 = bf16[2,2,304,128]{3,2,1,0:T(8,128)(2,1)S(1)} collective-permute-done((bf16[2,2,304,128]{3,2,1,0:T(8,128)(2,1)S(1)}, bf16[2,2,304,128]{3,2,1,0:T(8,128)(2,1)S(1)}, u32[]{:S(2)}, u32[]{:S(2)}) %collective-permute-start.33) | collective-permute-done | bytes 311328 | tf_op jit(solution)/shard_map/ppermute | solution.py:60
  414.7 3.6 collective-permute-done.34
  421.1 3.3 collective-permute-start.37
  425.7 2.4 collective-permute-done.39
  428.1 6.8 %collective-permute-done.38 = bf16[592,128]{1,0:T(8,128)(2,1)} collective-permute-done((bf16[592,128]{1,0:T(8,128)(2,1)S(1)}, bf16[592,128]{1,0:T(8,128)(2,1)}, u32[]{:S(2)}, u32[]{:S(2)}) %collective-permute-start.38) | collective-permute-done | bytes 151584 | tf_op jit(solution)/shard_map/ppermute | solution.py:154
  439.9 2.6 all-to-all-start.7
  444.0 9.0 %all-to-all-done.7 = f32[32,16,128]{2,1,0:T(8,128)S(1)} async-done(((f32[32,16,128]{2,1,0:T(8,128)}), f32[32,16,128]{2,1,0:T(8,128)S(1)}, u32[]{:S(2)}, u32[]{:S(2)}) %all-to-all-start.7) | async-done | bytes 262176 | tf_op jit(solution)/shard_map/all_to_all | solution.py:159
  (394 shorter events, 139.6 us)
Async XLA Ops:
  2.5 11.0 %copy-start.18 = (bf16[20,2,32,192]{3,2,1,0:T(8,128)(2,1)S(1)}, bf16[20,2,32,192]{3,2,1,0:T(8,128)(2,1)}, u32[]{:S(2)}) copy-start(bf16[20,2,32,192]{3,2,1,0:T(8,128)(2,1)} %param.9) | copy-start | bytes 1474564
  3.7 19.1 %all-to-all-start = ((bf16[4,432,160]{1,2,0:T(8,128)(2,1)}), bf16[4,432,160]{1,2,0:T(8,128)(2,1)S(1)}, u32[]{:S(2)}, u32[]{:S(2)}) async-start(bf16[4,432,160]{1,2,0:T(8,128)(2,1)} %copy.65), calls=%async_computation | async-start | bytes 1310720 | tf_op jit(solution)/shard_map/all_to_all | solution.py:1258
  9.4 11.7 %collective-permute-start = (bf16[1,592,128]{2,1,0:T(8,128)(2,1)S(1)}, bf16[1,592,128]{2,1,0:T(8,128)(2,1)S(1)}, u32[]{:S(2)}, u32[]{:S(2)}) collective-permute-start(bf16[1,592,128]{2,1,0:T(8,128)(2,1)S(1)} %bitcast.157), channel_id=1, source_target_pairs={{0,16},{4,20},{8,24},{12,28},{16,0},{20,4},{24,8},{28,12},{1,17},{... | collective-permute-start | bytes 454664 | tf_op jit(solution)/shard_map/ppermute | solution.py:60
  21.2 9.3 %collective-permute-start.1 = (bf16[2,592,128]{2,1,0:T(8,128)(2,1)S(1)}, bf16[2,592,128]{2,1,0:T(8,128)(2,1)S(1)}, u32[]{:S(2)}, u32[]{:S(2)}) collective-permute-start(bf16[2,592,128]{2,1,0:T(8,128)(2,1)S(1)} %pad_maximum_fusion.7), channel_id=1, source_target_pairs={{0,8},{4,12},{8,0},{12,4},{16,24},{20,28},{24,16},{28,20},{1,9},{5... | collective-permute-start | bytes 909320 | tf_op jit(solution)/shard_map/ppermute | solution.py:60
  30.7 7.5 %collective-permute-start.5 = (bf16[2,288,128]{2,1,0:T(8,128)(2,1)S(1)}, bf16[2,288,128]{2,1,0:T(8,128)(2,1)S(1)}, u32[]{:S(2)}, u32[]{:S(2)}) collective-permute-start(bf16[2,288,128]{2,1,0:T(8,128)(2,1)S(1)} %pad_maximum_fusion.11), channel_id=1, source_target_pairs={{0,2},{1,3},{2,0},{3,1},{4,6},{5,7},{6,4},{7,5},{8,10},{9,11},{10,... | collective-permute-start | bytes 442376 | tf_op jit(solution)/shard_map/ppermute | solution.py:60
  32.4 5.8 %collective-permute-start.4 = (bf16[2,304,128]{2,1,0:T(8,128)(2,1)S(1)}, bf16[2,304,128]{2,1,0:T(8,128)(2,1)S(1)}, u32[]{:S(2)}, u32[]{:S(2)}) collective-permute-start(bf16[2,304,128]{2,1,0:T(8,128)(2,1)S(1)} %fusion.25), channel_id=1, source_target_pairs={{0,4},{4,0},{8,12},{12,8},{16,20},{20,16},{24,28},{28,24},{1,5},{5... | collective-permute-start | bytes 466952 | tf_op jit(solution)/shard_map/ppermute | solution.py:60
  34.0 4.5 collective-permute-start.2
  36.4 6.9 %collective-permute-start.3 = (bf16[336,128]{1,0:T(8,128)(2,1)S(1)}, bf16[336,128]{1,0:T(8,128)(2,1)S(1)}, u32[]{:S(2)}, u32[]{:S(2)}) collective-permute-start(bf16[336,128]{1,0:T(8,128)(2,1)S(1)} %get-tuple-element.112), channel_id=1, source_target_pairs={{4,0},{8,4},{12,8},{16,12},{20,16},{24,20},{28,24},{5,1},{9,5},{13... | collective-permute-start | bytes 258056 | tf_op jit(solution)/shard_map/ppermute | solution.py:177
  43.3 8.0 %collective-permute-start.6 = (bf16[2,2,304,128]{3,2,1,0:T(8,128)(2,1)S(1)}, bf16[2,2,304,128]{3,2,1,0:T(8,128)(2,1)S(1)}, u32[]{:S(2)}, u32[]{:S(2)}) collective-permute-start(bf16[2,2,304,128]{3,2,1,0:T(8,128)(2,1)S(1)} %pad_maximum_fusion.5), channel_id=1, source_target_pairs={{0,2},{1,3},{2,0},{3,1},{4,6},{5,7},{6,4},{7,5},{8,10},{9,11},{10,... | collective-permute-start | bytes 933896 | tf_op jit(solution)/shard_map/ppermute | solution.py:60
  43.7 7.6 %collective-permute-start.7 = (bf16[2,2,288,128]{3,2,1,0:T(8,128)(2,1)S(1)}, bf16[2,2,288,128]{3,2,1,0:T(8,128)(2,1)S(1)}, u32[]{:S(2)}, u32[]{:S(2)}) collective-permute-start(bf16[2,2,288,128]{3,2,1,0:T(8,128)(2,1)S(1)} %pad_maximum_fusion.8), channel_id=1, source_target_pairs={{0,4},{4,0},{8,12},{12,8},{16,20},{20,16},{24,28},{28,24},{1,5},{5... | collective-permute-start | bytes 884744 | tf_op jit(solution)/shard_map/ppermute | solution.py:60
  48.1 21.5 %copy-start.28 = (bf16[5376,256]{1,0:T(8,128)(2,1)}, bf16[5376,256]{1,0:T(8,128)(2,1)S(1)}, u32[]{:S(2)}) copy-start(bf16[5376,256]{1,0:T(8,128)(2,1)S(1)} %get-tuple-element.122.refs_0_.refs_7_) | copy-start | bytes 8257540
  48.1 21.5 %copy-start.30 = (bf16[5376,256]{1,0:T(8,128)(2,1)}, bf16[5376,256]{1,0:T(8,128)(2,1)S(1)}, u32[]{:S(2)}) copy-start(bf16[5376,256]{1,0:T(8,128)(2,1)S(1)} %get-tuple-element.123.refs_1_.refs_8_) | copy-start | bytes 8257540
  48.1 21.5 %copy-start.32 = (bf16[5376,256]{1,0:T(8,128)(2,1)}, bf16[5376,256]{1,0:T(8,128)(2,1)S(1)}, u32[]{:S(2)}) copy-start(bf16[5376,256]{1,0:T(8,128)(2,1)S(1)} %get-tuple-element.124.refs_2_.refs_9_) | copy-start | bytes 8257540
  51.4 10.1 %collective-permute-start.8 = (bf16[8,592,128]{2,1,0:T(8,128)(2,1)S(1)}, bf16[8,592,128]{2,1,0:T(8,128)(2,1)S(1)}, u32[]{:S(2)}, u32[]{:S(2)}) collective-permute-start(bf16[8,592,128]{2,1,0:T(8,128)(2,1)S(1)} %bitcast.152), channel_id=1, source_target_pairs={{0,1},{1,0},{2,3},{3,2},{4,5},{5,4},{6,7},{7,6},{8,9},{9,8},{10,11... | collective-permute-start | bytes 3637256 | tf_op jit(solution)/shard_map/ppermute | solution.py:60
  52.2 6.3 %collective-permute-start.15 = (bf16[2,288,128]{2,1,0:T(8,128)(2,1)S(1)}, bf16[2,288,128]{2,1,0:T(8,128)(2,1)S(1)}, u32[]{:S(2)}, u32[]{:S(2)}) collective-permute-start(bf16[2,288,128]{2,1,0:T(8,128)(2,1)S(1)} %pad_maximum_fusion.10), channel_id=1, source_target_pairs={{0,2},{1,3},{2,0},{3,1},{4,6},{5,7},{6,4},{7,5},{8,10},{9,11},{10,... | collective-permute-start | bytes 442376 | tf_op jit(solution)/shard_map/ppermute | solution.py:60
  54.6 34.5 %collective-permute-start.13 = (bf16[2,304,128]{2,1,0:T(8,128)(2,1)}, bf16[2,304,128]{2,1,0:T(8,128)(2,1)}, u32[]{:S(2)}, u32[]{:S(2)}) collective-permute-start(bf16[2,304,128]{2,1,0:T(8,128)(2,1)} %fusion.24), channel_id=1, source_target_pairs={{0,4},{4,0},{8,12},{12,8},{16,20},{20,16},{24,28},{28,24},{1,5},{5... | collective-permute-start | bytes 466952 | tf_op jit(solution)/shard_map/ppermute | solution.py:60
  59.4 36.8 %collective-permute-start.16 = (bf16[2,2,288,128]{3,2,1,0:T(8,128)(2,1)}, bf16[2,2,288,128]{3,2,1,0:T(8,128)(2,1)}, u32[]{:S(2)}, u32[]{:S(2)}) collective-permute-start(bf16[2,2,288,128]{3,2,1,0:T(8,128)(2,1)} %get-tuple-element.232), channel_id=1, source_target_pairs={{0,4},{4,0},{8,12},{12,8},{16,20},{20,16},{24,28},{28,24},{1,5},{5... | collective-permute-start | bytes 884744 | tf_op jit(solution)/shard_map/ppermute | solution.py:60
  68.4 13.7 %copy-start.96 = (bf16[256,128]{1,0:T(8,128)(2,1)}, bf16[256,128]{1,0:T(8,128)(2,1)S(1)}, u32[]{:S(2)}) copy-start(bf16[256,128]{1,0:T(8,128)(2,1)S(1)} %get-tuple-element.127.refs_4_.refs_11_) | copy-start | bytes 196612
  68.4 13.7 %copy-start.98 = (bf16[256,128]{1,0:T(8,128)(2,1)}, bf16[256,128]{1,0:T(8,128)(2,1)S(1)}, u32[]{:S(2)}) copy-start(bf16[256,128]{1,0:T(8,128)(2,1)S(1)} %get-tuple-element.126.refs_3_.refs_10_) | copy-start | bytes 196612
  85.6 19.0 %all-to-all-start.1 = ((f32[32,8,256]{2,1,0:T(8,128)}), f32[32,8,256]{2,1,0:T(8,128)}, u32[]{:S(2)}, u32[]{:S(2)}) async-start(f32[32,8,256]{2,1,0:T(8,128)} %copy-done.7), calls=%async_computation.1 | async-start | bytes 524288 | tf_op jit(solution)/shard_map/all_to_all | solution.py:159
  91.0 11.3 %collective-permute-start.14 = (bf16[2,2,304,128]{3,2,1,0:T(8,128)(2,1)}, bf16[2,2,304,128]{3,2,1,0:T(8,128)(2,1)}, u32[]{:S(2)}, u32[]{:S(2)}) collective-permute-start(bf16[2,2,304,128]{3,2,1,0:T(8,128)(2,1)} %get-tuple-element.230), channel_id=1, source_target_pairs={{0,2},{1,3},{2,0},{3,1},{4,6},{5,7},{6,4},{7,5},{8,10},{9,11},{10,... | collective-permute-start | bytes 933896 | tf_op jit(solution)/shard_map/ppermute | solution.py:60
  104.6 30.4 %collective-permute-start.17 = (bf16[8,592,128]{2,1,0:T(8,128)(2,1)}, bf16[8,592,128]{2,1,0:T(8,128)(2,1)}, u32[]{:S(2)}, u32[]{:S(2)}) collective-permute-start(bf16[8,592,128]{2,1,0:T(8,128)(2,1)} %bitcast.31), channel_id=1, source_target_pairs={{0,1},{1,0},{2,3},{3,2},{4,5},{5,4},{6,7},{7,6},{8,9},{9,8},{10,11... | collective-permute-start | bytes 3637256 | tf_op jit(solution)/shard_map/ppermute | solution.py:60
  104.6 64.8 %all-to-all-start.3 = ((bf16[4,384,160]{1,2,0:T(8,128)(2,1)}), bf16[4,384,160]{1,2,0:T(8,128)(2,1)}, u32[]{:S(2)}, u32[]{:S(2)}) async-start(bf16[4,384,160]{1,2,0:T(8,128)(2,1)} %copy.74), calls=%async_computation.3 | async-start | bytes 983040 | tf_op jit(solution)/shard_map/all_to_all | solution.py:1258
  131.3 24.4 %copy-start.8 = (bf16[768,512]{1,0:T(8,128)(2,1)}, bf16[768,512]{1,0:T(8,128)(2,1)S(1)}, u32[]{:S(2)}) copy-start(bf16[768,512]{1,0:T(8,128)(2,1)S(1)} %get-tuple-element.137.refs_0_.refs_2_.refs_3_) | copy-start | bytes 2359300
  131.3 5.6 %collective-permute-start.9 = (bf16[96,512]{1,0:T(8,128)(2,1)S(1)}, bf16[96,512]{1,0:T(8,128)(2,1)S(1)}, u32[]{:S(2)}, u32[]{:S(2)}) collective-permute-start(bf16[96,512]{1,0:T(8,128)(2,1)S(1)} %bitcast.169), channel_id=1, source_target_pairs={{0,1},{1,2},{2,3},{4,5},{5,6},{6,7},{8,9},{9,10},{10,11},{12,13},{... | collective-permute-start | bytes 294920 | tf_op jit(solution)/shard_map/ppermute | solution.py:170
  133.7 4.3 collective-permute-start.10
  138.0 17.7 %copy-start.23 = (bf16[96,512]{1,0:T(8,128)(2,1)}, bf16[96,512]{1,0:T(8,128)(2,1)S(1)}, u32[]{:S(2)}) copy-start(bf16[96,512]{1,0:T(8,128)(2,1)S(1)} %collective-permute-done.10.refs_2_.refs_5_) | copy-start | bytes 294916
  138.4 17.0 %collective-permute-start.11 = (bf16[192,512]{1,0:T(8,128)(2,1)S(1)}, bf16[192,512]{1,0:T(8,128)(2,1)S(1)}, u32[]{:S(2)}, u32[]{:S(2)}) collective-permute-start(bf16[192,512]{1,0:T(8,128)(2,1)S(1)} %get-tuple-element.138), channel_id=1, source_target_pairs={{0,4},{4,8},{8,12},{12,16},{16,20},{20,24},{24,28},{1,5},{5,9},{9,... | collective-permute-start | bytes 589832 | tf_op jit(solution)/shard_map/ppermute | solution.py:177
  141.8 13.6 %collective-permute-start.12 = (bf16[192,512]{1,0:T(8,128)(2,1)S(1)}, bf16[192,512]{1,0:T(8,128)(2,1)S(1)}, u32[]{:S(2)}, u32[]{:S(2)}) collective-permute-start(bf16[192,512]{1,0:T(8,128)(2,1)S(1)} %get-tuple-element.139), channel_id=1, source_target_pairs={{4,0},{8,4},{12,8},{16,12},{20,16},{24,20},{28,24},{5,1},{9,5},{13... | collective-permute-start | bytes 589832 | tf_op jit(solution)/shard_map/ppermute | solution.py:177
  155.4 11.1 %copy-start.104 = (f32[8,256]{1,0:T(8,128)}, f32[8,256]{1,0:T(8,128)S(1)}, u32[]{:S(2)}) copy-start(f32[8,256]{1,0:T(8,128)S(1)} %get-tuple-element.148.refs_8_) | copy-start | bytes 24580
  155.4 11.1 %copy-start.106 = (f32[1,1664]{1,0:T(1,128)}, f32[1,1664]{1,0:T(1,128)S(1)}, u32[]{:S(2)}) copy-start(f32[1,1664]{1,0:T(1,128)S(1)} %get-tuple-element.145.refs_5_) | copy-start | bytes 19972
  169.5 23.4 %all-to-all-start.2 = ((f32[32,8,512]{2,1,0:T(8,128)}), f32[32,8,512]{2,1,0:T(8,128)S(1)}, u32[]{:S(2)}, u32[]{:S(2)}) async-start(f32[32,8,512]{2,1,0:T(8,128)} %get-tuple-element.141), calls=%async_computation.2 | async-start | bytes 1048576 | tf_op jit(solution)/shard_map/all_to_all | solution.py:159
  183.7 56.9 %collective-permute-start.20 = (bf16[96,512]{1,0:T(8,128)(2,1)}, bf16[96,512]{1,0:T(8,128)(2,1)}, u32[]{:S(2)}, u32[]{:S(2)}) collective-permute-start(bf16[96,512]{1,0:T(8,128)(2,1)} %bitcast.38), channel_id=1, source_target_pairs={{0,1},{1,2},{2,3},{4,5},{5,6},{6,7},{8,9},{9,10},{10,11},{12,13},{... | collective-permute-start | bytes 294920 | tf_op jit(solution)/shard_map/ppermute | solution.py:170
  204.3 36.3 %copy-start.12 = (bf16[768,512]{1,0:T(8,128)(2,1)S(1)}, bf16[768,512]{1,0:T(8,128)(2,1)}, u32[]{:S(2)}) copy-start(bf16[768,512]{1,0:T(8,128)(2,1)} %copy-done.11) | copy-start | bytes 2359300
  229.3 11.3 %collective-permute-start.18 = (bf16[96,512]{1,0:T(8,128)(2,1)}, bf16[96,512]{1,0:T(8,128)(2,1)}, u32[]{:S(2)}, u32[]{:S(2)}) collective-permute-start(bf16[96,512]{1,0:T(8,128)(2,1)} %bitcast.35), channel_id=1, source_target_pairs={{0,1},{1,2},{2,3},{4,5},{5,6},{6,7},{8,9},{9,10},{10,11},{12,13},{... | collective-permute-start | bytes 294920 | tf_op jit(solution)/shard_map/ppermute | solution.py:170
  231.7 8.9 %collective-permute-start.21 = (bf16[96,512]{1,0:T(8,128)(2,1)}, bf16[96,512]{1,0:T(8,128)(2,1)}, u32[]{:S(2)}, u32[]{:S(2)}) collective-permute-start(bf16[96,512]{1,0:T(8,128)(2,1)} %bitcast.39), channel_id=1, source_target_pairs={{1,0},{2,1},{3,2},{5,4},{6,5},{7,6},{9,8},{10,9},{11,10},{13,12},{... | collective-permute-start | bytes 294920 | tf_op jit(solution)/shard_map/ppermute | solution.py:171
  233.0 7.6 %collective-permute-start.19 = (bf16[96,512]{1,0:T(8,128)(2,1)}, bf16[96,512]{1,0:T(8,128)(2,1)}, u32[]{:S(2)}, u32[]{:S(2)}) collective-permute-start(bf16[96,512]{1,0:T(8,128)(2,1)} %bitcast.36), channel_id=1, source_target_pairs={{1,0},{2,1},{3,2},{5,4},{6,5},{7,6},{9,8},{10,9},{11,10},{13,12},{... | collective-permute-start | bytes 294920 | tf_op jit(solution)/shard_map/ppermute | solution.py:171
  234.3 32.1 %all-to-all-start.4 = ((f32[32,8,512]{2,1,0:T(8,128)}), f32[32,8,512]{2,1,0:T(8,128)S(1)}, u32[]{:S(2)}, u32[]{:S(2)}) async-start(f32[32,8,512]{2,1,0:T(8,128)} %get-tuple-element.153), calls=%async_computation.4 | async-start | bytes 1048576 | tf_op jit(solution)/shard_map/all_to_all | solution.py:159
  243.7 22.6 %collective-permute-start.22 = (bf16[384,512]{1,0:T(8,128)(2,1)S(1)}, bf16[384,512]{1,0:T(8,128)(2,1)S(1)}, u32[]{:S(2)}, u32[]{:S(2)}) collective-permute-start(bf16[384,512]{1,0:T(8,128)(2,1)S(1)} %get-tuple-element.158), channel_id=1, source_target_pairs={{0,4},{4,8},{8,12},{12,16},{16,20},{20,24},{24,28},{1,5},{5,9},{9,... | collective-permute-start | bytes 1179656 | tf_op jit(solution)/shard_map/ppermute | solution.py:177
  247.7 18.7 %collective-permute-start.23 = (bf16[384,512]{1,0:T(8,128)(2,1)S(1)}, bf16[384,512]{1,0:T(8,128)(2,1)S(1)}, u32[]{:S(2)}, u32[]{:S(2)}) collective-permute-start(bf16[384,512]{1,0:T(8,128)(2,1)S(1)} %get-tuple-element.159), channel_id=1, source_target_pairs={{4,0},{8,4},{12,8},{16,12},{20,16},{24,20},{28,24},{5,1},{9,5},{13... | collective-permute-start | bytes 1179656 | tf_op jit(solution)/shard_map/ppermute | solution.py:177
  263.1 37.0 %collective-permute-start.24 = (bf16[12,592,128]{2,1,0:T(8,128)(2,1)}, bf16[12,592,128]{2,1,0:T(8,128)(2,1)}, u32[]{:S(2)}, u32[]{:S(2)}) collective-permute-start(bf16[12,592,128]{2,1,0:T(8,128)(2,1)} %get-tuple-element.177), channel_id=1, source_target_pairs={{0,1},{1,0},{2,3},{3,2},{4,5},{5,4},{6,7},{7,6},{8,9},{9,8},{10,11... | collective-permute-start | bytes 5455880 | tf_op jit(solution)/shard_map/ppermute | solution.py:60
  275.1 25.0 %copy-start.1 = (f32[12,592,128]{2,1,0:T(8,128)S(1)}, f32[12,592,128]{2,1,0:T(8,128)}, u32[]{:S(2)}) copy-start(f32[12,592,128]{2,1,0:T(8,128)} %copy-done) | copy-start | bytes 10911748
  303.2 24.5 %collective-permute-start.25 = (bf16[2,3,304,128]{3,2,1,0:T(8,128)(2,1)S(1)}, bf16[2,3,304,128]{3,2,1,0:T(8,128)(2,1)S(1)}, u32[]{:S(2)}, u32[]{:S(2)}) collective-permute-start(bf16[2,3,304,128]{3,2,1,0:T(8,128)(2,1)S(1)} %slice_bitcast_fusion.4), channel_id=1, source_target_pairs={{0,2},{1,3},{2,0},{3,1},{4,6},{5,7},{6,4},{7,5},{8,10},{9,11},{10,... | collective-permute-start | bytes 1400840 | tf_op jit(solution)/shard_map/ppermute | solution.py:60
  304.5 21.7 %collective-permute-start.26 = (bf16[2,3,288,128]{3,2,1,0:T(8,128)(2,1)}, bf16[2,3,288,128]{3,2,1,0:T(8,128)(2,1)}, u32[]{:S(2)}, u32[]{:S(2)}) collective-permute-start(bf16[2,3,288,128]{3,2,1,0:T(8,128)(2,1)} %slice_bitcast_fusion.5), channel_id=1, source_target_pairs={{0,4},{4,0},{8,12},{12,8},{16,20},{20,16},{24,28},{28,24},{1,5},{5... | collective-permute-start | bytes 1327112 | tf_op jit(solution)/shard_map/ppermute | solution.py:60
  320.3 45.7 %all-to-all-start.5 = ((f32[32,8,256]{2,1,0:T(8,128)}), f32[32,8,256]{2,1,0:T(8,128)S(1)}, u32[]{:S(2)}, u32[]{:S(2)}) async-start(f32[32,8,256]{2,1,0:T(8,128)} %get-tuple-element.182), calls=%async_computation.5 | async-start | bytes 524288 | tf_op jit(solution)/shard_map/all_to_all | solution.py:159
  341.8 21.0 %collective-permute-start.29 = (bf16[8,592,128]{2,1,0:T(8,128)(2,1)S(1)}, bf16[8,592,128]{2,1,0:T(8,128)(2,1)S(1)}, u32[]{:S(2)}, u32[]{:S(2)}) collective-permute-start(bf16[8,592,128]{2,1,0:T(8,128)(2,1)S(1)} %get-tuple-element.202), channel_id=1, source_target_pairs={{0,1},{1,0},{2,3},{3,2},{4,5},{5,4},{6,7},{7,6},{8,9},{9,8},{10,11... | collective-permute-start | bytes 3637256 | tf_op jit(solution)/shard_map/ppermute | solution.py:60
  342.2 7.7 %collective-permute-start.28 = (bf16[3,288,128]{2,1,0:T(8,128)(2,1)S(1)}, bf16[3,288,128]{2,1,0:T(8,128)(2,1)S(1)}, u32[]{:S(2)}, u32[]{:S(2)}) collective-permute-start(bf16[3,288,128]{2,1,0:T(8,128)(2,1)S(1)} %fusion.23), channel_id=1, source_target_pairs={{0,2},{1,3},{2,0},{3,1},{4,6},{5,7},{6,4},{7,5},{8,10},{9,11},{10,... | collective-permute-start | bytes 663560 | tf_op jit(solution)/shard_map/ppermute | solution.py:60
  344.0 7.7 %collective-permute-start.27 = (bf16[3,304,128]{2,1,0:T(8,128)(2,1)S(1)}, bf16[3,304,128]{2,1,0:T(8,128)(2,1)S(1)}, u32[]{:S(2)}, u32[]{:S(2)}) collective-permute-start(bf16[3,304,128]{2,1,0:T(8,128)(2,1)S(1)} %fusion.22), channel_id=1, source_target_pairs={{0,4},{4,0},{8,12},{12,8},{16,20},{20,16},{24,28},{28,24},{1,5},{5... | collective-permute-start | bytes 700424 | tf_op jit(solution)/shard_map/ppermute | solution.py:60
  352.8 68.3 %collective-permute-start.32 = (bf16[592,128]{1,0:T(8,128)(2,1)}, bf16[592,128]{1,0:T(8,128)(2,1)}, u32[]{:S(2)}, u32[]{:S(2)}) collective-permute-start(bf16[592,128]{1,0:T(8,128)(2,1)} %get-tuple-element.214), channel_id=1, source_target_pairs={{0,24},{4,28},{8,16},{12,20},{16,8},{20,12},{1,25},{5,29},{9,17},{... | collective-permute-start | bytes 454664 | tf_op jit(solution)/shard_map/ppermute | solution.py:154
  358.7 67.0 %collective-permute-start.31 = (bf16[592,128]{1,0:T(8,128)(2,1)}, bf16[592,128]{1,0:T(8,128)(2,1)}, u32[]{:S(2)}, u32[]{:S(2)}) collective-permute-start(bf16[592,128]{1,0:T(8,128)(2,1)} %get-tuple-element.213), channel_id=1, source_target_pairs={{0,16},{4,20},{8,24},{12,28},{24,8},{28,12},{1,17},{5,21},{9,25},{... | collective-permute-start | bytes 454664 | tf_op jit(solution)/shard_map/ppermute | solution.py:154
  360.6 65.1 %collective-permute-start.30 = (bf16[592,128]{1,0:T(8,128)(2,1)}, bf16[592,128]{1,0:T(8,128)(2,1)}, u32[]{:S(2)}, u32[]{:S(2)}) collective-permute-start(bf16[592,128]{1,0:T(8,128)(2,1)} %get-tuple-element.212), channel_id=1, source_target_pairs={{0,8},{4,12},{16,24},{20,28},{24,16},{28,20},{1,9},{5,13},{17,25},... | collective-permute-start | bytes 454664 | tf_op jit(solution)/shard_map/ppermute | solution.py:154
  364.5 38.1 %collective-permute-start.35 = (bf16[2,2,288,128]{3,2,1,0:T(8,128)(2,1)}, bf16[2,2,288,128]{3,2,1,0:T(8,128)(2,1)}, u32[]{:S(2)}, u32[]{:S(2)}) collective-permute-start(bf16[2,2,288,128]{3,2,1,0:T(8,128)(2,1)} %slice_bitcast_fusion.9), channel_id=1, source_target_pairs={{0,4},{4,0},{8,12},{12,8},{16,20},{20,16},{24,28},{28,24},{1,5},{5... | collective-permute-start | bytes 884744 | tf_op jit(solution)/shard_map/ppermute | solution.py:60
  397.1 27.9 %all-to-all-start.6 = ((f32[32,8,128]{2,1,0:T(8,128)}), f32[32,8,128]{2,1,0:T(8,128)S(1)}, u32[]{:S(2)}, u32[]{:S(2)}) async-start(f32[32,8,128]{2,1,0:T(8,128)} %stem_back.1), calls=%async_computation.6 | async-start | bytes 262144 | tf_op jit(solution)/shard_map/all_to_all | solution.py:159
  400.8 11.0 %collective-permute-start.33 = (bf16[2,2,304,128]{3,2,1,0:T(8,128)(2,1)S(1)}, bf16[2,2,304,128]{3,2,1,0:T(8,128)(2,1)S(1)}, u32[]{:S(2)}, u32[]{:S(2)}) collective-permute-start(bf16[2,2,304,128]{3,2,1,0:T(8,128)(2,1)S(1)} %slice_bitcast_fusion.7), channel_id=1, source_target_pairs={{0,2},{1,3},{2,0},{3,1},{4,6},{5,7},{6,4},{7,5},{8,10},{9,11},{10,... | collective-permute-start | bytes 933896 | tf_op jit(solution)/shard_map/ppermute | solution.py:60
  403.8 10.9 %collective-permute-start.36 = (bf16[2,288,128]{2,1,0:T(8,128)(2,1)S(1)}, bf16[2,288,128]{2,1,0:T(8,128)(2,1)S(1)}, u32[]{:S(2)}, u32[]{:S(2)}) collective-permute-start(bf16[2,288,128]{2,1,0:T(8,128)(2,1)S(1)} %fusion.33), channel_id=1, source_target_pairs={{0,2},{1,3},{2,0},{3,1},{4,6},{5,7},{6,4},{7,5},{8,10},{9,11},{10,... | collective-permute-start | bytes 442376 | tf_op jit(solution)/shard_map/ppermute | solution.py:60
  413.0 21.9 %copy-start.111 = (f32[3,592,128]{2,1,0:T(8,128)S(1)}, f32[3,592,128]{2,1,0:T(8,128)}, u32[]{:S(2)}) copy-start(f32[3,592,128]{2,1,0:T(8,128)} %copy-done.110) | copy-start | bytes 2727940
  413.0 5.3 %collective-permute-start.34 = (bf16[2,304,128]{2,1,0:T(8,128)(2,1)S(1)}, bf16[2,304,128]{2,1,0:T(8,128)(2,1)S(1)}, u32[]{:S(2)}, u32[]{:S(2)}) collective-permute-start(bf16[2,304,128]{2,1,0:T(8,128)(2,1)S(1)} %fusion.26), channel_id=1, source_target_pairs={{0,4},{4,0},{8,12},{12,8},{16,20},{20,16},{24,28},{28,24},{1,5},{5... | collective-permute-start | bytes 466952 | tf_op jit(solution)/shard_map/ppermute | solution.py:60
  418.5 9.6 %collective-permute-start.39 = (bf16[592,128]{1,0:T(8,128)(2,1)S(1)}, bf16[592,128]{1,0:T(8,128)(2,1)}, u32[]{:S(2)}, u32[]{:S(2)}) collective-permute-start(bf16[592,128]{1,0:T(8,128)(2,1)S(1)} %get-tuple-element.211), channel_id=1, source_target_pairs={{16,8},{20,12},{24,0},{28,4},{17,9},{21,13},{25,1},{29,5},{18,10},... | collective-permute-start | bytes 454664 | tf_op jit(solution)/shard_map/ppermute | solution.py:154
  419.8 15.1 %collective-permute-start.38 = (bf16[592,128]{1,0:T(8,128)(2,1)S(1)}, bf16[592,128]{1,0:T(8,128)(2,1)}, u32[]{:S(2)}, u32[]{:S(2)}) collective-permute-start(bf16[592,128]{1,0:T(8,128)(2,1)S(1)} %get-tuple-element.210), channel_id=1, source_target_pairs={{16,0},{20,4},{24,8},{28,12},{17,1},{21,5},{25,9},{29,13},{18,2},{... | collective-permute-start | bytes 454664 | tf_op jit(solution)/shard_map/ppermute | solution.py:154
  421.1 13.8 %collective-permute-start.37 = (bf16[592,128]{1,0:T(8,128)(2,1)S(1)}, bf16[592,128]{1,0:T(8,128)(2,1)}, u32[]{:S(2)}, u32[]{:S(2)}) collective-permute-start(bf16[592,128]{1,0:T(8,128)(2,1)S(1)} %get-tuple-element.209), channel_id=1, source_target_pairs={{0,8},{4,12},{8,0},{12,4},{1,9},{5,13},{9,1},{13,5},{2,10},{6,14},... | collective-permute-start | bytes 454664 | tf_op jit(solution)/shard_map/ppermute | solution.py:154
  425.7 28.9 %copy-start.114 = (f32[72072]{0:T(1024)S(1)}, f32[72072]{0:T(1024)}, u32[]{:S(2)}) copy-start(f32[72072]{0:T(1024)} %param.12) | copy-start | bytes 864868
  425.7 28.9 %copy-start.115 = (f32[72072]{0:T(1024)S(1)}, f32[72072]{0:T(1024)}, u32[]{:S(2)}) copy-start(f32[72072]{0:T(1024)} %param.13) | copy-start | bytes 864868
  425.7 28.9 %copy-start.116 = (f32[72072]{0:T(1024)S(1)}, f32[72072]{0:T(1024)}, u32[]{:S(2)}) copy-start(f32[72072]{0:T(1024)} %param.14) | copy-start | bytes 864868
  439.9 13.2 %all-to-all-start.7 = ((f32[32,16,128]{2,1,0:T(8,128)}), f32[32,16,128]{2,1,0:T(8,128)S(1)}, u32[]{:S(2)}, u32[]{:S(2)}) async-start(f32[32,16,128]{2,1,0:T(8,128)} %broadcast_in_dim.97), calls=%async_computation.7 | async-start | bytes 524288 | tf_op jit(solution)/shard_map/all_to_all | solution.py:159
  (103 other events, 290.4 us)
